TPU v7x, 32 devices: a whole 2x2x4 slice. The times are simulated.
32 devices in a mesh: row: 4 (over x, core), col: 4 (over z), depth: 2 (over y).
Axes of the slice: x: 2, y: 2, z: 4, core: 2. Of those that a mesh axis runs over, the one named last changes fastest.
Arguments:
- amplitudes: bfloat16 [2, 128, 3072], P(None, 'col', ('row', 'depth')), may hold values from -6 to 6
- integrals: bfloat16 [2, 3072, 3072], P(None, ('row', 'depth'), 'col'), may hold values from -0.15625 to 0.15625
- occ_count: int32 [2], replicated, may hold values from 65 to 128, as said below
- virtual_pair_count: int32 [2], replicated, may hold values from 3009 to 3072, as said below
Outputs:
- ladder: bfloat16 [4, 768, 2, 128], P(None, ('row', 'depth'), None, 'col')
Inputs may be any that keep to these rules, and one draw needn't show every extreme that they name: `occ_count`: slots from the count up to 128 are padding; some block is full. `virtual_pair_count`: slots from the count up to 3072 are padding; some block is full.
All inputs are finite; a program needn't handle non-finite values.
Results may differ from a plain program's by a relative error of at most 0.001.
Values may be sent and summed in bfloat16 or wider, within the bound.
No kernel may reach another device: no remote copies, remote signals or barrier semaphores. Data moves between devices by JAX's collectives and lax.ppermute only.
A program may use at most 64 MiB of HBM per device.

v0:
```python
import jax
import jax.numpy as jnp
from jax import lax
from jax.sharding import PartitionSpec as P


def body(amplitudes, integrals, occ_count, virtual_pair_count):
    symmetry_labels = integrals.shape[0]
    kblock = integrals.shape[1]
    nblock = integrals.shape[2]
    kstart = lax.axis_index(("row", "depth")) * kblock
    nstart = lax.axis_index("col") * nblock
    kslots = kstart + jnp.arange(kblock, dtype=jnp.int32)
    k_live = kslots[None, :] < virtual_pair_count[:, None]
    piece = lax.all_gather(amplitudes, "col", axis=1, tiled=True)
    mslots = jnp.arange(piece.shape[1], dtype=jnp.int32)
    live = (mslots[None, :, None] < occ_count[:, None, None]) & k_live[:, None, :]
    gathered = jnp.where(live, piece, jnp.zeros_like(piece))
    summed = lax.psum_scatter(
        jnp.einsum("gkn,gmk->ngm", integrals, gathered, preferred_element_type=jnp.float32),
        ("row", "depth"),
        scatter_dimension=0,
        tiled=True,
    )
    height = summed.shape[0]
    padded_slot_total = (
        nstart + lax.axis_index(("row", "depth")) * height + jnp.arange(height, dtype=jnp.int32)
    )
    active_total = padded_slot_total[:, None] < virtual_pair_count[None, :]
    finished = jnp.where(active_total[:, :, None], summed, 0.0).astype(jnp.bfloat16)
    moved = lax.all_to_all(finished, "col", split_axis=2, concat_axis=0, tiled=True)
    return moved.reshape(lax.axis_size("col"), height, symmetry_labels, moved.shape[2])


def solution(mesh):
    in_specs = (P(None, "col", ("row", "depth")), P(None, ("row", "depth"), "col"), P(), P())
    out_specs = P(None, ("row", "depth"), None, "col")
    return jax.shard_map(body, mesh=mesh, in_specs=in_specs, out_specs=out_specs, check_vma=False)
```

profile of v0, /device:TPU:0, one launch (start us, length us, event | category | flops | bytes accessed | tf_op | source)
XLA Modules:
  0.0 70.4 jit_solution(3735212843793423277)
XLA Ops:
  0.0 0.0 copy-start
  0.0 15.8 %all_gather.3 = bf16[2,128,384]{2,1,0:T(8,128)(2,1)S(1)} all-gather(bf16[2,32,384]{2,1,0:T(8,128)(2,1)} %param.4), channel_id=1, replica_groups=mesh['row'=4,'col'=4,'depth'=2] {'col'}, dimensions={1}, use_global_device_ids=true | all-gather | bytes 245760 | tf_op jit(solution)/shard_map/all_gather | solution.py:15
  15.8 0.7 %iota_compare_fusion = pred[2,128]{1,0:T(4,128)(4,1)S(1)} fusion(s32[2]{0:T(128)} %param.6), kind=kLoop, calls=%fused_computation.11 | loop fusion | flops 256 | bytes 264 | tf_op jit(solution)/shard_map/lt | solution.py:17
  16.5 0.7 %broadcast_compare_fusion.1 = pred[2,384]{1,0:T(4,128)(4,1)S(1)} fusion(s32[384]{0:T(512)S(1)} %iota_add_fusion, s32[2]{0:T(128)} %param.7), kind=kLoop, calls=%fused_computation.10 | loop fusion | flops 768 | bytes 2312 | tf_op jit(solution)/shard_map/lt | solution.py:14
  17.2 0.0 copy-done
  17.3 0.4 convolution_bitcast_fusion
  17.7 0.0 copy-start.1
  17.7 0.0 copy-start.2
  17.7 0.5 copy.6
  18.2 39.5 %all-reduce.2 = bf16[768,2,128]{2,1,0:T(2,128)(2,1)S(1)} all-reduce(f32[768,2,128]{2,1,0:T(2,128)S(1)} %copy.6), channel_id=2, replica_groups=mesh['row'=4,'col'=4,'depth'=2] {'row','depth'}, use_global_device_ids=true, to_apply=%region_0.1.clone | all-reduce | flops 196608 | bytes 1179648
  57.7 0.0 copy-done.1
  57.7 0.1 broadcast_compare_fusion
  57.8 0.0 copy-done.2
  57.8 0.6 dynamic-slice
  59.1 0.2 fusion.2
  59.2 0.1 copy.7
  59.4 10.4 %all_to_all.15 = bf16[96,2,128]{0,1,2:T(2,128)(2,1)S(1)} all-to-all(bf16[96,2,128]{0,1,2:T(2,128)(2,1)S(1)} %copy.7), channel_id=1, replica_groups=mesh['row'=4,'col'=4,'depth'=2] {'col'}, dimensions={2} | all-to-all | bytes 98304 | tf_op jit(solution)/shard_map/all_to_all | solution.py:31
  69.8 0.6 copy.10
  (2 shorter events, 0.0 us)
Async XLA Ops:
  0.0 17.3 %copy-start = (bf16[2,384,768]{2,1,0:T(8,128)(2,1)S(1)}, bf16[2,384,768]{2,1,0:T(8,128)(2,1)}, u32[]{:S(2)}) copy-start(bf16[2,384,768]{2,1,0:T(8,128)(2,1)} %param.5) | copy-start | bytes 3538948
  17.7 40.1 %copy-start.1 = (s32[2]{0:T(128)S(1)}, s32[2]{0:T(128)}, u32[]{:S(2)}) copy-start(s32[2]{0:T(128)} %param.7) | copy-start | bytes 28
  17.7 40.1 %copy-start.2 = (u32[32]{0:T(128)S(1)}, u32[32]{0:T(128)}, u32[]{:S(2)}) copy-start(u32[32]{0:T(128)} %constant.25) | copy-start | bytes 388
where the time goes:
time: 70.7 us; the launch traced here: 70.4 us
  blocking collectives  65.7 us (93%)
  local copies, waits for them, and re-layouts  1.86 us (3%)
  other arithmetic  1.71 us (2%)
  between operations  0.76 us (1%)
    unnamed x1, blocking collectives  39.5 us
    all_gather x1, blocking collectives, body(): piece = lax.all_gather(amplitudes, 'col', axis=1, tiled=True)  15.8 us
    all_to_all x1, blocking collectives, body(): lax.all_to_all(finished, 'col', split_axis=2, concat_axis=0, tiled=True)  10.4 us

commit v1 on v0

v1 whole, which is shorter than its diff:
```python
import functools

import jax
import jax.numpy as jnp
from jax import lax
from jax.experimental import pallas as pl
from jax.experimental.pallas import tpu as pltpu
from jax.sharding import PartitionSpec as P

F32 = jnp.float32
BF16 = jnp.bfloat16
AXES = ("row", "col", "depth")


def given_to(i, step, n):
    return i ^ step if n & (n - 1) == 0 else (i + step) % n


def got_from(i, step, n):
    return i ^ step if n & (n - 1) == 0 else lax.rem(i - step + n, n)


def products(sizes, *refs):
    _, cols, depths = sizes
    occ, live = refs[:2]
    amps = refs[2 : 2 + cols]
    ints, send, keep = refs[2 + cols :]
    row, col, dep = (lax.axis_index(a) for a in AXES)
    core = lax.rem(row, 2)
    irreps, mb, kb = amps[0].shape
    kstart = (row * depths + dep) * kb
    wide = cols * mb
    nhalf = send.shape[1]
    for g in range(irreps):
        k_live = kstart + lax.broadcasted_iota(jnp.int32, (mb, kb), 1) < live[g]
        parts = []
        for j in range(cols):
            m = got_from(col, j, cols) * mb + lax.broadcasted_iota(jnp.int32, (mb, kb), 0)
            parts.append(jnp.where(k_live & (m < occ[g]), amps[j][g].astype(F32), 0.0))
        lhs = jnp.concatenate(parts, axis=0).astype(BF16)
        out = jnp.dot(lhs, ints[g], preferred_element_type=F32).T
        for x in range(sizes[0] // 2):
            at = slice(g * wide, (g + 1) * wide)
            first = out[2 * x * nhalf : (2 * x + 1) * nhalf]
            second = out[(2 * x + 1) * nhalf : (2 * x + 2) * nhalf]
            send[x, :, at] = jnp.where(core == 0, second, first)
            keep[x, :, at] = jnp.where(core == 0, first, second)


def pieces(sizes, steps, keep, came, *outs):
    rows, _, depths = sizes
    x = lax.axis_index("row") // 2
    dep = lax.axis_index("depth")
    h = outs[0].shape[0]
    for (sx, sd), out in zip(steps, outs):
        tx = given_to(x, sx, rows // 2)
        at = pl.ds(pl.multiple_of(given_to(dep, sd, depths) * h, 8), h)
        out[...] = keep[tx, at, :] + came[tx, at, :]


def finish(sizes, *refs):
    rows, cols, depths = sizes
    live = refs[0]
    outs = refs[-cols:]
    ins = refs[1:-cols]
    row, col, dep = (lax.axis_index(a) for a in AXES)
    h, lanes = ins[0].shape
    irreps = live.shape[0]
    wide = lanes // irreps
    mb = wide // cols
    total = ins[0][...]
    for ref in ins[1:]:
        total = total + ref[...]
    pad = -h % 128
    if pad:
        total = jnp.concatenate([total, jnp.zeros((pad, lanes), F32)], axis=0)
    slot = (col * rows * depths + row * depths + dep) * h + lax.broadcasted_iota(jnp.int32, (wide, h), 1)
    for g in range(irreps):
        turned = total[:, g * wide : (g + 1) * wide].T[:, :h]
        turned = jnp.where(slot < live[g], turned, 0.0)
        for j in range(cols):
            outs[j][g] = turned[j * mb : (j + 1) * mb].astype(BF16)


def assemble(cols, *refs):
    out = refs[-1]
    col = lax.axis_index("col")
    for j in range(cols):
        out[got_from(col, j, cols)] = refs[j][...]


VMEM = pl.BlockSpec(memory_space=pltpu.VMEM)
SMEM = pl.BlockSpec(memory_space=pltpu.SMEM)


def call(kernel, name, smem, outs, *args):
    many = isinstance(outs, list)
    return pl.pallas_call(
        kernel,
        name=name,
        out_shape=outs,
        in_specs=[SMEM] * smem + [VMEM] * (len(args) - smem),
        out_specs=[VMEM] * len(outs) if many else VMEM,
        compiler_params=pltpu.CompilerParams(vmem_limit_bytes=48 * 2**20),
    )(*args)


def body(sizes, amplitudes, integrals, occ_count, virtual_pair_count):
    rows, cols, depths = sizes
    chips = rows // 2
    irreps, mb, _ = amplitudes.shape
    nb = integrals.shape[2]
    h = nb // (rows * depths)
    lanes = irreps * cols * mb

    amps = [amplitudes]
    for j in range(1, cols):
        amps.append(lax.ppermute(amplitudes, "col", [(i, given_to(i, j, cols)) for i in range(cols)]))

    half = jax.ShapeDtypeStruct((chips, depths * h, lanes), F32)
    send, keep = call(
        functools.partial(products, sizes), "products", 2, [half, half],
        occ_count, virtual_pair_count, *amps, integrals,
    )
    came = lax.ppermute(send, "row", [(i, i ^ 1) for i in range(rows)])

    steps = [(sx, sd) for sx in range(chips) for sd in range(depths)]
    piece = jax.ShapeDtypeStruct((h, lanes), F32)
    out = call(functools.partial(pieces, sizes, steps), "pieces", 0, [piece] * len(steps), keep, came)
    sums = [out[0]]
    for (sx, sd), part in list(zip(steps, out))[1:]:
        pairs = []
        for row in range(rows):
            for dep in range(depths):
                to = (given_to(row // 2, sx, chips) * 2 + row % 2) * depths + given_to(dep, sd, depths)
                pairs.append((row * depths + dep, to))
        sums.append(lax.ppermute(part, ("row", "depth"), pairs))

    block = jax.ShapeDtypeStruct((irreps, mb, h), BF16)
    done = call(functools.partial(finish, sizes), "finish", 1, [block] * cols, virtual_pair_count, *sums)
    back = [done[0]]
    for j in range(1, cols):
        pairs = [(given_to(i, j, cols), i) for i in range(cols)]
        back.append(lax.ppermute(done[j], "col", pairs))
    whole = jax.ShapeDtypeStruct((cols, irreps, mb, h), BF16)
    result = call(functools.partial(assemble, cols), "assemble", 0, whole, *back)
    return result.transpose(0, 3, 1, 2)


def solution(mesh):
    sizes = tuple(mesh.shape[a] for a in AXES)
    in_specs = (P(None, "col", ("row", "depth")), P(None, ("row", "depth"), "col"), P(), P())
    out_specs = P(None, ("row", "depth"), None, "col")
    return jax.shard_map(
        functools.partial(body, sizes), mesh=mesh, in_specs=in_specs, out_specs=out_specs, check_vma=False
    )
```

time: 70.7 us -> 34.9 us (0.49)
  blocking collectives: 65.7 us -> 0 us
  waiting for transfers between devices: 0 us -> 15.2 us
  starting transfers between devices: 0 us -> 13.7 us
  Pallas kernels: 0 us -> 2.36 us
  other arithmetic: 1.71 us -> 0 us
  local copies, waits for them, and re-layouts: 1.86 us -> 3.38 us
  between operations: 0.76 us -> 0.04 us
    unnamed x1 -> x0, blocking collectives: 39.5 us -> none
    all_gather x1 -> x0, blocking collectives: 15.8 us -> none  [body(): piece = lax.all_gather(amplitudes, 'col', axis=1, tiled=True)]
    ppermute x0 -> x10, waiting for transfers between devices: none -> 15.2 us  [the longest x3 6.09 us: body(): lax.ppermute(amplitudes, 'col', [(i, given_to(i, j, cols)) for i in range...]
    ppermute x0 -> x10, starting transfers between devices: none -> 13.7 us  [the longest x3 5.62 us: body(): lax.ppermute(amplitudes, 'col', [(i, given_to(i, j, cols)) for i in range...]
    all_to_all x1 -> x0, blocking collectives: 10.4 us -> none  [body(): lax.all_to_all(finished, 'col', split_axis=2, concat_axis=0, tiled=True)]
    unnamed x7 -> x10, local copies, waits for them, and re-layouts: 0.6 us -> 3.38 us
    pallas_call x0 -> x4, Pallas kernels: none -> 2.36 us  [call(): pl.pallas_call(kernel, name=name, out_shape=outs, in_specs=[SMEM] * smem...]
    lt x3 -> x0, other arithmetic: 1.53 us -> none  [the longest x1 0.73 us: body(): mslots[None, :, None] < occ_count[:, None, None]]
  transfers between devices with their start and end apart: 0 -> 10, of which waited for: 0 -> 9; matrix products, arithmetic and copies ran while one was open for 0% -> 0% of each run, Pallas kernels for 0% -> 0%
where the time goes in v1:
time: 34.9 us; the launch traced here: 34.7 us
  waiting for transfers between devices  15.2 us (44%)
  starting transfers between devices  13.7 us (39%)
  local copies, waits for them, and re-layouts  3.38 us (10%)
  Pallas kernels  2.36 us (7%)
    ppermute x3, waiting for transfers between devices, body(): lax.ppermute(amplitudes, 'col', [(i, given_to(i, j, cols)) for i in range...  6.09 us
    ppermute x3, starting transfers between devices, body(): lax.ppermute(amplitudes, 'col', [(i, given_to(i, j, cols)) for i in range...  5.62 us
    ppermute x3, waiting for transfers between devices, body(): sums.append(lax.ppermute(part, ('row', 'depth'), pairs))  5.04 us
    ppermute x3, starting transfers between devices, body(): back.append(lax.ppermute(done[j], 'col', pairs))  4.44 us
    ppermute x3, starting transfers between devices, body(): sums.append(lax.ppermute(part, ('row', 'depth'), pairs))  3.55 us
    unnamed x10, local copies, waits for them, and re-layouts  3.38 us
    pallas_call x4, Pallas kernels, call(): pl.pallas_call(kernel, name=name, out_shape=outs, in_specs=[SMEM] * smem...  2.36 us
    ppermute x3, waiting for transfers between devices, body(): back.append(lax.ppermute(done[j], 'col', pairs))  2.35 us
  transfers between devices with their start and end apart: 10, of which 9 were waited for; matrix products, arithmetic and copies ran while one was open for 0% of the time, Pallas kernels for 0%

profile of v1, /device:TPU:0, one launch (start us, length us, event | category | flops | bytes accessed | tf_op | source)
XLA Modules:
  0.0 34.7 jit_solution(14651004660014548920)
XLA Ops:
  0.0 4.0 %collective-permute-start.1 = (bf16[2,32,384]{2,1,0:T(8,128)(2,1)}, bf16[2,32,384]{2,1,0:T(8,128)(2,1)S(1)}, u32[]{:S(2)}, u32[]{:S(2)}) collective-permute-start(bf16[2,32,384]{2,1,0:T(8,128)(2,1)} %refs_2_.1), channel_id=1, source_target_pairs={{0,4},{2,6},{4,0},{6,2},{1,5},{3,7},{5,1},{7,3},{8,12},{10,14},{12... | collective-permute-start | bytes 147464 | tf_op jit(solution)/shard_map/ppermute | solution.py:118
  4.0 1.6 %collective-permute-start = (bf16[2,32,384]{2,1,0:T(8,128)(2,1)}, bf16[2,32,384]{2,1,0:T(8,128)(2,1)S(1)}, u32[]{:S(2)}, u32[]{:S(2)}) collective-permute-start(bf16[2,32,384]{2,1,0:T(8,128)(2,1)} %refs_2_.1), channel_id=1, source_target_pairs={{0,2},{2,0},{4,6},{6,4},{1,3},{3,1},{5,7},{7,5},{8,10},{10,8},{12,... | collective-permute-start | bytes 147464 | tf_op jit(solution)/shard_map/ppermute | solution.py:118
  5.6 0.0 collective-permute-start.2
  5.6 1.3 %collective-permute-done.1.refs_4_ = bf16[2,32,384]{2,1,0:T(8,128)(2,1)S(1)} collective-permute-done((bf16[2,32,384]{2,1,0:T(8,128)(2,1)}, bf16[2,32,384]{2,1,0:T(8,128)(2,1)S(1)}, u32[]{:S(2)}, u32[]{:S(2)}) %collective-permute-start.1) | collective-permute-done | bytes 49184 | tf_op jit(solution)/shard_map/ppermute | solution.py:118
  7.0 1.4 %collective-permute-done.refs_3_ = bf16[2,32,384]{2,1,0:T(8,128)(2,1)S(1)} collective-permute-done((bf16[2,32,384]{2,1,0:T(8,128)(2,1)}, bf16[2,32,384]{2,1,0:T(8,128)(2,1)S(1)}, u32[]{:S(2)}, u32[]{:S(2)}) %collective-permute-start) | collective-permute-done | bytes 49184 | tf_op jit(solution)/shard_map/ppermute | solution.py:118
  8.3 3.4 %collective-permute-done.2.refs_5_ = bf16[2,32,384]{2,1,0:T(8,128)(2,1)S(1)} collective-permute-done((bf16[2,32,384]{2,1,0:T(8,128)(2,1)}, bf16[2,32,384]{2,1,0:T(8,128)(2,1)S(1)}, u32[]{:S(2)}, u32[]{:S(2)}) %collective-permute-start.2) | collective-permute-done | bytes 49184 | tf_op jit(solution)/shard_map/ppermute | solution.py:118
  11.7 0.0 copy-start
  11.7 1.3 %copy-done = bf16[2,384,768]{2,1,0:T(8,128)(2,1)S(1)} copy-done((bf16[2,384,768]{2,1,0:T(8,128)(2,1)S(1)}, bf16[2,384,768]{2,1,0:T(8,128)(2,1)}, u32[]{:S(2)}) %copy-start) | copy-done | bytes 1179672
  13.0 0.0 copy-start.1
  13.0 0.8 %copy-done.1 = bf16[2,32,384]{2,1,0:T(8,128)(2,1)S(1)} copy-done((bf16[2,32,384]{2,1,0:T(8,128)(2,1)S(1)}, bf16[2,32,384]{2,1,0:T(8,128)(2,1)}, u32[]{:S(2)}) %copy-start.1) | copy-done | bytes 49176
  13.8 0.0 copy-start.2
  13.8 0.7 %copy-done.2 = s32[2]{0:T(128)S(1)} copy-done((s32[2]{0:T(128)S(1)}, s32[2]{0:T(128)}, u32[]{:S(2)}) %copy-start.2) | copy-done | bytes 32
  14.4 0.0 copy-start.4
  14.4 0.7 %copy-done.4 = s32[2]{0:T(128)S(1)} copy-done((s32[2]{0:T(128)S(1)}, s32[2]{0:T(128)}, u32[]{:S(2)}) %copy-start.4) | copy-done | bytes 32
  15.1 0.0 copy-start.3
  15.1 1.0 %products.1 = (f32[2,192,256]{2,1,0:T(8,128)S(1)}, f32[2,192,256]{2,1,0:T(8,128)S(1)}) custom-call(s32[2]{0:T(128)S(1)} %copy-done.4, s32[2]{0:T(128)S(1)} %copy-done.2, bf16[2,32,384]{2,1,0:T(8,128)(2,1)S(1)} %copy-done.1, bf16[2,32,384]{2,1,0:T(8,128)(2,1)S(1)} %collective-permute-done.refs_3_, bf16[2,32,384]{2,1,0:T(8,128)(2,1)S(1)} %collective-permute-done.1.refs_4_, ...), custom_call_target="tpu_custom_call" | custom-call | tf_op jit(solution)/shard_map/products/pallas_call | solution.py:98
  16.1 0.1 collective-permute-start.3
  16.2 1.7 %collective-permute-done.3.came = f32[2,192,256]{2,1,0:T(8,128)S(1)} collective-permute-done((f32[2,192,256]{2,1,0:T(8,128)S(1)}, f32[2,192,256]{2,1,0:T(8,128)S(1)}, u32[]{:S(2)}, u32[]{:S(2)}) %collective-permute-start.3) | collective-permute-done | bytes 393248 | tf_op jit(solution)/shard_map/ppermute | solution.py:125
  17.9 0.1 pieces.1
  18.0 1.6 %collective-permute-start.4 = (f32[96,256]{1,0:T(8,128)S(1)}, f32[96,256]{1,0:T(8,128)S(1)}, u32[]{:S(2)}, u32[]{:S(2)}) collective-permute-start(f32[96,256]{1,0:T(8,128)S(1)} %get-tuple-element.18), channel_id=1, source_target_pairs={{0,1},{1,0},{8,9},{9,8},{16,17},{17,16},{24,25},{25,24},{2,3},{3,2... | collective-permute-start | bytes 294920 | tf_op jit(solution)/shard_map/ppermute | solution.py:137
  19.6 1.5 %collective-permute-start.5 = (f32[96,256]{1,0:T(8,128)S(1)}, f32[96,256]{1,0:T(8,128)S(1)}, u32[]{:S(2)}, u32[]{:S(2)}) collective-permute-start(f32[96,256]{1,0:T(8,128)S(1)} %get-tuple-element.19), channel_id=1, source_target_pairs={{0,16},{1,17},{8,24},{9,25},{16,0},{17,1},{24,8},{25,9},{2,18},{3,... | collective-permute-start | bytes 294920 | tf_op jit(solution)/shard_map/ppermute | solution.py:137
  21.0 0.5 %collective-permute-start.6 = (f32[96,256]{1,0:T(8,128)S(1)}, f32[96,256]{1,0:T(8,128)S(1)}, u32[]{:S(2)}, u32[]{:S(2)}) collective-permute-start(f32[96,256]{1,0:T(8,128)S(1)} %get-tuple-element.20), channel_id=1, source_target_pairs={{0,17},{1,16},{8,25},{9,24},{16,1},{17,0},{24,9},{25,8},{2,19},{3,... | collective-permute-start | bytes 294920 | tf_op jit(solution)/shard_map/ppermute | solution.py:137
  21.5 1.3 %collective-permute-done.4.refs_2_ = f32[96,256]{1,0:T(8,128)S(1)} collective-permute-done((f32[96,256]{1,0:T(8,128)S(1)}, f32[96,256]{1,0:T(8,128)S(1)}, u32[]{:S(2)}, u32[]{:S(2)}) %collective-permute-start.4) | collective-permute-done | bytes 98336 | tf_op jit(solution)/shard_map/ppermute | solution.py:137
  22.9 2.3 %collective-permute-done.5.refs_3_ = f32[96,256]{1,0:T(8,128)S(1)} collective-permute-done((f32[96,256]{1,0:T(8,128)S(1)}, f32[96,256]{1,0:T(8,128)S(1)}, u32[]{:S(2)}, u32[]{:S(2)}) %collective-permute-start.5) | collective-permute-done | bytes 98336 | tf_op jit(solution)/shard_map/ppermute | solution.py:137
  25.2 1.4 %collective-permute-done.6.refs_4_ = f32[96,256]{1,0:T(8,128)S(1)} collective-permute-done((f32[96,256]{1,0:T(8,128)S(1)}, f32[96,256]{1,0:T(8,128)S(1)}, u32[]{:S(2)}, u32[]{:S(2)}) %collective-permute-start.6) | collective-permute-done | bytes 98336 | tf_op jit(solution)/shard_map/ppermute | solution.py:137
  26.6 0.0 copy-done.3
  26.6 0.6 %finish.1 = (bf16[2,32,96]{2,1,0:T(8,128)(2,1)S(1)}, bf16[2,32,96]{2,1,0:T(8,128)(2,1)S(1)}, bf16[2,32,96]{2,1,0:T(8,128)(2,1)S(1)}, bf16[2,32,96]{2,1,0:T(8,128)(2,1)S(1)}) custom-call(s32[2]{0:T(128)S(1)} %copy-done.3, f32[96,256]{1,0:T(8,128)S(1)} %get-tuple-element.17.refs_1_, f32[96,256]{1,0:T(8,128)S(1)} %collective-permute-done.4.refs_2_, ...), custom_call_target="tpu_custom_call" | custom-call | tf_op jit(solution)/shard_map/finish/pallas_call | solution.py:98
  27.2 0.1 collective-permute-start.7
  27.3 1.2 %collective-permute-start.8 = (bf16[2,32,96]{2,1,0:T(8,128)(2,1)S(1)}, bf16[2,32,96]{2,1,0:T(8,128)(2,1)S(1)}, u32[]{:S(2)}, u32[]{:S(2)}) collective-permute-start(bf16[2,32,96]{2,1,0:T(8,128)(2,1)S(1)} %get-tuple-element.23), channel_id=1, source_target_pairs={{4,0},{6,2},{0,4},{2,6},{5,1},{7,3},{1,5},{3,7},{12,8},{14,10},{8,... | collective-permute-start | bytes 36872 | tf_op jit(solution)/shard_map/ppermute | solution.py:144
  28.5 3.2 %collective-permute-start.9 = (bf16[2,32,96]{2,1,0:T(8,128)(2,1)S(1)}, bf16[2,32,96]{2,1,0:T(8,128)(2,1)S(1)}, u32[]{:S(2)}, u32[]{:S(2)}) collective-permute-start(bf16[2,32,96]{2,1,0:T(8,128)(2,1)S(1)} %get-tuple-element.24), channel_id=1, source_target_pairs={{6,0},{4,2},{2,4},{0,6},{7,1},{5,3},{3,5},{1,7},{14,8},{12,10},{10... | collective-permute-start | bytes 36872 | tf_op jit(solution)/shard_map/ppermute | solution.py:144
  31.7 0.0 collective-permute-done.7.refs_1_
  31.7 0.3 collective-permute-done.8.refs_2_
  32.0 2.0 %collective-permute-done.9.refs_3_ = bf16[2,32,96]{2,1,0:T(8,128)(2,1)S(1)} collective-permute-done((bf16[2,32,96]{2,1,0:T(8,128)(2,1)S(1)}, bf16[2,32,96]{2,1,0:T(8,128)(2,1)S(1)}, u32[]{:S(2)}, u32[]{:S(2)}) %collective-permute-start.9) | collective-permute-done | bytes 12320 | tf_op jit(solution)/shard_map/ppermute | solution.py:144
  34.0 0.6 %assemble.1 = bf16[4,2,32,96]{3,2,1,0:T(8,128)(2,1)} custom-call(bf16[2,32,96]{2,1,0:T(8,128)(2,1)S(1)} %get-tuple-element.21.refs_0_, bf16[2,32,96]{2,1,0:T(8,128)(2,1)S(1)} %collective-permute-done.7.refs_1_, bf16[2,32,96]{2,1,0:T(8,128)(2,1)S(1)} %collective-permute-done.8.refs_2_, bf16[2,32,96]{2,1,0:T(8,128)(2,1)S(1)} %collective-permute-done.9.refs_3_), custom_call_target="tpu_custom_call" | custom-call | tf_op jit(solution)/shard_map/assemble/pallas_call | solution.py:98
Async XLA Ops:
  0.0 6.9 %collective-permute-start.1 = (bf16[2,32,384]{2,1,0:T(8,128)(2,1)}, bf16[2,32,384]{2,1,0:T(8,128)(2,1)S(1)}, u32[]{:S(2)}, u32[]{:S(2)}) collective-permute-start(bf16[2,32,384]{2,1,0:T(8,128)(2,1)} %refs_2_.1), channel_id=1, source_target_pairs={{0,4},{2,6},{4,0},{6,2},{1,5},{3,7},{5,1},{7,3},{8,12},{10,14},{12... | collective-permute-start | bytes 147464 | tf_op jit(solution)/shard_map/ppermute | solution.py:118
  4.0 4.3 %collective-permute-start = (bf16[2,32,384]{2,1,0:T(8,128)(2,1)}, bf16[2,32,384]{2,1,0:T(8,128)(2,1)S(1)}, u32[]{:S(2)}, u32[]{:S(2)}) collective-permute-start(bf16[2,32,384]{2,1,0:T(8,128)(2,1)} %refs_2_.1), channel_id=1, source_target_pairs={{0,2},{2,0},{4,6},{6,4},{1,3},{3,1},{5,7},{7,5},{8,10},{10,8},{12,... | collective-permute-start | bytes 147464 | tf_op jit(solution)/shard_map/ppermute | solution.py:118
  5.6 6.1 %collective-permute-start.2 = (bf16[2,32,384]{2,1,0:T(8,128)(2,1)}, bf16[2,32,384]{2,1,0:T(8,128)(2,1)S(1)}, u32[]{:S(2)}, u32[]{:S(2)}) collective-permute-start(bf16[2,32,384]{2,1,0:T(8,128)(2,1)} %refs_2_.1), channel_id=1, source_target_pairs={{0,6},{2,4},{4,2},{6,0},{1,7},{3,5},{5,3},{7,1},{8,14},{10,12},{12... | collective-permute-start | bytes 147464 | tf_op jit(solution)/shard_map/ppermute | solution.py:118
  11.7 1.3 %copy-start = (bf16[2,384,768]{2,1,0:T(8,128)(2,1)S(1)}, bf16[2,384,768]{2,1,0:T(8,128)(2,1)}, u32[]{:S(2)}) copy-start(bf16[2,384,768]{2,1,0:T(8,128)(2,1)} %refs_6_.1) | copy-start | bytes 3538948
  13.0 0.8 %copy-start.1 = (bf16[2,32,384]{2,1,0:T(8,128)(2,1)S(1)}, bf16[2,32,384]{2,1,0:T(8,128)(2,1)}, u32[]{:S(2)}) copy-start(bf16[2,32,384]{2,1,0:T(8,128)(2,1)} %refs_2_.1) | copy-start | bytes 147460
  13.8 0.7 %copy-start.2 = (s32[2]{0:T(128)S(1)}, s32[2]{0:T(128)}, u32[]{:S(2)}) copy-start(s32[2]{0:T(128)} %refs_0_.3) | copy-start | bytes 28
  14.4 0.7 %copy-start.4 = (s32[2]{0:T(128)S(1)}, s32[2]{0:T(128)}, u32[]{:S(2)}) copy-start(s32[2]{0:T(128)} %refs_0_.2) | copy-start | bytes 28
  15.1 11.5 %copy-start.3 = (s32[2]{0:T(128)S(1)}, s32[2]{0:T(128)}, u32[]{:S(2)}) copy-start(s32[2]{0:T(128)} %refs_0_.3) | copy-start | bytes 28
  16.1 1.8 %collective-permute-start.3 = (f32[2,192,256]{2,1,0:T(8,128)S(1)}, f32[2,192,256]{2,1,0:T(8,128)S(1)}, u32[]{:S(2)}, u32[]{:S(2)}) collective-permute-start(f32[2,192,256]{2,1,0:T(8,128)S(1)} %get-tuple-element.16), channel_id=1, source_target_pairs={{0,8},{8,0},{16,24},{24,16},{1,9},{9,1},{17,25},{25,17},{2,10},{10... | collective-permute-start | bytes 1179656 | tf_op jit(solution)/shard_map/ppermute | solution.py:125
  18.0 4.9 %collective-permute-start.4 = (f32[96,256]{1,0:T(8,128)S(1)}, f32[96,256]{1,0:T(8,128)S(1)}, u32[]{:S(2)}, u32[]{:S(2)}) collective-permute-start(f32[96,256]{1,0:T(8,128)S(1)} %get-tuple-element.18), channel_id=1, source_target_pairs={{0,1},{1,0},{8,9},{9,8},{16,17},{17,16},{24,25},{25,24},{2,3},{3,2... | collective-permute-start | bytes 294920 | tf_op jit(solution)/shard_map/ppermute | solution.py:137
  19.6 5.6 %collective-permute-start.5 = (f32[96,256]{1,0:T(8,128)S(1)}, f32[96,256]{1,0:T(8,128)S(1)}, u32[]{:S(2)}, u32[]{:S(2)}) collective-permute-start(f32[96,256]{1,0:T(8,128)S(1)} %get-tuple-element.19), channel_id=1, source_target_pairs={{0,16},{1,17},{8,24},{9,25},{16,0},{17,1},{24,8},{25,9},{2,18},{3,... | collective-permute-start | bytes 294920 | tf_op jit(solution)/shard_map/ppermute | solution.py:137
  21.0 5.5 %collective-permute-start.6 = (f32[96,256]{1,0:T(8,128)S(1)}, f32[96,256]{1,0:T(8,128)S(1)}, u32[]{:S(2)}, u32[]{:S(2)}) collective-permute-start(f32[96,256]{1,0:T(8,128)S(1)} %get-tuple-element.20), channel_id=1, source_target_pairs={{0,17},{1,16},{8,25},{9,24},{16,1},{17,0},{24,9},{25,8},{2,19},{3,... | collective-permute-start | bytes 294920 | tf_op jit(solution)/shard_map/ppermute | solution.py:137
  27.2 4.5 %collective-permute-start.7 = (bf16[2,32,96]{2,1,0:T(8,128)(2,1)S(1)}, bf16[2,32,96]{2,1,0:T(8,128)(2,1)S(1)}, u32[]{:S(2)}, u32[]{:S(2)}) collective-permute-start(bf16[2,32,96]{2,1,0:T(8,128)(2,1)S(1)} %get-tuple-element.22), channel_id=1, source_target_pairs={{2,0},{0,2},{6,4},{4,6},{3,1},{1,3},{7,5},{5,7},{10,8},{8,10},{14,... | collective-permute-start | bytes 36872 | tf_op jit(solution)/shard_map/ppermute | solution.py:144
  27.3 4.7 %collective-permute-start.8 = (bf16[2,32,96]{2,1,0:T(8,128)(2,1)S(1)}, bf16[2,32,96]{2,1,0:T(8,128)(2,1)S(1)}, u32[]{:S(2)}, u32[]{:S(2)}) collective-permute-start(bf16[2,32,96]{2,1,0:T(8,128)(2,1)S(1)} %get-tuple-element.23), channel_id=1, source_target_pairs={{4,0},{6,2},{0,4},{2,6},{5,1},{7,3},{1,5},{3,7},{12,8},{14,10},{8,... | collective-permute-start | bytes 36872 | tf_op jit(solution)/shard_map/ppermute | solution.py:144
  28.5 5.5 %collective-permute-start.9 = (bf16[2,32,96]{2,1,0:T(8,128)(2,1)S(1)}, bf16[2,32,96]{2,1,0:T(8,128)(2,1)S(1)}, u32[]{:S(2)}, u32[]{:S(2)}) collective-permute-start(bf16[2,32,96]{2,1,0:T(8,128)(2,1)S(1)} %get-tuple-element.24), channel_id=1, source_target_pairs={{6,0},{4,2},{2,4},{0,6},{7,1},{5,3},{3,5},{1,7},{14,8},{12,10},{10... | collective-permute-start | bytes 36872 | tf_op jit(solution)/shard_map/ppermute | solution.py:144

commit v2 on v0

v2 whole, which is shorter than its diff:
```python
import functools

import jax
import jax.numpy as jnp
from jax import lax
from jax.experimental import pallas as pl
from jax.experimental.pallas import tpu as pltpu
from jax.sharding import PartitionSpec as P

F32 = jnp.float32
BF16 = jnp.bfloat16
AXES = ("row", "col", "depth")
VMEM = pl.BlockSpec(memory_space=pltpu.VMEM)
SMEM = pl.BlockSpec(memory_space=pltpu.SMEM)
HBM = pl.BlockSpec(memory_space=pl.ANY)


def load(occ, live, ints, held, limits, sem):
    copies = [pltpu.make_async_copy(ints.at[g], held.at[g], sem.at[g]) for g in range(ints.shape[0])]
    for copy in copies:
        copy.start()
    for g in range(ints.shape[0]):
        limits[0, g] = jnp.full(limits.shape[2:], occ[g], jnp.int32)
        limits[1, g] = jnp.full(limits.shape[2:], live[g], jnp.int32)
    for copy in copies:
        copy.wait()


def join(mine, other, both):
    both[0] = mine[...]
    both[1] = other[...]


def chunk_masks(cols):
    half = cols // 2
    return list(range(half)), list(range(half, cols))


def products(sizes, steps, *refs):
    rows, cols, depths = sizes
    half = cols // 2
    limits, mine = refs[:2]
    came = refs[2 : 2 + half]
    ints, ints_other = refs[2 + half : 4 + half]
    outs = refs[4 + half : -1]
    turned = refs[-1]
    row, col, dep = (lax.axis_index(a) for a in AXES)
    core = lax.rem(row, 2)
    _, irreps, mb, kb = mine.shape
    row_of = (row, row ^ 1)
    for g in range(irreps):
        total = None
        for part in range(2):
            kstart = (row_of[part] * depths + dep) * kb
            live = limits[1, g][:1, :1]
            k_live = kstart + lax.broadcasted_iota(jnp.int32, (mb, kb), 1) < live
            lhs = []
            for q in range(half):
                m = (col ^ (q + core * half)) * mb + lax.broadcasted_iota(jnp.int32, (mb, kb), 0)
                amp = came[q][part, g].astype(F32)
                if q == 0:
                    amp = jnp.where(core == 0, mine[part, g].astype(F32), amp)
                lhs.append(jnp.where(k_live & (m < limits[0, g][:1, :1]), amp, 0.0))
            lhs = jnp.concatenate(lhs, axis=0).astype(BF16)
            term = jnp.dot(lhs, (ints, ints_other)[part][g], preferred_element_type=F32)
            total = term if total is None else total + term
        wide = half * mb
        turned[:, g * wide : (g + 1) * wide] = total.T
    h = outs[0].shape[0] // 2
    for (sx, sd), out in zip(steps, outs):
        for c in range(2):
            block = ((row // 2 ^ sx) * 2 + c) * depths + (dep ^ sd)
            out[c * h : (c + 1) * h] = turned[pl.ds(pl.multiple_of(block * h, 8), h), :]


def finish(sizes, *refs):
    rows, cols, depths = sizes
    half = cols // 2
    limits = refs[0]
    outs = refs[-half:]
    ins = refs[1:-half]
    row, col, dep = (lax.axis_index(a) for a in AXES)
    core = lax.rem(row, 2)
    _, irreps, mb, h = outs[0].shape
    total = ins[0][...]
    for ref in ins[1:]:
        total = total + ref[...]
    lanes = total.shape[1]
    for c in range(2):
        part = total[c * h : (c + 1) * h]
        if h % 128:
            part = jnp.concatenate([part, jnp.zeros((-h % 128, lanes), F32)], axis=0)
        part = part.T[:, :h]
        slot = ((col * rows + row - core + c) * depths + dep) * h + lax.broadcasted_iota(jnp.int32, (mb, h), 1)
        for g in range(irreps):
            for q in range(half):
                at = (g * half + q) * mb
                outs[q][c, g] = jnp.where(slot < limits[1, g][:1, :1], part[at : at + mb], 0.0).astype(BF16)


def settle(half, *refs):
    first, came, keep, send = refs[0], refs[1 : 1 + half], refs[-2], refs[-1]
    core = lax.rem(lax.axis_index("row"), 2)
    for ref, c in ((keep, core), (send, 1 - core)):
        ref[0] = jnp.where(core == 0, first[c].astype(F32), came[0][c].astype(F32)).astype(BF16)
        for q in range(1, half):
            ref[q] = came[q][c]


def assemble(half, keep, came, out):
    core = lax.rem(lax.axis_index("row"), 2)
    col = lax.axis_index("col")
    for q in range(half):
        out[col ^ (q + core * half)] = keep[q]
        out[col ^ (q + (1 - core) * half)] = came[q]


def call(kernel, name, specs, outs, *args, scratch=(), cost=None):
    many = isinstance(outs, list)
    return pl.pallas_call(
        kernel,
        name=name,
        out_shape=outs,
        in_specs=specs + [VMEM] * (len(args) - len(specs)),
        out_specs=[VMEM] * len(outs) if many else VMEM,
        scratch_shapes=list(scratch),
        cost_estimate=cost,
        compiler_params=pltpu.CompilerParams(vmem_limit_bytes=40 * 2**20),
    )(*args)


def body(sizes, amplitudes, integrals, occ_count, virtual_pair_count):
    rows, cols, depths = sizes
    chips, half = rows // 2, cols // 2
    irreps, mb, kb = amplitudes.shape
    nb = integrals.shape[2]
    h = nb // (rows * depths)
    shape = jax.ShapeDtypeStruct

    def pairs(move):
        out = []
        for row in range(rows):
            for col in range(cols):
                for dep in range(depths):
                    r, c, d = move(row, col, dep)
                    out.append(((row * cols + col) * depths + dep, (r * cols + c) * depths + d))
        return out

    def send(value, move):
        return lax.ppermute(value, AXES, pairs(move))

    def other_core(row, col, dep):
        return row ^ 1, col, dep

    def chunk(q):
        def move(row, col, dep):
            if row % 2:
                return row, col ^ (q + half), dep
            return (row, col ^ q, dep) if q else (row ^ 2, col, dep)

        return move

    amps_other = send(amplitudes, other_core)
    ints_other = send(integrals, other_core)
    both = call(join, "join", [], shape((2, irreps, mb, kb), BF16), amplitudes, amps_other)
    came = [send(both, chunk(q)) for q in range(half)]
    ints, limits = call(
        load, "load", [SMEM, SMEM, HBM],
        [shape(integrals.shape, BF16), shape((2, irreps, 8, 128), jnp.int32)],
        occ_count, virtual_pair_count, integrals,
        scratch=[pltpu.SemaphoreType.DMA((irreps,))],
        cost=pl.CostEstimate(flops=0, bytes_accessed=4 * integrals.size, transcendentals=0),
    )

    steps = [(sx, sd) for sx in range(chips) for sd in range(depths)]
    lanes = irreps * half * mb
    out = call(
        functools.partial(products, sizes, steps), "products", [], [shape((2 * h, lanes), F32)] * len(steps),
        limits, both, *came, ints, ints_other,
        scratch=[pltpu.VMEM((nb, lanes), F32)],
    )
    sums = [out[0]]
    for (sx, sd), part in list(zip(steps, out))[1:]:
        sums.append(send(part, lambda row, col, dep, sx=sx, sd=sd: (row ^ 2 * sx, col, dep ^ sd)))

    done = call(
        functools.partial(finish, sizes), "finish", [], [shape((2, irreps, mb, h), BF16)] * half, limits, *sums
    )
    back = [send(done[q], chunk(q)) for q in range(half)]
    blocks = shape((half, irreps, mb, h), BF16)
    keep, give = call(functools.partial(settle, half), "settle", [], [blocks, blocks], done[0], *back)
    result = call(
        functools.partial(assemble, half), "assemble", [], shape((cols, irreps, mb, h), BF16),
        keep, send(give, other_core),
    )
    return result.transpose(0, 3, 1, 2)


def solution(mesh):
    sizes = tuple(mesh.shape[a] for a in AXES)
    in_specs = (P(None, "col", ("row", "depth")), P(None, ("row", "depth"), "col"), P(), P())
    out_specs = P(None, ("row", "depth"), None, "col")
    return jax.shard_map(
        functools.partial(body, sizes), mesh=mesh, in_specs=in_specs, out_specs=out_specs, check_vma=False
    )
```

time: 70.7 us -> 29.2 us (0.41)
  blocking collectives: 65.7 us -> 0 us
  waiting for transfers between devices: 0 us -> 11.8 us
  starting transfers between devices: 0 us -> 11.3 us
  Pallas kernels: 0 us -> 2.44 us
  other arithmetic: 1.71 us -> 0 us
  local copies, waits for them, and re-layouts: 1.86 us -> 3.38 us
    unnamed x1 -> x0, blocking collectives: 39.5 us -> none
    all_gather x1 -> x0, blocking collectives: 15.8 us -> none  [body(): piece = lax.all_gather(amplitudes, 'col', axis=1, tiled=True)]
    ppermute x0 -> x10, waiting for transfers between devices: none -> 11.8 us  [send(): return lax.ppermute(value, AXES, pairs(move))]
    ppermute x0 -> x10, starting transfers between devices: none -> 11.3 us  [send(): return lax.ppermute(value, AXES, pairs(move))]
    all_to_all x1 -> x0, blocking collectives: 10.4 us -> none  [body(): lax.all_to_all(finished, 'col', split_axis=2, concat_axis=0, tiled=True)]
    unnamed x7 -> x8, local copies, waits for them, and re-layouts: 0.6 us -> 3.38 us
    pallas_call x0 -> x6, Pallas kernels: none -> 2.44 us  [call(): pl.pallas_call(kernel, name=name, out_shape=outs, in_specs=specs + [VMEM]...]
    lt x3 -> x0, other arithmetic: 1.53 us -> none  [the longest x1 0.73 us: body(): mslots[None, :, None] < occ_count[:, None, None]]
  transfers between devices with their start and end apart: 0 -> 10, of which waited for: 0 -> 7; matrix products, arithmetic and copies ran while one was open for 0% -> 0% of each run, Pallas kernels for 0% -> 3%
where the time goes in v2:
time: 29.2 us; the launch traced here: 29 us
  waiting for transfers between devices  11.8 us (40%)
  starting transfers between devices  11.3 us (39%)
  local copies, waits for them, and re-layouts  3.38 us (12%)
  Pallas kernels  2.44 us (8%)
    ppermute x10, waiting for transfers between devices, send(): return lax.ppermute(value, AXES, pairs(move))  11.8 us
    ppermute x10, starting transfers between devices, send(): return lax.ppermute(value, AXES, pairs(move))  11.3 us
    unnamed x8, local copies, waits for them, and re-layouts  3.38 us
    pallas_call x6, Pallas kernels, call(): pl.pallas_call(kernel, name=name, out_shape=outs, in_specs=specs + [VMEM]...  2.44 us
  transfers between devices with their start and end apart: 10, of which 7 were waited for; matrix products, arithmetic and copies ran while one was open for 0% of the time, Pallas kernels for 3%

profile of v2, /device:TPU:0, one launch (start us, length us, event | category | flops | bytes accessed | tf_op | source)
XLA Modules:
  0.0 29.0 jit_solution(15410226960070918686)
XLA Ops:
  0.0 0.5 %collective-permute-start.3 = (bf16[2,384,768]{2,1,0:T(8,128)(2,1)}, bf16[2,384,768]{2,1,0:T(8,128)(2,1)S(1)}, u32[]{:S(2)}, u32[]{:S(2)}) collective-permute-start(bf16[2,384,768]{2,1,0:T(8,128)(2,1)} %ints.1), channel_id=1, source_target_pairs={{0,8},{1,9},{2,10},{3,11},{4,12},{5,13},{6,14},{7,15},{8,0},{9,1},... | collective-permute-start | bytes 3538952 | tf_op jit(solution)/shard_map/ppermute | solution.py:150
  0.5 0.1 collective-permute-start
  0.5 2.7 %collective-permute-done.other = bf16[2,32,384]{2,1,0:T(8,128)(2,1)S(1)} collective-permute-done((bf16[2,32,384]{2,1,0:T(8,128)(2,1)}, bf16[2,32,384]{2,1,0:T(8,128)(2,1)S(1)}, u32[]{:S(2)}, u32[]{:S(2)}) %collective-permute-start) | collective-permute-done | bytes 49184 | tf_op jit(solution)/shard_map/ppermute | solution.py:150
  3.2 0.0 copy-start.1
  3.2 0.8 %copy-done.1 = bf16[2,32,384]{2,1,0:T(8,128)(2,1)S(1)} copy-done((bf16[2,32,384]{2,1,0:T(8,128)(2,1)S(1)}, bf16[2,32,384]{2,1,0:T(8,128)(2,1)}, u32[]{:S(2)}) %copy-start.1) | copy-done | bytes 49176
  4.0 3.0 %collective-permute-start.2 = (bf16[2,2,32,384]{3,2,1,0:T(8,128)(2,1)S(1)}, bf16[2,2,32,384]{3,2,1,0:T(8,128)(2,1)S(1)}, u32[]{:S(2)}, u32[]{:S(2)}) collective-permute-start(bf16[2,2,32,384]{3,2,1,0:T(8,128)(2,1)S(1)} %join.1.refs_1_), channel_id=1, source_target_pairs={{0,2},{1,3},{2,0},{3,1},{4,6},{5,7},{6,4},{7,5},{8,14},{9,15},{10,... | collective-permute-start | bytes 294920 | tf_op jit(solution)/shard_map/ppermute | solution.py:150
  7.0 1.5 %collective-permute-start.1 = (bf16[2,2,32,384]{3,2,1,0:T(8,128)(2,1)S(1)}, bf16[2,2,32,384]{3,2,1,0:T(8,128)(2,1)S(1)}, u32[]{:S(2)}, u32[]{:S(2)}) collective-permute-start(bf16[2,2,32,384]{3,2,1,0:T(8,128)(2,1)S(1)} %join.1.refs_1_), channel_id=1, source_target_pairs={{0,16},{1,17},{2,18},{3,19},{4,20},{5,21},{6,22},{7,23},{8,12},{9,... | collective-permute-start | bytes 294920 | tf_op jit(solution)/shard_map/ppermute | solution.py:150
  8.5 0.0 copy-start
  8.5 1.3 %copy-done = bf16[2,384,768]{2,1,0:T(8,128)(2,1)S(1)} copy-done((bf16[2,384,768]{2,1,0:T(8,128)(2,1)S(1)}, bf16[2,384,768]{2,1,0:T(8,128)(2,1)}, u32[]{:S(2)}) %copy-start) | copy-done | bytes 1179672
  9.8 0.0 copy-start.2
  9.8 0.7 %copy-done.2 = s32[2]{0:T(128)S(1)} copy-done((s32[2]{0:T(128)S(1)}, s32[2]{0:T(128)}, u32[]{:S(2)}) %copy-start.2) | copy-done | bytes 32
  10.4 0.0 copy-start.3
  10.5 0.7 %copy-done.3 = s32[2]{0:T(128)S(1)} copy-done((s32[2]{0:T(128)S(1)}, s32[2]{0:T(128)}, u32[]{:S(2)}) %copy-start.3) | copy-done | bytes 32
  11.1 0.8 %load.1 = (bf16[2,384,768]{2,1,0:T(8,128)(2,1)S(1)}, s32[2,2,8,128]{3,2,1,0:T(8,128)S(1)}) custom-call(s32[2]{0:T(128)S(1)} %copy-done.2, s32[2]{0:T(128)S(1)} %copy-done.3, bf16[2,384,768]{2,1,0:T(8,128)(2,1)S(1)} %copy-done), custom_call_target="tpu_custom_call" | custom-call | bytes 2359296 | tf_op jit(solution)/shard_map/load/pallas_call | solution.py:120
  11.9 0.0 collective-permute-done.2.refs_3_
  11.9 0.0 collective-permute-done.1.refs_2_
  11.9 0.0 collective-permute-done.3.refs_5_
  12.0 0.9 %products.1 = (f32[192,128]{1,0:T(8,128)S(1)}, f32[192,128]{1,0:T(8,128)S(1)}, f32[192,128]{1,0:T(8,128)S(1)}, f32[192,128]{1,0:T(8,128)S(1)}) custom-call(s32[2,2,8,128]{3,2,1,0:T(8,128)S(1)} %get-tuple-element.15.refs_0_, bf16[2,2,32,384]{3,2,1,0:T(8,128)(2,1)S(1)} %join.1.refs_1_, bf16[2,2,32,384]{3,2,1,0:T(8,128)(2,1)S(1)} %collective-permute-done.1.refs_2_, ...), custom_call_target="tpu_custom_call" | custom-call | tf_op jit(solution)/shard_map/products/pallas_call | solution.py:120
  12.8 1.6 %collective-permute-start.4 = (f32[192,128]{1,0:T(8,128)S(1)}, f32[192,128]{1,0:T(8,128)S(1)}, u32[]{:S(2)}, u32[]{:S(2)}) collective-permute-start(f32[192,128]{1,0:T(8,128)S(1)} %get-tuple-element.18), channel_id=1, source_target_pairs={{0,1},{1,0},{2,3},{3,2},{4,5},{5,4},{6,7},{7,6},{8,9},{9,8},{10,11... | collective-permute-start | bytes 294920 | tf_op jit(solution)/shard_map/ppermute | solution.py:150
  14.4 1.2 %collective-permute-start.5 = (f32[192,128]{1,0:T(8,128)S(1)}, f32[192,128]{1,0:T(8,128)S(1)}, u32[]{:S(2)}, u32[]{:S(2)}) collective-permute-start(f32[192,128]{1,0:T(8,128)S(1)} %get-tuple-element.19), channel_id=1, source_target_pairs={{0,16},{1,17},{2,18},{3,19},{4,20},{5,21},{6,22},{7,23},{8,24},{9,... | collective-permute-start | bytes 294920 | tf_op jit(solution)/shard_map/ppermute | solution.py:150
  15.6 0.8 %collective-permute-start.6 = (f32[192,128]{1,0:T(8,128)S(1)}, f32[192,128]{1,0:T(8,128)S(1)}, u32[]{:S(2)}, u32[]{:S(2)}) collective-permute-start(f32[192,128]{1,0:T(8,128)S(1)} %get-tuple-element.20), channel_id=1, source_target_pairs={{0,17},{1,16},{2,19},{3,18},{4,21},{5,20},{6,23},{7,22},{8,25},{9,... | collective-permute-start | bytes 294920 | tf_op jit(solution)/shard_map/ppermute | solution.py:150
  16.4 1.3 %collective-permute-done.4.refs_2_ = f32[192,128]{1,0:T(8,128)S(1)} collective-permute-done((f32[192,128]{1,0:T(8,128)S(1)}, f32[192,128]{1,0:T(8,128)S(1)}, u32[]{:S(2)}, u32[]{:S(2)}) %collective-permute-start.4) | collective-permute-done | bytes 98336 | tf_op jit(solution)/shard_map/ppermute | solution.py:150
  17.7 1.8 %collective-permute-done.5.refs_3_ = f32[192,128]{1,0:T(8,128)S(1)} collective-permute-done((f32[192,128]{1,0:T(8,128)S(1)}, f32[192,128]{1,0:T(8,128)S(1)}, u32[]{:S(2)}, u32[]{:S(2)}) %collective-permute-start.5) | collective-permute-done | bytes 98336 | tf_op jit(solution)/shard_map/ppermute | solution.py:150
  19.5 2.1 %collective-permute-done.6.refs_4_ = f32[192,128]{1,0:T(8,128)S(1)} collective-permute-done((f32[192,128]{1,0:T(8,128)S(1)}, f32[192,128]{1,0:T(8,128)S(1)}, u32[]{:S(2)}, u32[]{:S(2)}) %collective-permute-start.6) | collective-permute-done | bytes 98336 | tf_op jit(solution)/shard_map/ppermute | solution.py:150
  21.6 0.1 finish.1
  21.7 1.1 %collective-permute-start.8 = (bf16[2,2,32,96]{3,2,1,0:T(8,128)(2,1)S(1)}, bf16[2,2,32,96]{3,2,1,0:T(8,128)(2,1)S(1)}, u32[]{:S(2)}, u32[]{:S(2)}) collective-permute-start(bf16[2,2,32,96]{3,2,1,0:T(8,128)(2,1)S(1)} %get-tuple-element.22), channel_id=1, source_target_pairs={{0,2},{1,3},{2,0},{3,1},{4,6},{5,7},{6,4},{7,5},{8,14},{9,15},{10,... | collective-permute-start | bytes 73736 | tf_op jit(solution)/shard_map/ppermute | solution.py:150
  22.8 0.9 %collective-permute-start.7 = (bf16[2,2,32,96]{3,2,1,0:T(8,128)(2,1)S(1)}, bf16[2,2,32,96]{3,2,1,0:T(8,128)(2,1)S(1)}, u32[]{:S(2)}, u32[]{:S(2)}) collective-permute-start(bf16[2,2,32,96]{3,2,1,0:T(8,128)(2,1)S(1)} %get-tuple-element.21.refs_0_), channel_id=1, source_target_pairs={{0,16},{1,17},{2,18},{3,19},{4,20},{5,21},{6,22},{7,23},{8,12},{9,... | collective-permute-start | bytes 73736 | tf_op jit(solution)/shard_map/ppermute | solution.py:150
  23.7 2.0 %collective-permute-done.8.refs_2_ = bf16[2,2,32,96]{3,2,1,0:T(8,128)(2,1)S(1)} collective-permute-done((bf16[2,2,32,96]{3,2,1,0:T(8,128)(2,1)S(1)}, bf16[2,2,32,96]{3,2,1,0:T(8,128)(2,1)S(1)}, u32[]{:S(2)}, u32[]{:S(2)}) %collective-permute-start.8) | collective-permute-done | bytes 24608 | tf_op jit(solution)/shard_map/ppermute | solution.py:150
  25.7 1.0 %collective-permute-done.7.refs_1_ = bf16[2,2,32,96]{3,2,1,0:T(8,128)(2,1)S(1)} collective-permute-done((bf16[2,2,32,96]{3,2,1,0:T(8,128)(2,1)S(1)}, bf16[2,2,32,96]{3,2,1,0:T(8,128)(2,1)S(1)}, u32[]{:S(2)}, u32[]{:S(2)}) %collective-permute-start.7) | collective-permute-done | bytes 24608 | tf_op jit(solution)/shard_map/ppermute | solution.py:150
  26.7 0.8 %collective-permute-start.9 = (bf16[2,2,32,96]{3,2,1,0:T(8,128)(2,1)S(1)}, bf16[2,2,32,96]{3,2,1,0:T(8,128)(2,1)S(1)}, u32[]{:S(2)}, u32[]{:S(2)}) collective-permute-start(bf16[2,2,32,96]{3,2,1,0:T(8,128)(2,1)S(1)} %get-tuple-element.24), channel_id=1, source_target_pairs={{0,8},{1,9},{2,10},{3,11},{4,12},{5,13},{6,14},{7,15},{8,0},{9,1},... | collective-permute-start | bytes 73736 | tf_op jit(solution)/shard_map/ppermute | solution.py:150
  27.5 0.9 %collective-permute-done.9.came = bf16[2,2,32,96]{3,2,1,0:T(8,128)(2,1)S(1)} collective-permute-done((bf16[2,2,32,96]{3,2,1,0:T(8,128)(2,1)S(1)}, bf16[2,2,32,96]{3,2,1,0:T(8,128)(2,1)S(1)}, u32[]{:S(2)}, u32[]{:S(2)}) %collective-permute-start.9) | collective-permute-done | bytes 24608 | tf_op jit(solution)/shard_map/ppermute | solution.py:150
  28.4 0.6 %assemble.1 = bf16[4,2,32,96]{3,2,1,0:T(8,128)(2,1)} custom-call(bf16[2,2,32,96]{3,2,1,0:T(8,128)(2,1)S(1)} %get-tuple-element.23.keep, bf16[2,2,32,96]{3,2,1,0:T(8,128)(2,1)S(1)} %collective-permute-done.9.came), custom_call_target="tpu_custom_call" | custom-call | tf_op jit(solution)/shard_map/assemble/pallas_call | solution.py:120
  (2 shorter events, 0.0 us)
Async XLA Ops:
  0.0 11.9 %collective-permute-start.3 = (bf16[2,384,768]{2,1,0:T(8,128)(2,1)}, bf16[2,384,768]{2,1,0:T(8,128)(2,1)S(1)}, u32[]{:S(2)}, u32[]{:S(2)}) collective-permute-start(bf16[2,384,768]{2,1,0:T(8,128)(2,1)} %ints.1), channel_id=1, source_target_pairs={{0,8},{1,9},{2,10},{3,11},{4,12},{5,13},{6,14},{7,15},{8,0},{9,1},... | collective-permute-start | bytes 3538952 | tf_op jit(solution)/shard_map/ppermute | solution.py:150
  0.5 2.8 %collective-permute-start = (bf16[2,32,384]{2,1,0:T(8,128)(2,1)}, bf16[2,32,384]{2,1,0:T(8,128)(2,1)S(1)}, u32[]{:S(2)}, u32[]{:S(2)}) collective-permute-start(bf16[2,32,384]{2,1,0:T(8,128)(2,1)} %mine.1), channel_id=1, source_target_pairs={{0,8},{1,9},{2,10},{3,11},{4,12},{5,13},{6,14},{7,15},{8,0},{9,1},... | collective-permute-start | bytes 147464 | tf_op jit(solution)/shard_map/ppermute | solution.py:150
  3.2 0.8 %copy-start.1 = (bf16[2,32,384]{2,1,0:T(8,128)(2,1)S(1)}, bf16[2,32,384]{2,1,0:T(8,128)(2,1)}, u32[]{:S(2)}) copy-start(bf16[2,32,384]{2,1,0:T(8,128)(2,1)} %mine.1) | copy-start | bytes 147460
  4.0 7.9 %collective-permute-start.2 = (bf16[2,2,32,384]{3,2,1,0:T(8,128)(2,1)S(1)}, bf16[2,2,32,384]{3,2,1,0:T(8,128)(2,1)S(1)}, u32[]{:S(2)}, u32[]{:S(2)}) collective-permute-start(bf16[2,2,32,384]{3,2,1,0:T(8,128)(2,1)S(1)} %join.1.refs_1_), channel_id=1, source_target_pairs={{0,2},{1,3},{2,0},{3,1},{4,6},{5,7},{6,4},{7,5},{8,14},{9,15},{10,... | collective-permute-start | bytes 294920 | tf_op jit(solution)/shard_map/ppermute | solution.py:150
  7.0 4.9 %collective-permute-start.1 = (bf16[2,2,32,384]{3,2,1,0:T(8,128)(2,1)S(1)}, bf16[2,2,32,384]{3,2,1,0:T(8,128)(2,1)S(1)}, u32[]{:S(2)}, u32[]{:S(2)}) collective-permute-start(bf16[2,2,32,384]{3,2,1,0:T(8,128)(2,1)S(1)} %join.1.refs_1_), channel_id=1, source_target_pairs={{0,16},{1,17},{2,18},{3,19},{4,20},{5,21},{6,22},{7,23},{8,12},{9,... | collective-permute-start | bytes 294920 | tf_op jit(solution)/shard_map/ppermute | solution.py:150
  8.5 1.3 %copy-start = (bf16[2,384,768]{2,1,0:T(8,128)(2,1)S(1)}, bf16[2,384,768]{2,1,0:T(8,128)(2,1)}, u32[]{:S(2)}) copy-start(bf16[2,384,768]{2,1,0:T(8,128)(2,1)} %ints.1) | copy-start | bytes 3538948
  9.8 0.7 %copy-start.2 = (s32[2]{0:T(128)S(1)}, s32[2]{0:T(128)}, u32[]{:S(2)}) copy-start(s32[2]{0:T(128)} %occ.1) | copy-start | bytes 28
  10.4 0.7 %copy-start.3 = (s32[2]{0:T(128)S(1)}, s32[2]{0:T(128)}, u32[]{:S(2)}) copy-start(s32[2]{0:T(128)} %live.1) | copy-start | bytes 28
  12.8 4.8 %collective-permute-start.4 = (f32[192,128]{1,0:T(8,128)S(1)}, f32[192,128]{1,0:T(8,128)S(1)}, u32[]{:S(2)}, u32[]{:S(2)}) collective-permute-start(f32[192,128]{1,0:T(8,128)S(1)} %get-tuple-element.18), channel_id=1, source_target_pairs={{0,1},{1,0},{2,3},{3,2},{4,5},{5,4},{6,7},{7,6},{8,9},{9,8},{10,11... | collective-permute-start | bytes 294920 | tf_op jit(solution)/shard_map/ppermute | solution.py:150
  14.4 5.1 %collective-permute-start.5 = (f32[192,128]{1,0:T(8,128)S(1)}, f32[192,128]{1,0:T(8,128)S(1)}, u32[]{:S(2)}, u32[]{:S(2)}) collective-permute-start(f32[192,128]{1,0:T(8,128)S(1)} %get-tuple-element.19), channel_id=1, source_target_pairs={{0,16},{1,17},{2,18},{3,19},{4,20},{5,21},{6,22},{7,23},{8,24},{9,... | collective-permute-start | bytes 294920 | tf_op jit(solution)/shard_map/ppermute | solution.py:150
  15.6 6.0 %collective-permute-start.6 = (f32[192,128]{1,0:T(8,128)S(1)}, f32[192,128]{1,0:T(8,128)S(1)}, u32[]{:S(2)}, u32[]{:S(2)}) collective-permute-start(f32[192,128]{1,0:T(8,128)S(1)} %get-tuple-element.20), channel_id=1, source_target_pairs={{0,17},{1,16},{2,19},{3,18},{4,21},{5,20},{6,23},{7,22},{8,25},{9,... | collective-permute-start | bytes 294920 | tf_op jit(solution)/shard_map/ppermute | solution.py:150
  21.7 4.0 %collective-permute-start.8 = (bf16[2,2,32,96]{3,2,1,0:T(8,128)(2,1)S(1)}, bf16[2,2,32,96]{3,2,1,0:T(8,128)(2,1)S(1)}, u32[]{:S(2)}, u32[]{:S(2)}) collective-permute-start(bf16[2,2,32,96]{3,2,1,0:T(8,128)(2,1)S(1)} %get-tuple-element.22), channel_id=1, source_target_pairs={{0,2},{1,3},{2,0},{3,1},{4,6},{5,7},{6,4},{7,5},{8,14},{9,15},{10,... | collective-permute-start | bytes 73736 | tf_op jit(solution)/shard_map/ppermute | solution.py:150
  22.8 3.9 %collective-permute-start.7 = (bf16[2,2,32,96]{3,2,1,0:T(8,128)(2,1)S(1)}, bf16[2,2,32,96]{3,2,1,0:T(8,128)(2,1)S(1)}, u32[]{:S(2)}, u32[]{:S(2)}) collective-permute-start(bf16[2,2,32,96]{3,2,1,0:T(8,128)(2,1)S(1)} %get-tuple-element.21.refs_0_), channel_id=1, source_target_pairs={{0,16},{1,17},{2,18},{3,19},{4,20},{5,21},{6,22},{7,23},{8,12},{9,... | collective-permute-start | bytes 73736 | tf_op jit(solution)/shard_map/ppermute | solution.py:150
  26.7 1.7 %collective-permute-start.9 = (bf16[2,2,32,96]{3,2,1,0:T(8,128)(2,1)S(1)}, bf16[2,2,32,96]{3,2,1,0:T(8,128)(2,1)S(1)}, u32[]{:S(2)}, u32[]{:S(2)}) collective-permute-start(bf16[2,2,32,96]{3,2,1,0:T(8,128)(2,1)S(1)} %get-tuple-element.24), channel_id=1, source_target_pairs={{0,8},{1,9},{2,10},{3,11},{4,12},{5,13},{6,14},{7,15},{8,0},{9,1},... | collective-permute-start | bytes 73736 | tf_op jit(solution)/shard_map/ppermute | solution.py:150

commit v3 on v2

--- a/solution.py
+++ b/solution.py
@@ -12,18 +12,16 @@
 AXES = ("row", "col", "depth")
 VMEM = pl.BlockSpec(memory_space=pltpu.VMEM)
 SMEM = pl.BlockSpec(memory_space=pltpu.SMEM)
-HBM = pl.BlockSpec(memory_space=pl.ANY)
-
-
-def load(occ, live, ints, held, limits, sem):
-    copies = [pltpu.make_async_copy(ints.at[g], held.at[g], sem.at[g]) for g in range(ints.shape[0])]
-    for copy in copies:
-        copy.start()
-    for g in range(ints.shape[0]):
+
+
+def spread(occ, live, limits):
+    for g in range(limits.shape[1]):
         limits[0, g] = jnp.full(limits.shape[2:], occ[g], jnp.int32)
         limits[1, g] = jnp.full(limits.shape[2:], live[g], jnp.int32)
-    for copy in copies:
-        copy.wait()
+
+
+def copy(src, dst):
+    dst[...] = src[...]
 
 
 def join(mine, other, both):
@@ -115,7 +113,7 @@
         out[col ^ (q + (1 - core) * half)] = came[q]
 
 
-def call(kernel, name, specs, outs, *args, scratch=(), cost=None):
+def call(kernel, name, specs, outs, *args, scratch=()):
     many = isinstance(outs, list)
     return pl.pallas_call(
         kernel,
@@ -124,7 +122,6 @@
         in_specs=specs + [VMEM] * (len(args) - len(specs)),
         out_specs=[VMEM] * len(outs) if many else VMEM,
         scratch_shapes=list(scratch),
-        cost_estimate=cost,
         compiler_params=pltpu.CompilerParams(vmem_limit_bytes=40 * 2**20),
     )(*args)
 
@@ -161,16 +158,15 @@
         return move
 
     amps_other = send(amplitudes, other_core)
-    ints_other = send(integrals, other_core)
-    both = call(join, "join", [], shape((2, irreps, mb, kb), BF16), amplitudes, amps_other)
+    ints = call(copy, "load", [], shape(integrals.shape, BF16), integrals)
+    limits = call(
+        spread, "spread", [SMEM, SMEM], shape((2, irreps, 8, 128), jnp.int32), occ_count, virtual_pair_count
+    )
+    mine = call(copy, "fetch", [], shape(amplitudes.shape, BF16), amplitudes)
+    both = call(join, "join", [], shape((2, irreps, mb, kb), BF16), mine, amps_other)
+    later, both = lax.optimization_barrier((integrals, both))
+    ints_other = send(later, other_core)
     came = [send(both, chunk(q)) for q in range(half)]
-    ints, limits = call(
-        load, "load", [SMEM, SMEM, HBM],
-        [shape(integrals.shape, BF16), shape((2, irreps, 8, 128), jnp.int32)],
-        occ_count, virtual_pair_count, integrals,
-        scratch=[pltpu.SemaphoreType.DMA((irreps,))],
-        cost=pl.CostEstimate(flops=0, bytes_accessed=4 * integrals.size, transcendentals=0),
-    )
 
     steps = [(sx, sd) for sx in range(chips) for sd in range(depths)]
     lanes = irreps * half * mb

time: 29.2 us -> 26.9 us (0.921)
  local copies, waits for them, and re-layouts: 3.38 us -> 2.08 us
  waiting for transfers between devices: 11.8 us -> 10.6 us
  starting transfers between devices: 11.3 us -> 11.7 us
    unnamed x8, local copies, waits for them, and re-layouts: 3.38 us -> 2.08 us
    ppermute x10, waiting for transfers between devices: 11.8 us -> 10.6 us  [send(): return lax.ppermute(value, AXES, pairs(move))]
    ppermute x10, starting transfers between devices: 11.3 us -> 11.7 us  [send(): return lax.ppermute(value, AXES, pairs(move))]
    pallas_call x6 -> x8, Pallas kernels: 2.44 us -> 2.25 us  [call(): pl.pallas_call(kernel, name=name, out_shape=outs, in_specs=specs + [VMEM]...]
  transfers between devices with their start and end apart: 10 -> 10, of which waited for: 7 -> 8; matrix products, arithmetic and copies ran while one was open for 0% -> 0% of each run, Pallas kernels for 3% -> 2%
where the time goes in v3:
time: 26.9 us; the launch traced here: 26.7 us
  starting transfers between devices  11.7 us (43%)
  waiting for transfers between devices  10.6 us (39%)
  Pallas kernels  2.25 us (8%)
  local copies, waits for them, and re-layouts  2.08 us (8%)
    ppermute x10, starting transfers between devices, send(): return lax.ppermute(value, AXES, pairs(move))  11.7 us
    ppermute x10, waiting for transfers between devices, send(): return lax.ppermute(value, AXES, pairs(move))  10.6 us
    pallas_call x8, Pallas kernels, call(): pl.pallas_call(kernel, name=name, out_shape=outs, in_specs=specs + [VMEM]...  2.25 us
    unnamed x8, local copies, waits for them, and re-layouts  2.08 us
  transfers between devices with their start and end apart: 10, of which 8 were waited for; matrix products, arithmetic and copies ran while one was open for 0% of the time, Pallas kernels for 2%

profile of v3, /device:TPU:0, one launch (start us, length us, event | category | flops | bytes accessed | tf_op | source)
XLA Modules:
  0.0 26.7 jit_solution(16348753990563081114)
XLA Ops:
  0.0 0.5 %collective-permute-start = (bf16[2,32,384]{2,1,0:T(8,128)(2,1)}, bf16[2,32,384]{2,1,0:T(8,128)(2,1)S(1)}, u32[]{:S(2)}, u32[]{:S(2)}) collective-permute-start(bf16[2,32,384]{2,1,0:T(8,128)(2,1)} %src.2), channel_id=1, source_target_pairs={{0,8},{1,9},{2,10},{3,11},{4,12},{5,13},{6,14},{7,15},{8,0},{9,1},... | collective-permute-start | bytes 147464 | tf_op jit(solution)/shard_map/ppermute | solution.py:147
  0.5 0.0 copy-start.1
  0.5 0.8 %copy-done.1 = bf16[2,32,384]{2,1,0:T(8,128)(2,1)S(1)} copy-done((bf16[2,32,384]{2,1,0:T(8,128)(2,1)S(1)}, bf16[2,32,384]{2,1,0:T(8,128)(2,1)}, u32[]{:S(2)}) %copy-start.1) | copy-done | bytes 49176
  1.3 0.3 %collective-permute-done.other = bf16[2,32,384]{2,1,0:T(8,128)(2,1)S(1)} collective-permute-done((bf16[2,32,384]{2,1,0:T(8,128)(2,1)}, bf16[2,32,384]{2,1,0:T(8,128)(2,1)S(1)}, u32[]{:S(2)}, u32[]{:S(2)}) %collective-permute-start) | collective-permute-done | bytes 49184 | tf_op jit(solution)/shard_map/ppermute | solution.py:147
  1.5 0.0 copy-start.2
  1.5 0.0 copy-start.3
  1.6 0.4 %collective-permute-start.3 = (bf16[2,384,768]{2,1,0:T(8,128)(2,1)}, bf16[2,384,768]{2,1,0:T(8,128)(2,1)S(1)}, u32[]{:S(2)}, u32[]{:S(2)}) collective-permute-start(bf16[2,384,768]{2,1,0:T(8,128)(2,1)} %src.3), channel_id=1, source_target_pairs={{0,8},{1,9},{2,10},{3,11},{4,12},{5,13},{6,14},{7,15},{8,0},{9,1},... | collective-permute-start | bytes 3538952 | tf_op jit(solution)/shard_map/ppermute | solution.py:147
  2.0 2.7 %collective-permute-start.2 = (bf16[2,2,32,384]{3,2,1,0:T(8,128)(2,1)S(1)}, bf16[2,2,32,384]{3,2,1,0:T(8,128)(2,1)S(1)}, u32[]{:S(2)}, u32[]{:S(2)}) collective-permute-start(bf16[2,2,32,384]{3,2,1,0:T(8,128)(2,1)S(1)} %join.1.refs_1_), channel_id=1, source_target_pairs={{0,2},{1,3},{2,0},{3,1},{4,6},{5,7},{6,4},{7,5},{8,14},{9,15},{10,... | collective-permute-start | bytes 294920 | tf_op jit(solution)/shard_map/ppermute | solution.py:147
  4.7 1.5 %collective-permute-start.1 = (bf16[2,2,32,384]{3,2,1,0:T(8,128)(2,1)S(1)}, bf16[2,2,32,384]{3,2,1,0:T(8,128)(2,1)S(1)}, u32[]{:S(2)}, u32[]{:S(2)}) collective-permute-start(bf16[2,2,32,384]{3,2,1,0:T(8,128)(2,1)S(1)} %join.1.refs_1_), channel_id=1, source_target_pairs={{0,16},{1,17},{2,18},{3,19},{4,20},{5,21},{6,22},{7,23},{8,12},{9,... | collective-permute-start | bytes 294920 | tf_op jit(solution)/shard_map/ppermute | solution.py:147
  6.2 0.0 copy-start
  6.2 1.3 %copy-done = bf16[2,384,768]{2,1,0:T(8,128)(2,1)S(1)} copy-done((bf16[2,384,768]{2,1,0:T(8,128)(2,1)S(1)}, bf16[2,384,768]{2,1,0:T(8,128)(2,1)}, u32[]{:S(2)}) %copy-start) | copy-done | bytes 1179672
  7.5 0.1 load.1.refs_4_
  7.6 0.0 copy-done.2
  7.6 0.0 copy-done.3
  7.6 0.5 %spread.1.refs_0_ = s32[2,2,8,128]{3,2,1,0:T(8,128)S(1)} custom-call(s32[2]{0:T(128)S(1)} %copy-done.2, s32[2]{0:T(128)S(1)} %copy-done.3), custom_call_target="tpu_custom_call" | custom-call | tf_op jit(solution)/shard_map/spread/pallas_call | solution.py:118
  8.1 0.0 collective-permute-done.2.refs_3_
  8.1 1.2 %collective-permute-done.1.refs_2_ = bf16[2,2,32,384]{3,2,1,0:T(8,128)(2,1)S(1)} collective-permute-done((bf16[2,2,32,384]{3,2,1,0:T(8,128)(2,1)S(1)}, bf16[2,2,32,384]{3,2,1,0:T(8,128)(2,1)S(1)}, u32[]{:S(2)}, u32[]{:S(2)}) %collective-permute-start.1) | collective-permute-done | bytes 98336 | tf_op jit(solution)/shard_map/ppermute | solution.py:147
  9.3 0.0 collective-permute-done.3.refs_5_
  9.3 0.8 %products.1 = (f32[192,128]{1,0:T(8,128)S(1)}, f32[192,128]{1,0:T(8,128)S(1)}, f32[192,128]{1,0:T(8,128)S(1)}, f32[192,128]{1,0:T(8,128)S(1)}) custom-call(s32[2,2,8,128]{3,2,1,0:T(8,128)S(1)} %spread.1.refs_0_, bf16[2,2,32,384]{3,2,1,0:T(8,128)(2,1)S(1)} %join.1.refs_1_, bf16[2,2,32,384]{3,2,1,0:T(8,128)(2,1)S(1)} %collective-permute-done.1.refs_2_, ...), custom_call_target="tpu_custom_call" | custom-call | tf_op jit(solution)/shard_map/products/pallas_call | solution.py:118
  10.2 1.6 %collective-permute-start.4 = (f32[192,128]{1,0:T(8,128)S(1)}, f32[192,128]{1,0:T(8,128)S(1)}, u32[]{:S(2)}, u32[]{:S(2)}) collective-permute-start(f32[192,128]{1,0:T(8,128)S(1)} %get-tuple-element.18), channel_id=1, source_target_pairs={{0,1},{1,0},{2,3},{3,2},{4,5},{5,4},{6,7},{7,6},{8,9},{9,8},{10,11... | collective-permute-start | bytes 294920 | tf_op jit(solution)/shard_map/ppermute | solution.py:147
  11.8 1.5 %collective-permute-start.5 = (f32[192,128]{1,0:T(8,128)S(1)}, f32[192,128]{1,0:T(8,128)S(1)}, u32[]{:S(2)}, u32[]{:S(2)}) collective-permute-start(f32[192,128]{1,0:T(8,128)S(1)} %get-tuple-element.19), channel_id=1, source_target_pairs={{0,16},{1,17},{2,18},{3,19},{4,20},{5,21},{6,22},{7,23},{8,24},{9,... | collective-permute-start | bytes 294920 | tf_op jit(solution)/shard_map/ppermute | solution.py:147
  13.3 0.5 %collective-permute-start.6 = (f32[192,128]{1,0:T(8,128)S(1)}, f32[192,128]{1,0:T(8,128)S(1)}, u32[]{:S(2)}, u32[]{:S(2)}) collective-permute-start(f32[192,128]{1,0:T(8,128)S(1)} %get-tuple-element.20), channel_id=1, source_target_pairs={{0,17},{1,16},{2,19},{3,18},{4,21},{5,20},{6,23},{7,22},{8,25},{9,... | collective-permute-start | bytes 294920 | tf_op jit(solution)/shard_map/ppermute | solution.py:147
  13.7 1.1 %collective-permute-done.4.refs_2_ = f32[192,128]{1,0:T(8,128)S(1)} collective-permute-done((f32[192,128]{1,0:T(8,128)S(1)}, f32[192,128]{1,0:T(8,128)S(1)}, u32[]{:S(2)}, u32[]{:S(2)}) %collective-permute-start.4) | collective-permute-done | bytes 98336 | tf_op jit(solution)/shard_map/ppermute | solution.py:147
  14.9 1.5 %collective-permute-done.5.refs_3_ = f32[192,128]{1,0:T(8,128)S(1)} collective-permute-done((f32[192,128]{1,0:T(8,128)S(1)}, f32[192,128]{1,0:T(8,128)S(1)}, u32[]{:S(2)}, u32[]{:S(2)}) %collective-permute-start.5) | collective-permute-done | bytes 98336 | tf_op jit(solution)/shard_map/ppermute | solution.py:147
  16.4 2.6 %collective-permute-done.6.refs_4_ = f32[192,128]{1,0:T(8,128)S(1)} collective-permute-done((f32[192,128]{1,0:T(8,128)S(1)}, f32[192,128]{1,0:T(8,128)S(1)}, u32[]{:S(2)}, u32[]{:S(2)}) %collective-permute-start.6) | collective-permute-done | bytes 98336 | tf_op jit(solution)/shard_map/ppermute | solution.py:147
  19.0 0.1 finish.1
  19.1 1.2 %collective-permute-start.8 = (bf16[2,2,32,96]{3,2,1,0:T(8,128)(2,1)S(1)}, bf16[2,2,32,96]{3,2,1,0:T(8,128)(2,1)S(1)}, u32[]{:S(2)}, u32[]{:S(2)}) collective-permute-start(bf16[2,2,32,96]{3,2,1,0:T(8,128)(2,1)S(1)} %get-tuple-element.22), channel_id=1, source_target_pairs={{0,2},{1,3},{2,0},{3,1},{4,6},{5,7},{6,4},{7,5},{8,14},{9,15},{10,... | collective-permute-start | bytes 73736 | tf_op jit(solution)/shard_map/ppermute | solution.py:147
  20.3 0.9 %collective-permute-start.7 = (bf16[2,2,32,96]{3,2,1,0:T(8,128)(2,1)S(1)}, bf16[2,2,32,96]{3,2,1,0:T(8,128)(2,1)S(1)}, u32[]{:S(2)}, u32[]{:S(2)}) collective-permute-start(bf16[2,2,32,96]{3,2,1,0:T(8,128)(2,1)S(1)} %get-tuple-element.21.refs_0_), channel_id=1, source_target_pairs={{0,16},{1,17},{2,18},{3,19},{4,20},{5,21},{6,22},{7,23},{8,12},{9,... | collective-permute-start | bytes 73736 | tf_op jit(solution)/shard_map/ppermute | solution.py:147
  21.2 1.9 %collective-permute-done.8.refs_2_ = bf16[2,2,32,96]{3,2,1,0:T(8,128)(2,1)S(1)} collective-permute-done((bf16[2,2,32,96]{3,2,1,0:T(8,128)(2,1)S(1)}, bf16[2,2,32,96]{3,2,1,0:T(8,128)(2,1)S(1)}, u32[]{:S(2)}, u32[]{:S(2)}) %collective-permute-start.8) | collective-permute-done | bytes 24608 | tf_op jit(solution)/shard_map/ppermute | solution.py:147
  23.1 1.1 %collective-permute-done.7.refs_1_ = bf16[2,2,32,96]{3,2,1,0:T(8,128)(2,1)S(1)} collective-permute-done((bf16[2,2,32,96]{3,2,1,0:T(8,128)(2,1)S(1)}, bf16[2,2,32,96]{3,2,1,0:T(8,128)(2,1)S(1)}, u32[]{:S(2)}, u32[]{:S(2)}) %collective-permute-start.7) | collective-permute-done | bytes 24608 | tf_op jit(solution)/shard_map/ppermute | solution.py:147
  24.2 1.0 %collective-permute-start.9 = (bf16[2,2,32,96]{3,2,1,0:T(8,128)(2,1)S(1)}, bf16[2,2,32,96]{3,2,1,0:T(8,128)(2,1)S(1)}, u32[]{:S(2)}, u32[]{:S(2)}) collective-permute-start(bf16[2,2,32,96]{3,2,1,0:T(8,128)(2,1)S(1)} %get-tuple-element.24), channel_id=1, source_target_pairs={{0,8},{1,9},{2,10},{3,11},{4,12},{5,13},{6,14},{7,15},{8,0},{9,1},... | collective-permute-start | bytes 73736 | tf_op jit(solution)/shard_map/ppermute | solution.py:147
  25.2 0.9 %collective-permute-done.9.came = bf16[2,2,32,96]{3,2,1,0:T(8,128)(2,1)S(1)} collective-permute-done((bf16[2,2,32,96]{3,2,1,0:T(8,128)(2,1)S(1)}, bf16[2,2,32,96]{3,2,1,0:T(8,128)(2,1)S(1)}, u32[]{:S(2)}, u32[]{:S(2)}) %collective-permute-start.9) | collective-permute-done | bytes 24608 | tf_op jit(solution)/shard_map/ppermute | solution.py:147
  26.0 0.6 %assemble.1 = bf16[4,2,32,96]{3,2,1,0:T(8,128)(2,1)} custom-call(bf16[2,2,32,96]{3,2,1,0:T(8,128)(2,1)S(1)} %get-tuple-element.23.keep, bf16[2,2,32,96]{3,2,1,0:T(8,128)(2,1)S(1)} %collective-permute-done.9.came), custom_call_target="tpu_custom_call" | custom-call | tf_op jit(solution)/shard_map/assemble/pallas_call | solution.py:118
  (3 shorter events, 0.0 us)
Async XLA Ops:
  0.0 1.5 %collective-permute-start = (bf16[2,32,384]{2,1,0:T(8,128)(2,1)}, bf16[2,32,384]{2,1,0:T(8,128)(2,1)S(1)}, u32[]{:S(2)}, u32[]{:S(2)}) collective-permute-start(bf16[2,32,384]{2,1,0:T(8,128)(2,1)} %src.2), channel_id=1, source_target_pairs={{0,8},{1,9},{2,10},{3,11},{4,12},{5,13},{6,14},{7,15},{8,0},{9,1},... | collective-permute-start | bytes 147464 | tf_op jit(solution)/shard_map/ppermute | solution.py:147
  0.5 0.8 %copy-start.1 = (bf16[2,32,384]{2,1,0:T(8,128)(2,1)S(1)}, bf16[2,32,384]{2,1,0:T(8,128)(2,1)}, u32[]{:S(2)}) copy-start(bf16[2,32,384]{2,1,0:T(8,128)(2,1)} %src.2) | copy-start | bytes 147460
  1.5 6.0 %copy-start.2 = (s32[2]{0:T(128)S(1)}, s32[2]{0:T(128)}, u32[]{:S(2)}) copy-start(s32[2]{0:T(128)} %occ.1) | copy-start | bytes 28
  1.5 6.0 %copy-start.3 = (s32[2]{0:T(128)S(1)}, s32[2]{0:T(128)}, u32[]{:S(2)}) copy-start(s32[2]{0:T(128)} %live.1) | copy-start | bytes 28
  1.6 7.8 %collective-permute-start.3 = (bf16[2,384,768]{2,1,0:T(8,128)(2,1)}, bf16[2,384,768]{2,1,0:T(8,128)(2,1)S(1)}, u32[]{:S(2)}, u32[]{:S(2)}) collective-permute-start(bf16[2,384,768]{2,1,0:T(8,128)(2,1)} %src.3), channel_id=1, source_target_pairs={{0,8},{1,9},{2,10},{3,11},{4,12},{5,13},{6,14},{7,15},{8,0},{9,1},... | collective-permute-start | bytes 3538952 | tf_op jit(solution)/shard_map/ppermute | solution.py:147
  2.0 6.2 %collective-permute-start.2 = (bf16[2,2,32,384]{3,2,1,0:T(8,128)(2,1)S(1)}, bf16[2,2,32,384]{3,2,1,0:T(8,128)(2,1)S(1)}, u32[]{:S(2)}, u32[]{:S(2)}) collective-permute-start(bf16[2,2,32,384]{3,2,1,0:T(8,128)(2,1)S(1)} %join.1.refs_1_), channel_id=1, source_target_pairs={{0,2},{1,3},{2,0},{3,1},{4,6},{5,7},{6,4},{7,5},{8,14},{9,15},{10,... | collective-permute-start | bytes 294920 | tf_op jit(solution)/shard_map/ppermute | solution.py:147
  4.7 4.6 %collective-permute-start.1 = (bf16[2,2,32,384]{3,2,1,0:T(8,128)(2,1)S(1)}, bf16[2,2,32,384]{3,2,1,0:T(8,128)(2,1)S(1)}, u32[]{:S(2)}, u32[]{:S(2)}) collective-permute-start(bf16[2,2,32,384]{3,2,1,0:T(8,128)(2,1)S(1)} %join.1.refs_1_), channel_id=1, source_target_pairs={{0,16},{1,17},{2,18},{3,19},{4,20},{5,21},{6,22},{7,23},{8,12},{9,... | collective-permute-start | bytes 294920 | tf_op jit(solution)/shard_map/ppermute | solution.py:147
  6.2 1.3 %copy-start = (bf16[2,384,768]{2,1,0:T(8,128)(2,1)S(1)}, bf16[2,384,768]{2,1,0:T(8,128)(2,1)}, u32[]{:S(2)}) copy-start(bf16[2,384,768]{2,1,0:T(8,128)(2,1)} %src.3) | copy-start | bytes 3538948
  10.2 4.7 %collective-permute-start.4 = (f32[192,128]{1,0:T(8,128)S(1)}, f32[192,128]{1,0:T(8,128)S(1)}, u32[]{:S(2)}, u32[]{:S(2)}) collective-permute-start(f32[192,128]{1,0:T(8,128)S(1)} %get-tuple-element.18), channel_id=1, source_target_pairs={{0,1},{1,0},{2,3},{3,2},{4,5},{5,4},{6,7},{7,6},{8,9},{9,8},{10,11... | collective-permute-start | bytes 294920 | tf_op jit(solution)/shard_map/ppermute | solution.py:147
  11.8 4.6 %collective-permute-start.5 = (f32[192,128]{1,0:T(8,128)S(1)}, f32[192,128]{1,0:T(8,128)S(1)}, u32[]{:S(2)}, u32[]{:S(2)}) collective-permute-start(f32[192,128]{1,0:T(8,128)S(1)} %get-tuple-element.19), channel_id=1, source_target_pairs={{0,16},{1,17},{2,18},{3,19},{4,20},{5,21},{6,22},{7,23},{8,24},{9,... | collective-permute-start | bytes 294920 | tf_op jit(solution)/shard_map/ppermute | solution.py:147
  13.3 5.7 %collective-permute-start.6 = (f32[192,128]{1,0:T(8,128)S(1)}, f32[192,128]{1,0:T(8,128)S(1)}, u32[]{:S(2)}, u32[]{:S(2)}) collective-permute-start(f32[192,128]{1,0:T(8,128)S(1)} %get-tuple-element.20), channel_id=1, source_target_pairs={{0,17},{1,16},{2,19},{3,18},{4,21},{5,20},{6,23},{7,22},{8,25},{9,... | collective-permute-start | bytes 294920 | tf_op jit(solution)/shard_map/ppermute | solution.py:147
  19.1 4.0 %collective-permute-start.8 = (bf16[2,2,32,96]{3,2,1,0:T(8,128)(2,1)S(1)}, bf16[2,2,32,96]{3,2,1,0:T(8,128)(2,1)S(1)}, u32[]{:S(2)}, u32[]{:S(2)}) collective-permute-start(bf16[2,2,32,96]{3,2,1,0:T(8,128)(2,1)S(1)} %get-tuple-element.22), channel_id=1, source_target_pairs={{0,2},{1,3},{2,0},{3,1},{4,6},{5,7},{6,4},{7,5},{8,14},{9,15},{10,... | collective-permute-start | bytes 73736 | tf_op jit(solution)/shard_map/ppermute | solution.py:147
  20.3 3.9 %collective-permute-start.7 = (bf16[2,2,32,96]{3,2,1,0:T(8,128)(2,1)S(1)}, bf16[2,2,32,96]{3,2,1,0:T(8,128)(2,1)S(1)}, u32[]{:S(2)}, u32[]{:S(2)}) collective-permute-start(bf16[2,2,32,96]{3,2,1,0:T(8,128)(2,1)S(1)} %get-tuple-element.21.refs_0_), channel_id=1, source_target_pairs={{0,16},{1,17},{2,18},{3,19},{4,20},{5,21},{6,22},{7,23},{8,12},{9,... | collective-permute-start | bytes 73736 | tf_op jit(solution)/shard_map/ppermute | solution.py:147
  24.2 1.8 %collective-permute-start.9 = (bf16[2,2,32,96]{3,2,1,0:T(8,128)(2,1)S(1)}, bf16[2,2,32,96]{3,2,1,0:T(8,128)(2,1)S(1)}, u32[]{:S(2)}, u32[]{:S(2)}) collective-permute-start(bf16[2,2,32,96]{3,2,1,0:T(8,128)(2,1)S(1)} %get-tuple-element.24), channel_id=1, source_target_pairs={{0,8},{1,9},{2,10},{3,11},{4,12},{5,13},{6,14},{7,15},{8,0},{9,1},... | collective-permute-start | bytes 73736 | tf_op jit(solution)/shard_map/ppermute | solution.py:147

commit v4 on v3

--- a/solution.py
+++ b/solution.py
@@ -27,11 +27,6 @@
 def join(mine, other, both):
     both[0] = mine[...]
     both[1] = other[...]
-
-
-def chunk_masks(cols):
-    half = cols // 2
-    return list(range(half)), list(range(half, cols))
 
 
 def products(sizes, steps, *refs):
@@ -97,19 +92,24 @@
 
 
 def settle(half, *refs):
-    first, came, keep, send = refs[0], refs[1 : 1 + half], refs[-2], refs[-1]
+    back, give = refs[:half][::-1], refs[-1]
     core = lax.rem(lax.axis_index("row"), 2)
-    for ref, c in ((keep, core), (send, 1 - core)):
-        ref[0] = jnp.where(core == 0, first[c].astype(F32), came[0][c].astype(F32)).astype(BF16)
-        for q in range(1, half):
-            ref[q] = came[q][c]
-
-
-def assemble(half, keep, came, out):
+    for q in range(half):
+        give[q] = back[q][1 - core]
+
+
+def assemble(half, first, *refs):
+    back, came, out = refs[:half][::-1], refs[-2], refs[-1]
     core = lax.rem(lax.axis_index("row"), 2)
     col = lax.axis_index("col")
-    for q in range(half):
-        out[col ^ (q + core * half)] = keep[q]
+
+    def pick(zero, one):
+        return jnp.where(core == 0, zero.astype(F32), one.astype(F32)).astype(BF16)
+
+    out[col] = pick(first[0], back[0][1])
+    out[col ^ half] = pick(back[0][0], came[0])
+    for q in range(1, half):
+        out[col ^ (q + core * half)] = back[q][core]
         out[col ^ (q + (1 - core) * half)] = came[q]
 
 
@@ -168,7 +168,8 @@
     ints_other = send(later, other_core)
     came = [send(both, chunk(q)) for q in range(half)]
 
-    steps = [(sx, sd) for sx in range(chips) for sd in range(depths)]
+    steps = [(sx, sd) for sx in range(chips) for sd in reversed(range(depths))]
+    steps = [(0, 0)] + [step for step in steps if any(step)]
     lanes = irreps * half * mb
     out = call(
         functools.partial(products, sizes, steps), "products", [], [shape((2 * h, lanes), F32)] * len(steps),
@@ -176,18 +177,20 @@
         scratch=[pltpu.VMEM((nb, lanes), F32)],
     )
     sums = [out[0]]
-    for (sx, sd), part in list(zip(steps, out))[1:]:
+    for (sx, sd), part in zip(steps[1:], out[1:]):
         sums.append(send(part, lambda row, col, dep, sx=sx, sd=sd: (row ^ 2 * sx, col, dep ^ sd)))
 
     done = call(
         functools.partial(finish, sizes), "finish", [], [shape((2, irreps, mb, h), BF16)] * half, limits, *sums
     )
-    back = [send(done[q], chunk(q)) for q in range(half)]
-    blocks = shape((half, irreps, mb, h), BF16)
-    keep, give = call(functools.partial(settle, half), "settle", [], [blocks, blocks], done[0], *back)
+    def home(row, col, dep):
+        return (row ^ 1, col ^ half, dep) if row % 2 else (row ^ 1, col, dep)
+
+    back = [send(done[q], chunk(q) if q else home) for q in range(half)]
+    give = call(functools.partial(settle, half), "settle", [], shape((half, irreps, mb, h), BF16), *back[::-1])
     result = call(
         functools.partial(assemble, half), "assemble", [], shape((cols, irreps, mb, h), BF16),
-        keep, send(give, other_core),
+        done[0], *back[::-1], send(give, other_core),
     )
     return result.transpose(0, 3, 1, 2)
 

time: 26.9 us -> 26.2 us (0.974)
  waiting for transfers between devices: 10.6 us -> 9.45 us
  starting transfers between devices: 11.7 us -> 12.2 us
    ppermute x10, waiting for transfers between devices: 10.6 us -> 9.45 us  [send(): return lax.ppermute(value, AXES, pairs(move))]
    ppermute x10, starting transfers between devices: 11.7 us -> 12.2 us  [send(): return lax.ppermute(value, AXES, pairs(move))]
where the time goes in v4:
time: 26.2 us; the launch traced here: 26 us
  starting transfers between devices  12.2 us (47%)
  waiting for transfers between devices  9.45 us (36%)
  Pallas kernels  2.24 us (9%)
  local copies, waits for them, and re-layouts  2.08 us (8%)
    ppermute x10, starting transfers between devices, send(): return lax.ppermute(value, AXES, pairs(move))  12.2 us
    ppermute x10, waiting for transfers between devices, send(): return lax.ppermute(value, AXES, pairs(move))  9.45 us
    pallas_call x8, Pallas kernels, call(): pl.pallas_call(kernel, name=name, out_shape=outs, in_specs=specs + [VMEM]...  2.24 us
    unnamed x8, local copies, waits for them, and re-layouts  2.08 us
  transfers between devices with their start and end apart: 10, of which 8 were waited for; matrix products, arithmetic and copies ran while one was open for 0% of the time, Pallas kernels for 2%

profile of v4, /device:TPU:0, one launch (start us, length us, event | category | flops | bytes accessed | tf_op | source)
XLA Modules:
  0.0 26.0 jit_solution(9247046115172324129)
XLA Ops:
  0.0 0.5 %collective-permute-start = (bf16[2,32,384]{2,1,0:T(8,128)(2,1)}, bf16[2,32,384]{2,1,0:T(8,128)(2,1)S(1)}, u32[]{:S(2)}, u32[]{:S(2)}) collective-permute-start(bf16[2,32,384]{2,1,0:T(8,128)(2,1)} %src.2), channel_id=1, source_target_pairs={{0,8},{1,9},{2,10},{3,11},{4,12},{5,13},{6,14},{7,15},{8,0},{9,1},... | collective-permute-start | bytes 147464 | tf_op jit(solution)/shard_map/ppermute | solution.py:147
  0.5 0.0 copy-start.1
  0.5 0.8 %copy-done.1 = bf16[2,32,384]{2,1,0:T(8,128)(2,1)S(1)} copy-done((bf16[2,32,384]{2,1,0:T(8,128)(2,1)S(1)}, bf16[2,32,384]{2,1,0:T(8,128)(2,1)}, u32[]{:S(2)}) %copy-start.1) | copy-done | bytes 49176
  1.3 0.3 %collective-permute-done.other = bf16[2,32,384]{2,1,0:T(8,128)(2,1)S(1)} collective-permute-done((bf16[2,32,384]{2,1,0:T(8,128)(2,1)}, bf16[2,32,384]{2,1,0:T(8,128)(2,1)S(1)}, u32[]{:S(2)}, u32[]{:S(2)}) %collective-permute-start) | collective-permute-done | bytes 49184 | tf_op jit(solution)/shard_map/ppermute | solution.py:147
  1.5 0.0 copy-start.2
  1.5 0.0 copy-start.3
  1.6 0.4 %collective-permute-start.3 = (bf16[2,384,768]{2,1,0:T(8,128)(2,1)}, bf16[2,384,768]{2,1,0:T(8,128)(2,1)S(1)}, u32[]{:S(2)}, u32[]{:S(2)}) collective-permute-start(bf16[2,384,768]{2,1,0:T(8,128)(2,1)} %src.3), channel_id=1, source_target_pairs={{0,8},{1,9},{2,10},{3,11},{4,12},{5,13},{6,14},{7,15},{8,0},{9,1},... | collective-permute-start | bytes 3538952 | tf_op jit(solution)/shard_map/ppermute | solution.py:147
  2.0 2.7 %collective-permute-start.2 = (bf16[2,2,32,384]{3,2,1,0:T(8,128)(2,1)S(1)}, bf16[2,2,32,384]{3,2,1,0:T(8,128)(2,1)S(1)}, u32[]{:S(2)}, u32[]{:S(2)}) collective-permute-start(bf16[2,2,32,384]{3,2,1,0:T(8,128)(2,1)S(1)} %join.1.refs_1_), channel_id=1, source_target_pairs={{0,2},{1,3},{2,0},{3,1},{4,6},{5,7},{6,4},{7,5},{8,14},{9,15},{10,... | collective-permute-start | bytes 294920 | tf_op jit(solution)/shard_map/ppermute | solution.py:147
  4.7 1.5 %collective-permute-start.1 = (bf16[2,2,32,384]{3,2,1,0:T(8,128)(2,1)S(1)}, bf16[2,2,32,384]{3,2,1,0:T(8,128)(2,1)S(1)}, u32[]{:S(2)}, u32[]{:S(2)}) collective-permute-start(bf16[2,2,32,384]{3,2,1,0:T(8,128)(2,1)S(1)} %join.1.refs_1_), channel_id=1, source_target_pairs={{0,16},{1,17},{2,18},{3,19},{4,20},{5,21},{6,22},{7,23},{8,12},{9,... | collective-permute-start | bytes 294920 | tf_op jit(solution)/shard_map/ppermute | solution.py:147
  6.2 0.0 copy-start
  6.2 1.3 %copy-done = bf16[2,384,768]{2,1,0:T(8,128)(2,1)S(1)} copy-done((bf16[2,384,768]{2,1,0:T(8,128)(2,1)S(1)}, bf16[2,384,768]{2,1,0:T(8,128)(2,1)}, u32[]{:S(2)}) %copy-start) | copy-done | bytes 1179672
  7.5 0.1 load.1.refs_4_
  7.6 0.0 copy-done.2
  7.6 0.0 copy-done.3
  7.6 0.5 %spread.1.refs_0_ = s32[2,2,8,128]{3,2,1,0:T(8,128)S(1)} custom-call(s32[2]{0:T(128)S(1)} %copy-done.2, s32[2]{0:T(128)S(1)} %copy-done.3), custom_call_target="tpu_custom_call" | custom-call | tf_op jit(solution)/shard_map/spread/pallas_call | solution.py:118
  8.1 0.0 collective-permute-done.2.refs_3_
  8.1 1.2 %collective-permute-done.1.refs_2_ = bf16[2,2,32,384]{3,2,1,0:T(8,128)(2,1)S(1)} collective-permute-done((bf16[2,2,32,384]{3,2,1,0:T(8,128)(2,1)S(1)}, bf16[2,2,32,384]{3,2,1,0:T(8,128)(2,1)S(1)}, u32[]{:S(2)}, u32[]{:S(2)}) %collective-permute-start.1) | collective-permute-done | bytes 98336 | tf_op jit(solution)/shard_map/ppermute | solution.py:147
  9.3 0.0 collective-permute-done.3.refs_5_
  9.3 0.8 %products.1 = (f32[192,128]{1,0:T(8,128)S(1)}, f32[192,128]{1,0:T(8,128)S(1)}, f32[192,128]{1,0:T(8,128)S(1)}, f32[192,128]{1,0:T(8,128)S(1)}) custom-call(s32[2,2,8,128]{3,2,1,0:T(8,128)S(1)} %spread.1.refs_0_, bf16[2,2,32,384]{3,2,1,0:T(8,128)(2,1)S(1)} %join.1.refs_1_, bf16[2,2,32,384]{3,2,1,0:T(8,128)(2,1)S(1)} %collective-permute-done.1.refs_2_, ...), custom_call_target="tpu_custom_call" | custom-call | tf_op jit(solution)/shard_map/products/pallas_call | solution.py:118
  10.2 1.6 %collective-permute-start.4 = (f32[192,128]{1,0:T(8,128)S(1)}, f32[192,128]{1,0:T(8,128)S(1)}, u32[]{:S(2)}, u32[]{:S(2)}) collective-permute-start(f32[192,128]{1,0:T(8,128)S(1)} %get-tuple-element.16), channel_id=1, source_target_pairs={{0,1},{1,0},{2,3},{3,2},{4,5},{5,4},{6,7},{7,6},{8,9},{9,8},{10,11... | collective-permute-start | bytes 294920 | tf_op jit(solution)/shard_map/ppermute | solution.py:147
  11.8 1.4 %collective-permute-start.5 = (f32[192,128]{1,0:T(8,128)S(1)}, f32[192,128]{1,0:T(8,128)S(1)}, u32[]{:S(2)}, u32[]{:S(2)}) collective-permute-start(f32[192,128]{1,0:T(8,128)S(1)} %get-tuple-element.17), channel_id=1, source_target_pairs={{0,17},{1,16},{2,19},{3,18},{4,21},{5,20},{6,23},{7,22},{8,25},{9,... | collective-permute-start | bytes 294920 | tf_op jit(solution)/shard_map/ppermute | solution.py:147
  13.2 0.5 %collective-permute-start.6 = (f32[192,128]{1,0:T(8,128)S(1)}, f32[192,128]{1,0:T(8,128)S(1)}, u32[]{:S(2)}, u32[]{:S(2)}) collective-permute-start(f32[192,128]{1,0:T(8,128)S(1)} %get-tuple-element.18), channel_id=1, source_target_pairs={{0,16},{1,17},{2,18},{3,19},{4,20},{5,21},{6,22},{7,23},{8,24},{9,... | collective-permute-start | bytes 294920 | tf_op jit(solution)/shard_map/ppermute | solution.py:147
  13.7 1.1 %collective-permute-done.4.refs_2_ = f32[192,128]{1,0:T(8,128)S(1)} collective-permute-done((f32[192,128]{1,0:T(8,128)S(1)}, f32[192,128]{1,0:T(8,128)S(1)}, u32[]{:S(2)}, u32[]{:S(2)}) %collective-permute-start.4) | collective-permute-done | bytes 98336 | tf_op jit(solution)/shard_map/ppermute | solution.py:147
  14.9 2.5 %collective-permute-done.5.refs_3_ = f32[192,128]{1,0:T(8,128)S(1)} collective-permute-done((f32[192,128]{1,0:T(8,128)S(1)}, f32[192,128]{1,0:T(8,128)S(1)}, u32[]{:S(2)}, u32[]{:S(2)}) %collective-permute-start.5) | collective-permute-done | bytes 98336 | tf_op jit(solution)/shard_map/ppermute | solution.py:147
  17.3 1.4 %collective-permute-done.6.refs_4_ = f32[192,128]{1,0:T(8,128)S(1)} collective-permute-done((f32[192,128]{1,0:T(8,128)S(1)}, f32[192,128]{1,0:T(8,128)S(1)}, u32[]{:S(2)}, u32[]{:S(2)}) %collective-permute-start.6) | collective-permute-done | bytes 98336 | tf_op jit(solution)/shard_map/ppermute | solution.py:147
  18.8 0.1 finish.1
  18.9 0.6 %collective-permute-start.7 = (bf16[2,2,32,96]{3,2,1,0:T(8,128)(2,1)S(1)}, bf16[2,2,32,96]{3,2,1,0:T(8,128)(2,1)S(1)}, u32[]{:S(2)}, u32[]{:S(2)}) collective-permute-start(bf16[2,2,32,96]{3,2,1,0:T(8,128)(2,1)S(1)} %get-tuple-element.20), channel_id=1, source_target_pairs={{0,2},{1,3},{2,0},{3,1},{4,6},{5,7},{6,4},{7,5},{8,14},{9,15},{10,... | collective-permute-start | bytes 73736 | tf_op jit(solution)/shard_map/ppermute | solution.py:147
  19.5 2.2 %collective-permute-start.8 = (bf16[2,2,32,96]{3,2,1,0:T(8,128)(2,1)S(1)}, bf16[2,2,32,96]{3,2,1,0:T(8,128)(2,1)S(1)}, u32[]{:S(2)}, u32[]{:S(2)}) collective-permute-start(bf16[2,2,32,96]{3,2,1,0:T(8,128)(2,1)S(1)} %get-tuple-element.19.first), channel_id=1, source_target_pairs={{0,8},{1,9},{2,10},{3,11},{4,12},{5,13},{6,14},{7,15},{8,4},{9,5},... | collective-permute-start | bytes 73736 | tf_op jit(solution)/shard_map/ppermute | solution.py:147
  21.7 1.2 %collective-permute-done.7.refs_0_ = bf16[2,2,32,96]{3,2,1,0:T(8,128)(2,1)S(1)} collective-permute-done((bf16[2,2,32,96]{3,2,1,0:T(8,128)(2,1)S(1)}, bf16[2,2,32,96]{3,2,1,0:T(8,128)(2,1)S(1)}, u32[]{:S(2)}, u32[]{:S(2)}) %collective-permute-start.7) | collective-permute-done | bytes 24608 | tf_op jit(solution)/shard_map/ppermute | solution.py:147
  22.9 0.9 %collective-permute-done.8.refs_1_ = bf16[2,2,32,96]{3,2,1,0:T(8,128)(2,1)S(1)} collective-permute-done((bf16[2,2,32,96]{3,2,1,0:T(8,128)(2,1)S(1)}, bf16[2,2,32,96]{3,2,1,0:T(8,128)(2,1)S(1)}, u32[]{:S(2)}, u32[]{:S(2)}) %collective-permute-start.8) | collective-permute-done | bytes 24608 | tf_op jit(solution)/shard_map/ppermute | solution.py:147
  23.8 0.7 %collective-permute-start.9 = (bf16[2,2,32,96]{3,2,1,0:T(8,128)(2,1)S(1)}, bf16[2,2,32,96]{3,2,1,0:T(8,128)(2,1)S(1)}, u32[]{:S(2)}, u32[]{:S(2)}) collective-permute-start(bf16[2,2,32,96]{3,2,1,0:T(8,128)(2,1)S(1)} %settle.1), channel_id=1, source_target_pairs={{0,8},{1,9},{2,10},{3,11},{4,12},{5,13},{6,14},{7,15},{8,0},{9,1},... | collective-permute-start | bytes 73736 | tf_op jit(solution)/shard_map/ppermute | solution.py:147
  24.5 0.9 %collective-permute-done.9.refs_2_ = bf16[2,2,32,96]{3,2,1,0:T(8,128)(2,1)S(1)} collective-permute-done((bf16[2,2,32,96]{3,2,1,0:T(8,128)(2,1)S(1)}, bf16[2,2,32,96]{3,2,1,0:T(8,128)(2,1)S(1)}, u32[]{:S(2)}, u32[]{:S(2)}) %collective-permute-start.9) | collective-permute-done | bytes 24608 | tf_op jit(solution)/shard_map/ppermute | solution.py:147
  25.4 0.6 %assemble.1 = bf16[4,2,32,96]{3,2,1,0:T(8,128)(2,1)} custom-call(bf16[2,2,32,96]{3,2,1,0:T(8,128)(2,1)S(1)} %get-tuple-element.19.first, bf16[2,2,32,96]{3,2,1,0:T(8,128)(2,1)S(1)} %collective-permute-done.7.refs_0_, bf16[2,2,32,96]{3,2,1,0:T(8,128)(2,1)S(1)} %collective-permute-done.8.refs_1_, bf16[2,2,32,96]{3,2,1,0:T(8,128)(2,1)S(1)} %collective-permute-done.9.refs_2_), custom_call_target="tpu_custom_call" | custom-call | tf_op jit(solution)/shard_map/assemble/pallas_call | solution.py:118
  (3 shorter events, 0.0 us)
Async XLA Ops:
  0.0 1.5 %collective-permute-start = (bf16[2,32,384]{2,1,0:T(8,128)(2,1)}, bf16[2,32,384]{2,1,0:T(8,128)(2,1)S(1)}, u32[]{:S(2)}, u32[]{:S(2)}) collective-permute-start(bf16[2,32,384]{2,1,0:T(8,128)(2,1)} %src.2), channel_id=1, source_target_pairs={{0,8},{1,9},{2,10},{3,11},{4,12},{5,13},{6,14},{7,15},{8,0},{9,1},... | collective-permute-start | bytes 147464 | tf_op jit(solution)/shard_map/ppermute | solution.py:147
  0.5 0.8 %copy-start.1 = (bf16[2,32,384]{2,1,0:T(8,128)(2,1)S(1)}, bf16[2,32,384]{2,1,0:T(8,128)(2,1)}, u32[]{:S(2)}) copy-start(bf16[2,32,384]{2,1,0:T(8,128)(2,1)} %src.2) | copy-start | bytes 147460
  1.5 6.0 %copy-start.2 = (s32[2]{0:T(128)S(1)}, s32[2]{0:T(128)}, u32[]{:S(2)}) copy-start(s32[2]{0:T(128)} %occ.1) | copy-start | bytes 28
  1.5 6.0 %copy-start.3 = (s32[2]{0:T(128)S(1)}, s32[2]{0:T(128)}, u32[]{:S(2)}) copy-start(s32[2]{0:T(128)} %live.1) | copy-start | bytes 28
  1.6 7.8 %collective-permute-start.3 = (bf16[2,384,768]{2,1,0:T(8,128)(2,1)}, bf16[2,384,768]{2,1,0:T(8,128)(2,1)S(1)}, u32[]{:S(2)}, u32[]{:S(2)}) collective-permute-start(bf16[2,384,768]{2,1,0:T(8,128)(2,1)} %src.3), channel_id=1, source_target_pairs={{0,8},{1,9},{2,10},{3,11},{4,12},{5,13},{6,14},{7,15},{8,0},{9,1},... | collective-permute-start | bytes 3538952 | tf_op jit(solution)/shard_map/ppermute | solution.py:147
  2.0 6.2 %collective-permute-start.2 = (bf16[2,2,32,384]{3,2,1,0:T(8,128)(2,1)S(1)}, bf16[2,2,32,384]{3,2,1,0:T(8,128)(2,1)S(1)}, u32[]{:S(2)}, u32[]{:S(2)}) collective-permute-start(bf16[2,2,32,384]{3,2,1,0:T(8,128)(2,1)S(1)} %join.1.refs_1_), channel_id=1, source_target_pairs={{0,2},{1,3},{2,0},{3,1},{4,6},{5,7},{6,4},{7,5},{8,14},{9,15},{10,... | collective-permute-start | bytes 294920 | tf_op jit(solution)/shard_map/ppermute | solution.py:147
  4.7 4.6 %collective-permute-start.1 = (bf16[2,2,32,384]{3,2,1,0:T(8,128)(2,1)S(1)}, bf16[2,2,32,384]{3,2,1,0:T(8,128)(2,1)S(1)}, u32[]{:S(2)}, u32[]{:S(2)}) collective-permute-start(bf16[2,2,32,384]{3,2,1,0:T(8,128)(2,1)S(1)} %join.1.refs_1_), channel_id=1, source_target_pairs={{0,16},{1,17},{2,18},{3,19},{4,20},{5,21},{6,22},{7,23},{8,12},{9,... | collective-permute-start | bytes 294920 | tf_op jit(solution)/shard_map/ppermute | solution.py:147
  6.2 1.3 %copy-start = (bf16[2,384,768]{2,1,0:T(8,128)(2,1)S(1)}, bf16[2,384,768]{2,1,0:T(8,128)(2,1)}, u32[]{:S(2)}) copy-start(bf16[2,384,768]{2,1,0:T(8,128)(2,1)} %src.3) | copy-start | bytes 3538948
  10.2 4.7 %collective-permute-start.4 = (f32[192,128]{1,0:T(8,128)S(1)}, f32[192,128]{1,0:T(8,128)S(1)}, u32[]{:S(2)}, u32[]{:S(2)}) collective-permute-start(f32[192,128]{1,0:T(8,128)S(1)} %get-tuple-element.16), channel_id=1, source_target_pairs={{0,1},{1,0},{2,3},{3,2},{4,5},{5,4},{6,7},{7,6},{8,9},{9,8},{10,11... | collective-permute-start | bytes 294920 | tf_op jit(solution)/shard_map/ppermute | solution.py:147
  11.8 5.6 %collective-permute-start.5 = (f32[192,128]{1,0:T(8,128)S(1)}, f32[192,128]{1,0:T(8,128)S(1)}, u32[]{:S(2)}, u32[]{:S(2)}) collective-permute-start(f32[192,128]{1,0:T(8,128)S(1)} %get-tuple-element.17), channel_id=1, source_target_pairs={{0,17},{1,16},{2,19},{3,18},{4,21},{5,20},{6,23},{7,22},{8,25},{9,... | collective-permute-start | bytes 294920 | tf_op jit(solution)/shard_map/ppermute | solution.py:147
  13.2 5.6 %collective-permute-start.6 = (f32[192,128]{1,0:T(8,128)S(1)}, f32[192,128]{1,0:T(8,128)S(1)}, u32[]{:S(2)}, u32[]{:S(2)}) collective-permute-start(f32[192,128]{1,0:T(8,128)S(1)} %get-tuple-element.18), channel_id=1, source_target_pairs={{0,16},{1,17},{2,18},{3,19},{4,20},{5,21},{6,22},{7,23},{8,24},{9,... | collective-permute-start | bytes 294920 | tf_op jit(solution)/shard_map/ppermute | solution.py:147
  18.9 4.0 %collective-permute-start.7 = (bf16[2,2,32,96]{3,2,1,0:T(8,128)(2,1)S(1)}, bf16[2,2,32,96]{3,2,1,0:T(8,128)(2,1)S(1)}, u32[]{:S(2)}, u32[]{:S(2)}) collective-permute-start(bf16[2,2,32,96]{3,2,1,0:T(8,128)(2,1)S(1)} %get-tuple-element.20), channel_id=1, source_target_pairs={{0,2},{1,3},{2,0},{3,1},{4,6},{5,7},{6,4},{7,5},{8,14},{9,15},{10,... | collective-permute-start | bytes 73736 | tf_op jit(solution)/shard_map/ppermute | solution.py:147
  19.5 4.2 %collective-permute-start.8 = (bf16[2,2,32,96]{3,2,1,0:T(8,128)(2,1)S(1)}, bf16[2,2,32,96]{3,2,1,0:T(8,128)(2,1)S(1)}, u32[]{:S(2)}, u32[]{:S(2)}) collective-permute-start(bf16[2,2,32,96]{3,2,1,0:T(8,128)(2,1)S(1)} %get-tuple-element.19.first), channel_id=1, source_target_pairs={{0,8},{1,9},{2,10},{3,11},{4,12},{5,13},{6,14},{7,15},{8,4},{9,5},... | collective-permute-start | bytes 73736 | tf_op jit(solution)/shard_map/ppermute | solution.py:147
  23.8 1.6 %collective-permute-start.9 = (bf16[2,2,32,96]{3,2,1,0:T(8,128)(2,1)S(1)}, bf16[2,2,32,96]{3,2,1,0:T(8,128)(2,1)S(1)}, u32[]{:S(2)}, u32[]{:S(2)}) collective-permute-start(bf16[2,2,32,96]{3,2,1,0:T(8,128)(2,1)S(1)} %settle.1), channel_id=1, source_target_pairs={{0,8},{1,9},{2,10},{3,11},{4,12},{5,13},{6,14},{7,15},{8,0},{9,1},... | collective-permute-start | bytes 73736 | tf_op jit(solution)/shard_map/ppermute | solution.py:147

commit v5 on v4

--- a/solution.py
+++ b/solution.py
@@ -41,6 +41,7 @@
     core = lax.rem(row, 2)
     _, irreps, mb, kb = mine.shape
     row_of = (row, row ^ 1)
+    totals = []
     for g in range(irreps):
         total = None
         for part in range(2):
@@ -57,8 +58,8 @@
             lhs = jnp.concatenate(lhs, axis=0).astype(BF16)
             term = jnp.dot(lhs, (ints, ints_other)[part][g], preferred_element_type=F32)
             total = term if total is None else total + term
-        wide = half * mb
-        turned[:, g * wide : (g + 1) * wide] = total.T
+        totals.append(total)
+    turned[...] = jnp.concatenate(totals, axis=0).T
     h = outs[0].shape[0] // 2
     for (sx, sd), out in zip(steps, outs):
         for c in range(2):
@@ -168,8 +169,8 @@
     ints_other = send(later, other_core)
     came = [send(both, chunk(q)) for q in range(half)]
 
-    steps = [(sx, sd) for sx in range(chips) for sd in reversed(range(depths))]
-    steps = [(0, 0)] + [step for step in steps if any(step)]
+    steps = [(sx, sd) for sx in range(chips) for sd in range(depths)]
+    steps = steps[:1] + steps[:0:-1]
     lanes = irreps * half * mb
     out = call(
         functools.partial(products, sizes, steps), "products", [], [shape((2 * h, lanes), F32)] * len(steps),

time: 26.2 us -> 25.8 us (0.985)
  starting transfers between devices: 12.2 us -> 11.6 us
  waiting for transfers between devices: 9.45 us -> 9.75 us
    ppermute x10, starting transfers between devices: 12.2 us -> 11.6 us  [send(): return lax.ppermute(value, AXES, pairs(move))]
    ppermute x10, waiting for transfers between devices: 9.45 us -> 9.75 us  [send(): return lax.ppermute(value, AXES, pairs(move))]
where the time goes in v5:
time: 25.8 us; the launch traced here: 25.6 us
  starting transfers between devices  11.6 us (45%)
  waiting for transfers between devices  9.75 us (38%)
  local copies, waits for them, and re-layouts  2.08 us (8%)
  Pallas kernels  2.07 us (8%)
    ppermute x10, starting transfers between devices, send(): return lax.ppermute(value, AXES, pairs(move))  11.6 us
    ppermute x10, waiting for transfers between devices, send(): return lax.ppermute(value, AXES, pairs(move))  9.75 us
    unnamed x8, local copies, waits for them, and re-layouts  2.08 us
    pallas_call x8, Pallas kernels, call(): pl.pallas_call(kernel, name=name, out_shape=outs, in_specs=specs + [VMEM]...  2.07 us
  transfers between devices with their start and end apart: 10, of which 8 were waited for; matrix products, arithmetic and copies ran while one was open for 0% of the time, Pallas kernels for 2%

profile of v5, /device:TPU:0, one launch (start us, length us, event | category | flops | bytes accessed | tf_op | source)
XLA Modules:
  0.0 25.6 jit_solution(13496269792890744830)
XLA Ops:
  0.0 0.5 %collective-permute-start = (bf16[2,32,384]{2,1,0:T(8,128)(2,1)}, bf16[2,32,384]{2,1,0:T(8,128)(2,1)S(1)}, u32[]{:S(2)}, u32[]{:S(2)}) collective-permute-start(bf16[2,32,384]{2,1,0:T(8,128)(2,1)} %src.2), channel_id=1, source_target_pairs={{0,8},{1,9},{2,10},{3,11},{4,12},{5,13},{6,14},{7,15},{8,0},{9,1},... | collective-permute-start | bytes 147464 | tf_op jit(solution)/shard_map/ppermute | solution.py:148
  0.5 0.0 copy-start.1
  0.5 0.8 %copy-done.1 = bf16[2,32,384]{2,1,0:T(8,128)(2,1)S(1)} copy-done((bf16[2,32,384]{2,1,0:T(8,128)(2,1)S(1)}, bf16[2,32,384]{2,1,0:T(8,128)(2,1)}, u32[]{:S(2)}) %copy-start.1) | copy-done | bytes 49176
  1.3 0.3 %collective-permute-done.other = bf16[2,32,384]{2,1,0:T(8,128)(2,1)S(1)} collective-permute-done((bf16[2,32,384]{2,1,0:T(8,128)(2,1)}, bf16[2,32,384]{2,1,0:T(8,128)(2,1)S(1)}, u32[]{:S(2)}, u32[]{:S(2)}) %collective-permute-start) | collective-permute-done | bytes 49184 | tf_op jit(solution)/shard_map/ppermute | solution.py:148
  1.5 0.0 copy-start.2
  1.5 0.0 copy-start.3
  1.6 0.4 %collective-permute-start.3 = (bf16[2,384,768]{2,1,0:T(8,128)(2,1)}, bf16[2,384,768]{2,1,0:T(8,128)(2,1)S(1)}, u32[]{:S(2)}, u32[]{:S(2)}) collective-permute-start(bf16[2,384,768]{2,1,0:T(8,128)(2,1)} %src.3), channel_id=1, source_target_pairs={{0,8},{1,9},{2,10},{3,11},{4,12},{5,13},{6,14},{7,15},{8,0},{9,1},... | collective-permute-start | bytes 3538952 | tf_op jit(solution)/shard_map/ppermute | solution.py:148
  2.0 2.7 %collective-permute-start.2 = (bf16[2,2,32,384]{3,2,1,0:T(8,128)(2,1)S(1)}, bf16[2,2,32,384]{3,2,1,0:T(8,128)(2,1)S(1)}, u32[]{:S(2)}, u32[]{:S(2)}) collective-permute-start(bf16[2,2,32,384]{3,2,1,0:T(8,128)(2,1)S(1)} %join.1.refs_1_), channel_id=1, source_target_pairs={{0,2},{1,3},{2,0},{3,1},{4,6},{5,7},{6,4},{7,5},{8,14},{9,15},{10,... | collective-permute-start | bytes 294920 | tf_op jit(solution)/shard_map/ppermute | solution.py:148
  4.7 1.5 %collective-permute-start.1 = (bf16[2,2,32,384]{3,2,1,0:T(8,128)(2,1)S(1)}, bf16[2,2,32,384]{3,2,1,0:T(8,128)(2,1)S(1)}, u32[]{:S(2)}, u32[]{:S(2)}) collective-permute-start(bf16[2,2,32,384]{3,2,1,0:T(8,128)(2,1)S(1)} %join.1.refs_1_), channel_id=1, source_target_pairs={{0,16},{1,17},{2,18},{3,19},{4,20},{5,21},{6,22},{7,23},{8,12},{9,... | collective-permute-start | bytes 294920 | tf_op jit(solution)/shard_map/ppermute | solution.py:148
  6.2 0.0 copy-start
  6.2 1.3 %copy-done = bf16[2,384,768]{2,1,0:T(8,128)(2,1)S(1)} copy-done((bf16[2,384,768]{2,1,0:T(8,128)(2,1)S(1)}, bf16[2,384,768]{2,1,0:T(8,128)(2,1)}, u32[]{:S(2)}) %copy-start) | copy-done | bytes 1179672
  7.5 0.1 load.1.refs_4_
  7.6 0.0 copy-done.2
  7.6 0.0 copy-done.3
  7.6 0.5 %spread.1.refs_0_ = s32[2,2,8,128]{3,2,1,0:T(8,128)S(1)} custom-call(s32[2]{0:T(128)S(1)} %copy-done.2, s32[2]{0:T(128)S(1)} %copy-done.3), custom_call_target="tpu_custom_call" | custom-call | tf_op jit(solution)/shard_map/spread/pallas_call | solution.py:119
  8.1 0.0 collective-permute-done.2.refs_3_
  8.1 1.2 %collective-permute-done.1.refs_2_ = bf16[2,2,32,384]{3,2,1,0:T(8,128)(2,1)S(1)} collective-permute-done((bf16[2,2,32,384]{3,2,1,0:T(8,128)(2,1)S(1)}, bf16[2,2,32,384]{3,2,1,0:T(8,128)(2,1)S(1)}, u32[]{:S(2)}, u32[]{:S(2)}) %collective-permute-start.1) | collective-permute-done | bytes 98336 | tf_op jit(solution)/shard_map/ppermute | solution.py:148
  9.3 0.0 collective-permute-done.3.refs_5_
  9.3 0.7 %products.1 = (f32[192,128]{1,0:T(8,128)S(1)}, f32[192,128]{1,0:T(8,128)S(1)}, f32[192,128]{1,0:T(8,128)S(1)}, f32[192,128]{1,0:T(8,128)S(1)}) custom-call(s32[2,2,8,128]{3,2,1,0:T(8,128)S(1)} %spread.1.refs_0_, bf16[2,2,32,384]{3,2,1,0:T(8,128)(2,1)S(1)} %join.1.refs_1_, bf16[2,2,32,384]{3,2,1,0:T(8,128)(2,1)S(1)} %collective-permute-done.1.refs_2_, ...), custom_call_target="tpu_custom_call" | custom-call | tf_op jit(solution)/shard_map/products/pallas_call | solution.py:119
  10.0 2.5 %collective-permute-start.4 = (f32[192,128]{1,0:T(8,128)S(1)}, f32[192,128]{1,0:T(8,128)S(1)}, u32[]{:S(2)}, u32[]{:S(2)}) collective-permute-start(f32[192,128]{1,0:T(8,128)S(1)} %get-tuple-element.16), channel_id=1, source_target_pairs={{0,17},{1,16},{2,19},{3,18},{4,21},{5,20},{6,23},{7,22},{8,25},{9,... | collective-permute-start | bytes 294920 | tf_op jit(solution)/shard_map/ppermute | solution.py:148
  12.5 0.5 %collective-permute-start.5 = (f32[192,128]{1,0:T(8,128)S(1)}, f32[192,128]{1,0:T(8,128)S(1)}, u32[]{:S(2)}, u32[]{:S(2)}) collective-permute-start(f32[192,128]{1,0:T(8,128)S(1)} %get-tuple-element.17), channel_id=1, source_target_pairs={{0,16},{1,17},{2,18},{3,19},{4,20},{5,21},{6,22},{7,23},{8,24},{9,... | collective-permute-start | bytes 294920 | tf_op jit(solution)/shard_map/ppermute | solution.py:148
  13.1 0.5 %collective-permute-start.6 = (f32[192,128]{1,0:T(8,128)S(1)}, f32[192,128]{1,0:T(8,128)S(1)}, u32[]{:S(2)}, u32[]{:S(2)}) collective-permute-start(f32[192,128]{1,0:T(8,128)S(1)} %get-tuple-element.18), channel_id=1, source_target_pairs={{0,1},{1,0},{2,3},{3,2},{4,5},{5,4},{6,7},{7,6},{8,9},{9,8},{10,11... | collective-permute-start | bytes 294920 | tf_op jit(solution)/shard_map/ppermute | solution.py:148
  13.6 2.0 %collective-permute-done.4.refs_2_ = f32[192,128]{1,0:T(8,128)S(1)} collective-permute-done((f32[192,128]{1,0:T(8,128)S(1)}, f32[192,128]{1,0:T(8,128)S(1)}, u32[]{:S(2)}, u32[]{:S(2)}) %collective-permute-start.4) | collective-permute-done | bytes 98336 | tf_op jit(solution)/shard_map/ppermute | solution.py:148
  15.6 2.6 %collective-permute-done.5.refs_3_ = f32[192,128]{1,0:T(8,128)S(1)} collective-permute-done((f32[192,128]{1,0:T(8,128)S(1)}, f32[192,128]{1,0:T(8,128)S(1)}, u32[]{:S(2)}, u32[]{:S(2)}) %collective-permute-start.5) | collective-permute-done | bytes 98336 | tf_op jit(solution)/shard_map/ppermute | solution.py:148
  18.2 0.8 %collective-permute-done.6.refs_4_ = f32[192,128]{1,0:T(8,128)S(1)} collective-permute-done((f32[192,128]{1,0:T(8,128)S(1)}, f32[192,128]{1,0:T(8,128)S(1)}, u32[]{:S(2)}, u32[]{:S(2)}) %collective-permute-start.6) | collective-permute-done | bytes 98336 | tf_op jit(solution)/shard_map/ppermute | solution.py:148
  19.0 0.1 finish.1
  19.1 0.1 collective-permute-start.7
  19.2 2.3 %collective-permute-start.8 = (bf16[2,2,32,96]{3,2,1,0:T(8,128)(2,1)S(1)}, bf16[2,2,32,96]{3,2,1,0:T(8,128)(2,1)S(1)}, u32[]{:S(2)}, u32[]{:S(2)}) collective-permute-start(bf16[2,2,32,96]{3,2,1,0:T(8,128)(2,1)S(1)} %get-tuple-element.19.first), channel_id=1, source_target_pairs={{0,8},{1,9},{2,10},{3,11},{4,12},{5,13},{6,14},{7,15},{8,4},{9,5},... | collective-permute-start | bytes 73736 | tf_op jit(solution)/shard_map/ppermute | solution.py:148
  21.5 1.6 %collective-permute-done.7.refs_0_ = bf16[2,2,32,96]{3,2,1,0:T(8,128)(2,1)S(1)} collective-permute-done((bf16[2,2,32,96]{3,2,1,0:T(8,128)(2,1)S(1)}, bf16[2,2,32,96]{3,2,1,0:T(8,128)(2,1)S(1)}, u32[]{:S(2)}, u32[]{:S(2)}) %collective-permute-start.7) | collective-permute-done | bytes 24608 | tf_op jit(solution)/shard_map/ppermute | solution.py:148
  23.1 0.4 %collective-permute-done.8.refs_1_ = bf16[2,2,32,96]{3,2,1,0:T(8,128)(2,1)S(1)} collective-permute-done((bf16[2,2,32,96]{3,2,1,0:T(8,128)(2,1)S(1)}, bf16[2,2,32,96]{3,2,1,0:T(8,128)(2,1)S(1)}, u32[]{:S(2)}, u32[]{:S(2)}) %collective-permute-start.8) | collective-permute-done | bytes 24608 | tf_op jit(solution)/shard_map/ppermute | solution.py:148
  23.5 0.6 %collective-permute-start.9 = (bf16[2,2,32,96]{3,2,1,0:T(8,128)(2,1)S(1)}, bf16[2,2,32,96]{3,2,1,0:T(8,128)(2,1)S(1)}, u32[]{:S(2)}, u32[]{:S(2)}) collective-permute-start(bf16[2,2,32,96]{3,2,1,0:T(8,128)(2,1)S(1)} %settle.1), channel_id=1, source_target_pairs={{0,8},{1,9},{2,10},{3,11},{4,12},{5,13},{6,14},{7,15},{8,0},{9,1},... | collective-permute-start | bytes 73736 | tf_op jit(solution)/shard_map/ppermute | solution.py:148
  24.1 0.9 %collective-permute-done.9.refs_2_ = bf16[2,2,32,96]{3,2,1,0:T(8,128)(2,1)S(1)} collective-permute-done((bf16[2,2,32,96]{3,2,1,0:T(8,128)(2,1)S(1)}, bf16[2,2,32,96]{3,2,1,0:T(8,128)(2,1)S(1)}, u32[]{:S(2)}, u32[]{:S(2)}) %collective-permute-start.9) | collective-permute-done | bytes 24608 | tf_op jit(solution)/shard_map/ppermute | solution.py:148
  24.9 0.6 %assemble.1 = bf16[4,2,32,96]{3,2,1,0:T(8,128)(2,1)} custom-call(bf16[2,2,32,96]{3,2,1,0:T(8,128)(2,1)S(1)} %get-tuple-element.19.first, bf16[2,2,32,96]{3,2,1,0:T(8,128)(2,1)S(1)} %collective-permute-done.7.refs_0_, bf16[2,2,32,96]{3,2,1,0:T(8,128)(2,1)S(1)} %collective-permute-done.8.refs_1_, bf16[2,2,32,96]{3,2,1,0:T(8,128)(2,1)S(1)} %collective-permute-done.9.refs_2_), custom_call_target="tpu_custom_call" | custom-call | tf_op jit(solution)/shard_map/assemble/pallas_call | solution.py:119
  (3 shorter events, 0.0 us)
Async XLA Ops:
  0.0 1.5 %collective-permute-start = (bf16[2,32,384]{2,1,0:T(8,128)(2,1)}, bf16[2,32,384]{2,1,0:T(8,128)(2,1)S(1)}, u32[]{:S(2)}, u32[]{:S(2)}) collective-permute-start(bf16[2,32,384]{2,1,0:T(8,128)(2,1)} %src.2), channel_id=1, source_target_pairs={{0,8},{1,9},{2,10},{3,11},{4,12},{5,13},{6,14},{7,15},{8,0},{9,1},... | collective-permute-start | bytes 147464 | tf_op jit(solution)/shard_map/ppermute | solution.py:148
  0.5 0.8 %copy-start.1 = (bf16[2,32,384]{2,1,0:T(8,128)(2,1)S(1)}, bf16[2,32,384]{2,1,0:T(8,128)(2,1)}, u32[]{:S(2)}) copy-start(bf16[2,32,384]{2,1,0:T(8,128)(2,1)} %src.2) | copy-start | bytes 147460
  1.5 6.0 %copy-start.2 = (s32[2]{0:T(128)S(1)}, s32[2]{0:T(128)}, u32[]{:S(2)}) copy-start(s32[2]{0:T(128)} %occ.1) | copy-start | bytes 28
  1.5 6.0 %copy-start.3 = (s32[2]{0:T(128)S(1)}, s32[2]{0:T(128)}, u32[]{:S(2)}) copy-start(s32[2]{0:T(128)} %live.1) | copy-start | bytes 28
  1.6 7.8 %collective-permute-start.3 = (bf16[2,384,768]{2,1,0:T(8,128)(2,1)}, bf16[2,384,768]{2,1,0:T(8,128)(2,1)S(1)}, u32[]{:S(2)}, u32[]{:S(2)}) collective-permute-start(bf16[2,384,768]{2,1,0:T(8,128)(2,1)} %src.3), channel_id=1, source_target_pairs={{0,8},{1,9},{2,10},{3,11},{4,12},{5,13},{6,14},{7,15},{8,0},{9,1},... | collective-permute-start | bytes 3538952 | tf_op jit(solution)/shard_map/ppermute | solution.py:148
  2.0 6.2 %collective-permute-start.2 = (bf16[2,2,32,384]{3,2,1,0:T(8,128)(2,1)S(1)}, bf16[2,2,32,384]{3,2,1,0:T(8,128)(2,1)S(1)}, u32[]{:S(2)}, u32[]{:S(2)}) collective-permute-start(bf16[2,2,32,384]{3,2,1,0:T(8,128)(2,1)S(1)} %join.1.refs_1_), channel_id=1, source_target_pairs={{0,2},{1,3},{2,0},{3,1},{4,6},{5,7},{6,4},{7,5},{8,14},{9,15},{10,... | collective-permute-start | bytes 294920 | tf_op jit(solution)/shard_map/ppermute | solution.py:148
  4.7 4.6 %collective-permute-start.1 = (bf16[2,2,32,384]{3,2,1,0:T(8,128)(2,1)S(1)}, bf16[2,2,32,384]{3,2,1,0:T(8,128)(2,1)S(1)}, u32[]{:S(2)}, u32[]{:S(2)}) collective-permute-start(bf16[2,2,32,384]{3,2,1,0:T(8,128)(2,1)S(1)} %join.1.refs_1_), channel_id=1, source_target_pairs={{0,16},{1,17},{2,18},{3,19},{4,20},{5,21},{6,22},{7,23},{8,12},{9,... | collective-permute-start | bytes 294920 | tf_op jit(solution)/shard_map/ppermute | solution.py:148
  6.2 1.3 %copy-start = (bf16[2,384,768]{2,1,0:T(8,128)(2,1)S(1)}, bf16[2,384,768]{2,1,0:T(8,128)(2,1)}, u32[]{:S(2)}) copy-start(bf16[2,384,768]{2,1,0:T(8,128)(2,1)} %src.3) | copy-start | bytes 3538948
  10.0 5.6 %collective-permute-start.4 = (f32[192,128]{1,0:T(8,128)S(1)}, f32[192,128]{1,0:T(8,128)S(1)}, u32[]{:S(2)}, u32[]{:S(2)}) collective-permute-start(f32[192,128]{1,0:T(8,128)S(1)} %get-tuple-element.16), channel_id=1, source_target_pairs={{0,17},{1,16},{2,19},{3,18},{4,21},{5,20},{6,23},{7,22},{8,25},{9,... | collective-permute-start | bytes 294920 | tf_op jit(solution)/shard_map/ppermute | solution.py:148
  12.5 5.7 %collective-permute-start.5 = (f32[192,128]{1,0:T(8,128)S(1)}, f32[192,128]{1,0:T(8,128)S(1)}, u32[]{:S(2)}, u32[]{:S(2)}) collective-permute-start(f32[192,128]{1,0:T(8,128)S(1)} %get-tuple-element.17), channel_id=1, source_target_pairs={{0,16},{1,17},{2,18},{3,19},{4,20},{5,21},{6,22},{7,23},{8,24},{9,... | collective-permute-start | bytes 294920 | tf_op jit(solution)/shard_map/ppermute | solution.py:148
  13.1 6.0 %collective-permute-start.6 = (f32[192,128]{1,0:T(8,128)S(1)}, f32[192,128]{1,0:T(8,128)S(1)}, u32[]{:S(2)}, u32[]{:S(2)}) collective-permute-start(f32[192,128]{1,0:T(8,128)S(1)} %get-tuple-element.18), channel_id=1, source_target_pairs={{0,1},{1,0},{2,3},{3,2},{4,5},{5,4},{6,7},{7,6},{8,9},{9,8},{10,11... | collective-permute-start | bytes 294920 | tf_op jit(solution)/shard_map/ppermute | solution.py:148
  19.1 4.0 %collective-permute-start.7 = (bf16[2,2,32,96]{3,2,1,0:T(8,128)(2,1)S(1)}, bf16[2,2,32,96]{3,2,1,0:T(8,128)(2,1)S(1)}, u32[]{:S(2)}, u32[]{:S(2)}) collective-permute-start(bf16[2,2,32,96]{3,2,1,0:T(8,128)(2,1)S(1)} %get-tuple-element.20), channel_id=1, source_target_pairs={{0,2},{1,3},{2,0},{3,1},{4,6},{5,7},{6,4},{7,5},{8,14},{9,15},{10,... | collective-permute-start | bytes 73736 | tf_op jit(solution)/shard_map/ppermute | solution.py:148
  19.2 4.3 %collective-permute-start.8 = (bf16[2,2,32,96]{3,2,1,0:T(8,128)(2,1)S(1)}, bf16[2,2,32,96]{3,2,1,0:T(8,128)(2,1)S(1)}, u32[]{:S(2)}, u32[]{:S(2)}) collective-permute-start(bf16[2,2,32,96]{3,2,1,0:T(8,128)(2,1)S(1)} %get-tuple-element.19.first), channel_id=1, source_target_pairs={{0,8},{1,9},{2,10},{3,11},{4,12},{5,13},{6,14},{7,15},{8,4},{9,5},... | collective-permute-start | bytes 73736 | tf_op jit(solution)/shard_map/ppermute | solution.py:148
  23.5 1.4 %collective-permute-start.9 = (bf16[2,2,32,96]{3,2,1,0:T(8,128)(2,1)S(1)}, bf16[2,2,32,96]{3,2,1,0:T(8,128)(2,1)S(1)}, u32[]{:S(2)}, u32[]{:S(2)}) collective-permute-start(bf16[2,2,32,96]{3,2,1,0:T(8,128)(2,1)S(1)} %settle.1), channel_id=1, source_target_pairs={{0,8},{1,9},{2,10},{3,11},{4,12},{5,13},{6,14},{7,15},{8,0},{9,1},... | collective-permute-start | bytes 73736 | tf_op jit(solution)/shard_map/ppermute | solution.py:148

commit v6 on v5

--- a/solution.py
+++ b/solution.py
@@ -11,13 +11,20 @@
 BF16 = jnp.bfloat16
 AXES = ("row", "col", "depth")
 VMEM = pl.BlockSpec(memory_space=pltpu.VMEM)
-SMEM = pl.BlockSpec(memory_space=pltpu.SMEM)
-
-
-def spread(occ, live, limits):
-    for g in range(limits.shape[1]):
-        limits[0, g] = jnp.full(limits.shape[2:], occ[g], jnp.int32)
-        limits[1, g] = jnp.full(limits.shape[2:], live[g], jnp.int32)
+HBM = pl.BlockSpec(memory_space=pltpu.HBM)
+
+
+def load(occ, live, ints, held, limits, counts, sem):
+    irreps = ints.shape[0]
+    copies = [(occ, counts.at[0]), (live, counts.at[1])] + [(ints.at[g], held.at[g]) for g in range(irreps)]
+    copies = [pltpu.make_async_copy(src, dst, sem.at[i]) for i, (src, dst) in enumerate(copies)]
+    for one in reversed(copies):
+        one.start()
+    for one in copies:
+        one.wait()
+    for kind in range(2):
+        for g in range(irreps):
+            limits[kind, g] = jnp.full(limits.shape[2:], counts[kind, g], jnp.int32)
 
 
 def copy(src, dst):
@@ -159,9 +166,11 @@
         return move
 
     amps_other = send(amplitudes, other_core)
-    ints = call(copy, "load", [], shape(integrals.shape, BF16), integrals)
-    limits = call(
-        spread, "spread", [SMEM, SMEM], shape((2, irreps, 8, 128), jnp.int32), occ_count, virtual_pair_count
+    held = (occ_count, virtual_pair_count, integrals)
+    held = [pltpu.with_memory_space_constraint(x, pltpu.HBM) for x in held]
+    ints, limits = call(
+        load, "load", [HBM] * 3, [shape(integrals.shape, BF16), shape((2, irreps, 8, 128), jnp.int32)], *held,
+        scratch=[pltpu.SMEM((2, irreps), jnp.int32), pltpu.SemaphoreType.DMA((2 + irreps,))],
     )
     mine = call(copy, "fetch", [], shape(amplitudes.shape, BF16), amplitudes)
     both = call(join, "join", [], shape((2, irreps, mb, kb), BF16), mine, amps_other)

time: 25.8 us -> 25.8 us (level)
  local copies, waits for them, and re-layouts: 2.08 us -> 0.8 us
  Pallas kernels: 2.07 us -> 2.73 us
  waiting for transfers between devices: 9.75 us -> 10.4 us
    unnamed x8 -> x2, local copies, waits for them, and re-layouts: 2.08 us -> 0.8 us
    pallas_call x8 -> x7, Pallas kernels: 2.07 us -> 2.73 us  [call(): pl.pallas_call(kernel, name=name, out_shape=outs, in_specs=specs + [VMEM]...]
    ppermute x10, waiting for transfers between devices: 9.75 us -> 10.4 us  [send(): return lax.ppermute(value, AXES, pairs(move))]
  transfers between devices with their start and end apart: 10 -> 10, of which waited for: 8 -> 8; matrix products, arithmetic and copies ran while one was open for 0% -> 0% of each run, Pallas kernels for 2% -> 5%
where the time goes in v6:
time: 25.8 us; the launch traced here: 25.6 us
  starting transfers between devices  11.6 us (45%)
  waiting for transfers between devices  10.4 us (40%)
  Pallas kernels  2.73 us (11%)
  local copies, waits for them, and re-layouts  0.8 us (3%)
    ppermute x10, starting transfers between devices, send(): return lax.ppermute(value, AXES, pairs(move))  11.6 us
    ppermute x10, waiting for transfers between devices, send(): return lax.ppermute(value, AXES, pairs(move))  10.4 us
    pallas_call x7, Pallas kernels, call(): pl.pallas_call(kernel, name=name, out_shape=outs, in_specs=specs + [VMEM]...  2.73 us
    unnamed x2, local copies, waits for them, and re-layouts  0.8 us
  transfers between devices with their start and end apart: 10, of which 8 were waited for; matrix products, arithmetic and copies ran while one was open for 0% of the time, Pallas kernels for 5%

profile of v6, /device:TPU:0, one launch (start us, length us, event | category | flops | bytes accessed | tf_op | source)
XLA Modules:
  0.0 25.6 jit_solution(12816575805993672401)
XLA Ops:
  0.0 0.5 %collective-permute-start = (bf16[2,32,384]{2,1,0:T(8,128)(2,1)}, bf16[2,32,384]{2,1,0:T(8,128)(2,1)S(1)}, u32[]{:S(2)}, u32[]{:S(2)}) collective-permute-start(bf16[2,32,384]{2,1,0:T(8,128)(2,1)} %src.1), channel_id=1, source_target_pairs={{0,8},{1,9},{2,10},{3,11},{4,12},{5,13},{6,14},{7,15},{8,0},{9,1},... | collective-permute-start | bytes 147464 | tf_op jit(solution)/shard_map/ppermute | solution.py:155
  0.5 0.0 copy-start
  0.5 0.8 %copy-done = bf16[2,32,384]{2,1,0:T(8,128)(2,1)S(1)} copy-done((bf16[2,32,384]{2,1,0:T(8,128)(2,1)S(1)}, bf16[2,32,384]{2,1,0:T(8,128)(2,1)}, u32[]{:S(2)}) %copy-start) | copy-done | bytes 49176
  1.3 0.3 %collective-permute-done.other = bf16[2,32,384]{2,1,0:T(8,128)(2,1)S(1)} collective-permute-done((bf16[2,32,384]{2,1,0:T(8,128)(2,1)}, bf16[2,32,384]{2,1,0:T(8,128)(2,1)S(1)}, u32[]{:S(2)}, u32[]{:S(2)}) %collective-permute-start) | collective-permute-done | bytes 49184 | tf_op jit(solution)/shard_map/ppermute | solution.py:155
  1.6 0.4 %collective-permute-start.3 = (bf16[2,384,768]{2,1,0:T(8,128)(2,1)}, bf16[2,384,768]{2,1,0:T(8,128)(2,1)S(1)}, u32[]{:S(2)}, u32[]{:S(2)}) collective-permute-start(bf16[2,384,768]{2,1,0:T(8,128)(2,1)} %ints.1), channel_id=1, source_target_pairs={{0,8},{1,9},{2,10},{3,11},{4,12},{5,13},{6,14},{7,15},{8,0},{9,1},... | collective-permute-start | bytes 3538952 | tf_op jit(solution)/shard_map/ppermute | solution.py:155
  2.0 2.7 %collective-permute-start.2 = (bf16[2,2,32,384]{3,2,1,0:T(8,128)(2,1)S(1)}, bf16[2,2,32,384]{3,2,1,0:T(8,128)(2,1)S(1)}, u32[]{:S(2)}, u32[]{:S(2)}) collective-permute-start(bf16[2,2,32,384]{3,2,1,0:T(8,128)(2,1)S(1)} %join.1.refs_1_), channel_id=1, source_target_pairs={{0,2},{1,3},{2,0},{3,1},{4,6},{5,7},{6,4},{7,5},{8,14},{9,15},{10,... | collective-permute-start | bytes 294920 | tf_op jit(solution)/shard_map/ppermute | solution.py:155
  4.7 1.5 %collective-permute-start.1 = (bf16[2,2,32,384]{3,2,1,0:T(8,128)(2,1)S(1)}, bf16[2,2,32,384]{3,2,1,0:T(8,128)(2,1)S(1)}, u32[]{:S(2)}, u32[]{:S(2)}) collective-permute-start(bf16[2,2,32,384]{3,2,1,0:T(8,128)(2,1)S(1)} %join.1.refs_1_), channel_id=1, source_target_pairs={{0,16},{1,17},{2,18},{3,19},{4,20},{5,21},{6,22},{7,23},{8,12},{9,... | collective-permute-start | bytes 294920 | tf_op jit(solution)/shard_map/ppermute | solution.py:155
  6.2 1.3 %load.1 = (bf16[2,384,768]{2,1,0:T(8,128)(2,1)S(1)}, s32[2,2,8,128]{3,2,1,0:T(8,128)S(1)}) custom-call(s32[2]{0:T(128)} %occ.1, s32[2]{0:T(128)} %live.1, bf16[2,384,768]{2,1,0:T(8,128)(2,1)} %ints.1), custom_call_target="tpu_custom_call" | custom-call | tf_op jit(solution)/shard_map/load/pallas_call | solution.py:126
  7.5 0.0 collective-permute-done.2.refs_3_
  7.5 1.8 %collective-permute-done.1.refs_2_ = bf16[2,2,32,384]{3,2,1,0:T(8,128)(2,1)S(1)} collective-permute-done((bf16[2,2,32,384]{3,2,1,0:T(8,128)(2,1)S(1)}, bf16[2,2,32,384]{3,2,1,0:T(8,128)(2,1)S(1)}, u32[]{:S(2)}, u32[]{:S(2)}) %collective-permute-start.1) | collective-permute-done | bytes 98336 | tf_op jit(solution)/shard_map/ppermute | solution.py:155
  9.3 0.0 collective-permute-done.3.refs_5_
  9.3 0.7 %products.1 = (f32[192,128]{1,0:T(8,128)S(1)}, f32[192,128]{1,0:T(8,128)S(1)}, f32[192,128]{1,0:T(8,128)S(1)}, f32[192,128]{1,0:T(8,128)S(1)}) custom-call(s32[2,2,8,128]{3,2,1,0:T(8,128)S(1)} %get-tuple-element.15.refs_0_, bf16[2,2,32,384]{3,2,1,0:T(8,128)(2,1)S(1)} %join.1.refs_1_, bf16[2,2,32,384]{3,2,1,0:T(8,128)(2,1)S(1)} %collective-permute-done.1.refs_2_, ...), custom_call_target="tpu_custom_call" | custom-call | tf_op jit(solution)/shard_map/products/pallas_call | solution.py:126
  10.0 2.5 %collective-permute-start.4 = (f32[192,128]{1,0:T(8,128)S(1)}, f32[192,128]{1,0:T(8,128)S(1)}, u32[]{:S(2)}, u32[]{:S(2)}) collective-permute-start(f32[192,128]{1,0:T(8,128)S(1)} %get-tuple-element.20), channel_id=1, source_target_pairs={{0,17},{1,16},{2,19},{3,18},{4,21},{5,20},{6,23},{7,22},{8,25},{9,... | collective-permute-start | bytes 294920 | tf_op jit(solution)/shard_map/ppermute | solution.py:155
  12.5 0.5 %collective-permute-start.5 = (f32[192,128]{1,0:T(8,128)S(1)}, f32[192,128]{1,0:T(8,128)S(1)}, u32[]{:S(2)}, u32[]{:S(2)}) collective-permute-start(f32[192,128]{1,0:T(8,128)S(1)} %get-tuple-element.21), channel_id=1, source_target_pairs={{0,16},{1,17},{2,18},{3,19},{4,20},{5,21},{6,22},{7,23},{8,24},{9,... | collective-permute-start | bytes 294920 | tf_op jit(solution)/shard_map/ppermute | solution.py:155
  13.1 0.5 %collective-permute-start.6 = (f32[192,128]{1,0:T(8,128)S(1)}, f32[192,128]{1,0:T(8,128)S(1)}, u32[]{:S(2)}, u32[]{:S(2)}) collective-permute-start(f32[192,128]{1,0:T(8,128)S(1)} %get-tuple-element.22), channel_id=1, source_target_pairs={{0,1},{1,0},{2,3},{3,2},{4,5},{5,4},{6,7},{7,6},{8,9},{9,8},{10,11... | collective-permute-start | bytes 294920 | tf_op jit(solution)/shard_map/ppermute | solution.py:155
  13.6 2.0 %collective-permute-done.4.refs_2_ = f32[192,128]{1,0:T(8,128)S(1)} collective-permute-done((f32[192,128]{1,0:T(8,128)S(1)}, f32[192,128]{1,0:T(8,128)S(1)}, u32[]{:S(2)}, u32[]{:S(2)}) %collective-permute-start.4) | collective-permute-done | bytes 98336 | tf_op jit(solution)/shard_map/ppermute | solution.py:155
  15.6 2.6 %collective-permute-done.5.refs_3_ = f32[192,128]{1,0:T(8,128)S(1)} collective-permute-done((f32[192,128]{1,0:T(8,128)S(1)}, f32[192,128]{1,0:T(8,128)S(1)}, u32[]{:S(2)}, u32[]{:S(2)}) %collective-permute-start.5) | collective-permute-done | bytes 98336 | tf_op jit(solution)/shard_map/ppermute | solution.py:155
  18.2 0.8 %collective-permute-done.6.refs_4_ = f32[192,128]{1,0:T(8,128)S(1)} collective-permute-done((f32[192,128]{1,0:T(8,128)S(1)}, f32[192,128]{1,0:T(8,128)S(1)}, u32[]{:S(2)}, u32[]{:S(2)}) %collective-permute-start.6) | collective-permute-done | bytes 98336 | tf_op jit(solution)/shard_map/ppermute | solution.py:155
  19.0 0.1 finish.1
  19.1 0.1 collective-permute-start.7
  19.2 2.3 %collective-permute-start.8 = (bf16[2,2,32,96]{3,2,1,0:T(8,128)(2,1)S(1)}, bf16[2,2,32,96]{3,2,1,0:T(8,128)(2,1)S(1)}, u32[]{:S(2)}, u32[]{:S(2)}) collective-permute-start(bf16[2,2,32,96]{3,2,1,0:T(8,128)(2,1)S(1)} %get-tuple-element.23.first), channel_id=1, source_target_pairs={{0,8},{1,9},{2,10},{3,11},{4,12},{5,13},{6,14},{7,15},{8,4},{9,5},... | collective-permute-start | bytes 73736 | tf_op jit(solution)/shard_map/ppermute | solution.py:155
  21.5 1.6 %collective-permute-done.7.refs_0_ = bf16[2,2,32,96]{3,2,1,0:T(8,128)(2,1)S(1)} collective-permute-done((bf16[2,2,32,96]{3,2,1,0:T(8,128)(2,1)S(1)}, bf16[2,2,32,96]{3,2,1,0:T(8,128)(2,1)S(1)}, u32[]{:S(2)}, u32[]{:S(2)}) %collective-permute-start.7) | collective-permute-done | bytes 24608 | tf_op jit(solution)/shard_map/ppermute | solution.py:155
  23.1 0.4 %collective-permute-done.8.refs_1_ = bf16[2,2,32,96]{3,2,1,0:T(8,128)(2,1)S(1)} collective-permute-done((bf16[2,2,32,96]{3,2,1,0:T(8,128)(2,1)S(1)}, bf16[2,2,32,96]{3,2,1,0:T(8,128)(2,1)S(1)}, u32[]{:S(2)}, u32[]{:S(2)}) %collective-permute-start.8) | collective-permute-done | bytes 24608 | tf_op jit(solution)/shard_map/ppermute | solution.py:155
  23.5 0.6 %collective-permute-start.9 = (bf16[2,2,32,96]{3,2,1,0:T(8,128)(2,1)S(1)}, bf16[2,2,32,96]{3,2,1,0:T(8,128)(2,1)S(1)}, u32[]{:S(2)}, u32[]{:S(2)}) collective-permute-start(bf16[2,2,32,96]{3,2,1,0:T(8,128)(2,1)S(1)} %settle.1), channel_id=1, source_target_pairs={{0,8},{1,9},{2,10},{3,11},{4,12},{5,13},{6,14},{7,15},{8,0},{9,1},... | collective-permute-start | bytes 73736 | tf_op jit(solution)/shard_map/ppermute | solution.py:155
  24.1 0.9 %collective-permute-done.9.refs_2_ = bf16[2,2,32,96]{3,2,1,0:T(8,128)(2,1)S(1)} collective-permute-done((bf16[2,2,32,96]{3,2,1,0:T(8,128)(2,1)S(1)}, bf16[2,2,32,96]{3,2,1,0:T(8,128)(2,1)S(1)}, u32[]{:S(2)}, u32[]{:S(2)}) %collective-permute-start.9) | collective-permute-done | bytes 24608 | tf_op jit(solution)/shard_map/ppermute | solution.py:155
  24.9 0.6 %assemble.1 = bf16[4,2,32,96]{3,2,1,0:T(8,128)(2,1)} custom-call(bf16[2,2,32,96]{3,2,1,0:T(8,128)(2,1)S(1)} %get-tuple-element.23.first, bf16[2,2,32,96]{3,2,1,0:T(8,128)(2,1)S(1)} %collective-permute-done.7.refs_0_, bf16[2,2,32,96]{3,2,1,0:T(8,128)(2,1)S(1)} %collective-permute-done.8.refs_1_, bf16[2,2,32,96]{3,2,1,0:T(8,128)(2,1)S(1)} %collective-permute-done.9.refs_2_), custom_call_target="tpu_custom_call" | custom-call | tf_op jit(solution)/shard_map/assemble/pallas_call | solution.py:126
  (3 shorter events, 0.0 us)
Async XLA Ops:
  0.0 1.5 %collective-permute-start = (bf16[2,32,384]{2,1,0:T(8,128)(2,1)}, bf16[2,32,384]{2,1,0:T(8,128)(2,1)S(1)}, u32[]{:S(2)}, u32[]{:S(2)}) collective-permute-start(bf16[2,32,384]{2,1,0:T(8,128)(2,1)} %src.1), channel_id=1, source_target_pairs={{0,8},{1,9},{2,10},{3,11},{4,12},{5,13},{6,14},{7,15},{8,0},{9,1},... | collective-permute-start | bytes 147464 | tf_op jit(solution)/shard_map/ppermute | solution.py:155
  0.5 0.8 %copy-start = (bf16[2,32,384]{2,1,0:T(8,128)(2,1)S(1)}, bf16[2,32,384]{2,1,0:T(8,128)(2,1)}, u32[]{:S(2)}) copy-start(bf16[2,32,384]{2,1,0:T(8,128)(2,1)} %src.1) | copy-start | bytes 147460
  1.6 7.8 %collective-permute-start.3 = (bf16[2,384,768]{2,1,0:T(8,128)(2,1)}, bf16[2,384,768]{2,1,0:T(8,128)(2,1)S(1)}, u32[]{:S(2)}, u32[]{:S(2)}) collective-permute-start(bf16[2,384,768]{2,1,0:T(8,128)(2,1)} %ints.1), channel_id=1, source_target_pairs={{0,8},{1,9},{2,10},{3,11},{4,12},{5,13},{6,14},{7,15},{8,0},{9,1},... | collective-permute-start | bytes 3538952 | tf_op jit(solution)/shard_map/ppermute | solution.py:155
  2.0 5.5 %collective-permute-start.2 = (bf16[2,2,32,384]{3,2,1,0:T(8,128)(2,1)S(1)}, bf16[2,2,32,384]{3,2,1,0:T(8,128)(2,1)S(1)}, u32[]{:S(2)}, u32[]{:S(2)}) collective-permute-start(bf16[2,2,32,384]{3,2,1,0:T(8,128)(2,1)S(1)} %join.1.refs_1_), channel_id=1, source_target_pairs={{0,2},{1,3},{2,0},{3,1},{4,6},{5,7},{6,4},{7,5},{8,14},{9,15},{10,... | collective-permute-start | bytes 294920 | tf_op jit(solution)/shard_map/ppermute | solution.py:155
  4.7 4.6 %collective-permute-start.1 = (bf16[2,2,32,384]{3,2,1,0:T(8,128)(2,1)S(1)}, bf16[2,2,32,384]{3,2,1,0:T(8,128)(2,1)S(1)}, u32[]{:S(2)}, u32[]{:S(2)}) collective-permute-start(bf16[2,2,32,384]{3,2,1,0:T(8,128)(2,1)S(1)} %join.1.refs_1_), channel_id=1, source_target_pairs={{0,16},{1,17},{2,18},{3,19},{4,20},{5,21},{6,22},{7,23},{8,12},{9,... | collective-permute-start | bytes 294920 | tf_op jit(solution)/shard_map/ppermute | solution.py:155
  10.0 5.6 %collective-permute-start.4 = (f32[192,128]{1,0:T(8,128)S(1)}, f32[192,128]{1,0:T(8,128)S(1)}, u32[]{:S(2)}, u32[]{:S(2)}) collective-permute-start(f32[192,128]{1,0:T(8,128)S(1)} %get-tuple-element.20), channel_id=1, source_target_pairs={{0,17},{1,16},{2,19},{3,18},{4,21},{5,20},{6,23},{7,22},{8,25},{9,... | collective-permute-start | bytes 294920 | tf_op jit(solution)/shard_map/ppermute | solution.py:155
  12.5 5.7 %collective-permute-start.5 = (f32[192,128]{1,0:T(8,128)S(1)}, f32[192,128]{1,0:T(8,128)S(1)}, u32[]{:S(2)}, u32[]{:S(2)}) collective-permute-start(f32[192,128]{1,0:T(8,128)S(1)} %get-tuple-element.21), channel_id=1, source_target_pairs={{0,16},{1,17},{2,18},{3,19},{4,20},{5,21},{6,22},{7,23},{8,24},{9,... | collective-permute-start | bytes 294920 | tf_op jit(solution)/shard_map/ppermute | solution.py:155
  13.1 5.9 %collective-permute-start.6 = (f32[192,128]{1,0:T(8,128)S(1)}, f32[192,128]{1,0:T(8,128)S(1)}, u32[]{:S(2)}, u32[]{:S(2)}) collective-permute-start(f32[192,128]{1,0:T(8,128)S(1)} %get-tuple-element.22), channel_id=1, source_target_pairs={{0,1},{1,0},{2,3},{3,2},{4,5},{5,4},{6,7},{7,6},{8,9},{9,8},{10,11... | collective-permute-start | bytes 294920 | tf_op jit(solution)/shard_map/ppermute | solution.py:155
  19.1 4.0 %collective-permute-start.7 = (bf16[2,2,32,96]{3,2,1,0:T(8,128)(2,1)S(1)}, bf16[2,2,32,96]{3,2,1,0:T(8,128)(2,1)S(1)}, u32[]{:S(2)}, u32[]{:S(2)}) collective-permute-start(bf16[2,2,32,96]{3,2,1,0:T(8,128)(2,1)S(1)} %get-tuple-element.24), channel_id=1, source_target_pairs={{0,2},{1,3},{2,0},{3,1},{4,6},{5,7},{6,4},{7,5},{8,14},{9,15},{10,... | collective-permute-start | bytes 73736 | tf_op jit(solution)/shard_map/ppermute | solution.py:155
  19.2 4.3 %collective-permute-start.8 = (bf16[2,2,32,96]{3,2,1,0:T(8,128)(2,1)S(1)}, bf16[2,2,32,96]{3,2,1,0:T(8,128)(2,1)S(1)}, u32[]{:S(2)}, u32[]{:S(2)}) collective-permute-start(bf16[2,2,32,96]{3,2,1,0:T(8,128)(2,1)S(1)} %get-tuple-element.23.first), channel_id=1, source_target_pairs={{0,8},{1,9},{2,10},{3,11},{4,12},{5,13},{6,14},{7,15},{8,4},{9,5},... | collective-permute-start | bytes 73736 | tf_op jit(solution)/shard_map/ppermute | solution.py:155
  23.5 1.4 %collective-permute-start.9 = (bf16[2,2,32,96]{3,2,1,0:T(8,128)(2,1)S(1)}, bf16[2,2,32,96]{3,2,1,0:T(8,128)(2,1)S(1)}, u32[]{:S(2)}, u32[]{:S(2)}) collective-permute-start(bf16[2,2,32,96]{3,2,1,0:T(8,128)(2,1)S(1)} %settle.1), channel_id=1, source_target_pairs={{0,8},{1,9},{2,10},{3,11},{4,12},{5,13},{6,14},{7,15},{8,0},{9,1},... | collective-permute-start | bytes 73736 | tf_op jit(solution)/shard_map/ppermute | solution.py:155

commit v7 on v6

--- a/solution.py
+++ b/solution.py
@@ -106,29 +106,44 @@
         give[q] = back[q][1 - core]
 
 
-def assemble(half, first, *refs):
-    back, came, out = refs[:half][::-1], refs[-2], refs[-1]
+def pick(core, zero, one):
+    return jnp.where(core == 0, zero.astype(F32), one.astype(F32)).astype(BF16)
+
+
+def copy_all(sem, pairs):
+    copies = [pltpu.make_async_copy(src, dst, sem.at[i]) for i, (src, dst) in enumerate(pairs)]
+    for one in copies:
+        one.start()
+    for one in copies:
+        one.wait()
+
+
+def place(half, first, *refs):
+    back, out, picked, sem = refs[:half][::-1], refs[-3], refs[-2], refs[-1]
     core = lax.rem(lax.axis_index("row"), 2)
     col = lax.axis_index("col")
-
-    def pick(zero, one):
-        return jnp.where(core == 0, zero.astype(F32), one.astype(F32)).astype(BF16)
-
-    out[col] = pick(first[0], back[0][1])
-    out[col ^ half] = pick(back[0][0], came[0])
-    for q in range(1, half):
-        out[col ^ (q + core * half)] = back[q][core]
-        out[col ^ (q + (1 - core) * half)] = came[q]
-
-
-def call(kernel, name, specs, outs, *args, scratch=()):
+    picked[...] = pick(core, first[0], back[0][1])
+    pairs = [(back[q].at[core], out.at[col ^ (q + core * half)]) for q in range(1, half)]
+    copy_all(sem, pairs + [(picked, out.at[col])])
+
+
+def complete(half, far, came, placed, out, picked, sem):
+    core = lax.rem(lax.axis_index("row"), 2)
+    col = lax.axis_index("col")
+    picked[...] = pick(core, far[0], came[0])
+    pairs = [(came.at[q], out.at[col ^ (q + (1 - core) * half)]) for q in range(1, half)]
+    copy_all(sem, pairs + [(picked, out.at[col ^ half])])
+
+
+def call(kernel, name, specs, outs, *args, scratch=(), to=VMEM, last=(), aliases=None):
     many = isinstance(outs, list)
     return pl.pallas_call(
         kernel,
         name=name,
         out_shape=outs,
-        in_specs=specs + [VMEM] * (len(args) - len(specs)),
-        out_specs=[VMEM] * len(outs) if many else VMEM,
+        in_specs=specs + [VMEM] * (len(args) - len(specs) - len(last)) + list(last),
+        out_specs=[to] * len(outs) if many else to,
+        input_output_aliases=aliases or {},
         scratch_shapes=list(scratch),
         compiler_params=pltpu.CompilerParams(vmem_limit_bytes=40 * 2**20),
     )(*args)
@@ -198,9 +213,12 @@
 
     back = [send(done[q], chunk(q) if q else home) for q in range(half)]
     give = call(functools.partial(settle, half), "settle", [], shape((half, irreps, mb, h), BF16), *back[::-1])
+    whole = shape((cols, irreps, mb, h), BF16)
+    scratch = [pltpu.VMEM((irreps, mb, h), BF16), pltpu.SemaphoreType.DMA((half,))]
+    placed = call(functools.partial(place, half), "place", [], whole, done[0], *back[::-1], scratch=scratch, to=HBM)
     result = call(
-        functools.partial(assemble, half), "assemble", [], shape((cols, irreps, mb, h), BF16),
-        done[0], *back[::-1], send(give, other_core),
+        functools.partial(complete, half), "complete", [], whole, back[0], send(give, other_core), placed,
+        scratch=scratch, to=HBM, last=[HBM], aliases={2: 0},
     )
     return result.transpose(0, 3, 1, 2)
 

time: 25.8 us -> 25.8 us (level)
  waiting for transfers between devices: 10.4 us -> 9.75 us
  Pallas kernels: 2.73 us -> 3.34 us
    ppermute x10, waiting for transfers between devices: 10.4 us -> 9.75 us  [send(): return lax.ppermute(value, AXES, pairs(move))]
    pallas_call x7 -> x8, Pallas kernels: 2.73 us -> 3.34 us  [call(): pl.pallas_call(kernel, name=name, out_shape=outs, in_specs=specs + [VMEM]...]
  transfers between devices with their start and end apart: 10 -> 10, of which waited for: 8 -> 8; matrix products, arithmetic and copies ran while one was open for 0% -> 0% of each run, Pallas kernels for 5% -> 7%
where the time goes in v7:
time: 25.8 us; the launch traced here: 25.6 us
  starting transfers between devices  11.6 us (45%)
  waiting for transfers between devices  9.75 us (38%)
  Pallas kernels  3.34 us (13%)
  local copies, waits for them, and re-layouts  0.8 us (3%)
    ppermute x10, starting transfers between devices, send(): return lax.ppermute(value, AXES, pairs(move))  11.6 us
    ppermute x10, waiting for transfers between devices, send(): return lax.ppermute(value, AXES, pairs(move))  9.75 us
    pallas_call x8, Pallas kernels, call(): pl.pallas_call(kernel, name=name, out_shape=outs, in_specs=specs + [VMEM]...  3.34 us
    unnamed x2, local copies, waits for them, and re-layouts  0.8 us
  transfers between devices with their start and end apart: 10, of which 8 were waited for; matrix products, arithmetic and copies ran while one was open for 0% of the time, Pallas kernels for 7%

profile of v7, /device:TPU:0, one launch (start us, length us, event | category | flops | bytes accessed | tf_op | source)
XLA Modules:
  0.0 25.6 jit_solution(10398417004839999001)
XLA Ops:
  0.0 0.5 %collective-permute-start = (bf16[2,32,384]{2,1,0:T(8,128)(2,1)}, bf16[2,32,384]{2,1,0:T(8,128)(2,1)S(1)}, u32[]{:S(2)}, u32[]{:S(2)}) collective-permute-start(bf16[2,32,384]{2,1,0:T(8,128)(2,1)} %src.1), channel_id=1, source_target_pairs={{0,8},{1,9},{2,10},{3,11},{4,12},{5,13},{6,14},{7,15},{8,0},{9,1},... | collective-permute-start | bytes 147464 | tf_op jit(solution)/shard_map/ppermute | solution.py:170
  0.5 0.0 copy-start
  0.5 0.8 %copy-done = bf16[2,32,384]{2,1,0:T(8,128)(2,1)S(1)} copy-done((bf16[2,32,384]{2,1,0:T(8,128)(2,1)S(1)}, bf16[2,32,384]{2,1,0:T(8,128)(2,1)}, u32[]{:S(2)}) %copy-start) | copy-done | bytes 49176
  1.3 0.3 %collective-permute-done.other = bf16[2,32,384]{2,1,0:T(8,128)(2,1)S(1)} collective-permute-done((bf16[2,32,384]{2,1,0:T(8,128)(2,1)}, bf16[2,32,384]{2,1,0:T(8,128)(2,1)S(1)}, u32[]{:S(2)}, u32[]{:S(2)}) %collective-permute-start) | collective-permute-done | bytes 49184 | tf_op jit(solution)/shard_map/ppermute | solution.py:170
  1.6 0.4 %collective-permute-start.3 = (bf16[2,384,768]{2,1,0:T(8,128)(2,1)}, bf16[2,384,768]{2,1,0:T(8,128)(2,1)S(1)}, u32[]{:S(2)}, u32[]{:S(2)}) collective-permute-start(bf16[2,384,768]{2,1,0:T(8,128)(2,1)} %ints.1), channel_id=1, source_target_pairs={{0,8},{1,9},{2,10},{3,11},{4,12},{5,13},{6,14},{7,15},{8,0},{9,1},... | collective-permute-start | bytes 3538952 | tf_op jit(solution)/shard_map/ppermute | solution.py:170
  2.0 2.7 %collective-permute-start.2 = (bf16[2,2,32,384]{3,2,1,0:T(8,128)(2,1)S(1)}, bf16[2,2,32,384]{3,2,1,0:T(8,128)(2,1)S(1)}, u32[]{:S(2)}, u32[]{:S(2)}) collective-permute-start(bf16[2,2,32,384]{3,2,1,0:T(8,128)(2,1)S(1)} %join.1.refs_1_), channel_id=1, source_target_pairs={{0,2},{1,3},{2,0},{3,1},{4,6},{5,7},{6,4},{7,5},{8,14},{9,15},{10,... | collective-permute-start | bytes 294920 | tf_op jit(solution)/shard_map/ppermute | solution.py:170
  4.7 1.5 %collective-permute-start.1 = (bf16[2,2,32,384]{3,2,1,0:T(8,128)(2,1)S(1)}, bf16[2,2,32,384]{3,2,1,0:T(8,128)(2,1)S(1)}, u32[]{:S(2)}, u32[]{:S(2)}) collective-permute-start(bf16[2,2,32,384]{3,2,1,0:T(8,128)(2,1)S(1)} %join.1.refs_1_), channel_id=1, source_target_pairs={{0,16},{1,17},{2,18},{3,19},{4,20},{5,21},{6,22},{7,23},{8,12},{9,... | collective-permute-start | bytes 294920 | tf_op jit(solution)/shard_map/ppermute | solution.py:170
  6.2 1.3 %load.1 = (bf16[2,384,768]{2,1,0:T(8,128)(2,1)S(1)}, s32[2,2,8,128]{3,2,1,0:T(8,128)S(1)}) custom-call(s32[2]{0:T(128)} %occ.1, s32[2]{0:T(128)} %live.1, bf16[2,384,768]{2,1,0:T(8,128)(2,1)} %ints.1), custom_call_target="tpu_custom_call" | custom-call | tf_op jit(solution)/shard_map/load/pallas_call | solution.py:140
  7.5 0.0 collective-permute-done.2.refs_3_
  7.5 1.8 %collective-permute-done.1.refs_2_ = bf16[2,2,32,384]{3,2,1,0:T(8,128)(2,1)S(1)} collective-permute-done((bf16[2,2,32,384]{3,2,1,0:T(8,128)(2,1)S(1)}, bf16[2,2,32,384]{3,2,1,0:T(8,128)(2,1)S(1)}, u32[]{:S(2)}, u32[]{:S(2)}) %collective-permute-start.1) | collective-permute-done | bytes 98336 | tf_op jit(solution)/shard_map/ppermute | solution.py:170
  9.3 0.0 collective-permute-done.3.refs_5_
  9.3 0.7 %products.1 = (f32[192,128]{1,0:T(8,128)S(1)}, f32[192,128]{1,0:T(8,128)S(1)}, f32[192,128]{1,0:T(8,128)S(1)}, f32[192,128]{1,0:T(8,128)S(1)}) custom-call(s32[2,2,8,128]{3,2,1,0:T(8,128)S(1)} %get-tuple-element.15.refs_0_, bf16[2,2,32,384]{3,2,1,0:T(8,128)(2,1)S(1)} %join.1.refs_1_, bf16[2,2,32,384]{3,2,1,0:T(8,128)(2,1)S(1)} %collective-permute-done.1.refs_2_, ...), custom_call_target="tpu_custom_call" | custom-call | tf_op jit(solution)/shard_map/products/pallas_call | solution.py:140
  10.0 2.5 %collective-permute-start.4 = (f32[192,128]{1,0:T(8,128)S(1)}, f32[192,128]{1,0:T(8,128)S(1)}, u32[]{:S(2)}, u32[]{:S(2)}) collective-permute-start(f32[192,128]{1,0:T(8,128)S(1)} %get-tuple-element.20), channel_id=1, source_target_pairs={{0,17},{1,16},{2,19},{3,18},{4,21},{5,20},{6,23},{7,22},{8,25},{9,... | collective-permute-start | bytes 294920 | tf_op jit(solution)/shard_map/ppermute | solution.py:170
  12.5 0.5 %collective-permute-start.5 = (f32[192,128]{1,0:T(8,128)S(1)}, f32[192,128]{1,0:T(8,128)S(1)}, u32[]{:S(2)}, u32[]{:S(2)}) collective-permute-start(f32[192,128]{1,0:T(8,128)S(1)} %get-tuple-element.21), channel_id=1, source_target_pairs={{0,16},{1,17},{2,18},{3,19},{4,20},{5,21},{6,22},{7,23},{8,24},{9,... | collective-permute-start | bytes 294920 | tf_op jit(solution)/shard_map/ppermute | solution.py:170
  13.1 0.5 %collective-permute-start.6 = (f32[192,128]{1,0:T(8,128)S(1)}, f32[192,128]{1,0:T(8,128)S(1)}, u32[]{:S(2)}, u32[]{:S(2)}) collective-permute-start(f32[192,128]{1,0:T(8,128)S(1)} %get-tuple-element.22), channel_id=1, source_target_pairs={{0,1},{1,0},{2,3},{3,2},{4,5},{5,4},{6,7},{7,6},{8,9},{9,8},{10,11... | collective-permute-start | bytes 294920 | tf_op jit(solution)/shard_map/ppermute | solution.py:170
  13.6 2.0 %collective-permute-done.4.refs_2_ = f32[192,128]{1,0:T(8,128)S(1)} collective-permute-done((f32[192,128]{1,0:T(8,128)S(1)}, f32[192,128]{1,0:T(8,128)S(1)}, u32[]{:S(2)}, u32[]{:S(2)}) %collective-permute-start.4) | collective-permute-done | bytes 98336 | tf_op jit(solution)/shard_map/ppermute | solution.py:170
  15.6 2.6 %collective-permute-done.5.refs_3_ = f32[192,128]{1,0:T(8,128)S(1)} collective-permute-done((f32[192,128]{1,0:T(8,128)S(1)}, f32[192,128]{1,0:T(8,128)S(1)}, u32[]{:S(2)}, u32[]{:S(2)}) %collective-permute-start.5) | collective-permute-done | bytes 98336 | tf_op jit(solution)/shard_map/ppermute | solution.py:170
  18.2 0.8 %collective-permute-done.6.refs_4_ = f32[192,128]{1,0:T(8,128)S(1)} collective-permute-done((f32[192,128]{1,0:T(8,128)S(1)}, f32[192,128]{1,0:T(8,128)S(1)}, u32[]{:S(2)}, u32[]{:S(2)}) %collective-permute-start.6) | collective-permute-done | bytes 98336 | tf_op jit(solution)/shard_map/ppermute | solution.py:170
  19.0 0.1 finish.1
  19.1 0.1 collective-permute-start.8
  19.2 2.3 %collective-permute-start.7 = (bf16[2,2,32,96]{3,2,1,0:T(8,128)(2,1)S(1)}, bf16[2,2,32,96]{3,2,1,0:T(8,128)(2,1)S(1)}, u32[]{:S(2)}, u32[]{:S(2)}) collective-permute-start(bf16[2,2,32,96]{3,2,1,0:T(8,128)(2,1)S(1)} %get-tuple-element.23.first), channel_id=1, source_target_pairs={{0,8},{1,9},{2,10},{3,11},{4,12},{5,13},{6,14},{7,15},{8,4},{9,5},... | collective-permute-start | bytes 73736 | tf_op jit(solution)/shard_map/ppermute | solution.py:170
  21.5 1.6 %collective-permute-done.8.refs_0_ = bf16[2,2,32,96]{3,2,1,0:T(8,128)(2,1)S(1)} collective-permute-done((bf16[2,2,32,96]{3,2,1,0:T(8,128)(2,1)S(1)}, bf16[2,2,32,96]{3,2,1,0:T(8,128)(2,1)S(1)}, u32[]{:S(2)}, u32[]{:S(2)}) %collective-permute-start.8) | collective-permute-done | bytes 24608 | tf_op jit(solution)/shard_map/ppermute | solution.py:170
  23.1 0.4 %collective-permute-done.7.refs_1_.far = bf16[2,2,32,96]{3,2,1,0:T(8,128)(2,1)S(1)} collective-permute-done((bf16[2,2,32,96]{3,2,1,0:T(8,128)(2,1)S(1)}, bf16[2,2,32,96]{3,2,1,0:T(8,128)(2,1)S(1)}, u32[]{:S(2)}, u32[]{:S(2)}) %collective-permute-start.7) | collective-permute-done | bytes 24608 | tf_op jit(solution)/shard_map/ppermute | solution.py:170
  23.5 0.6 %collective-permute-start.9 = (bf16[2,2,32,96]{3,2,1,0:T(8,128)(2,1)S(1)}, bf16[2,2,32,96]{3,2,1,0:T(8,128)(2,1)S(1)}, u32[]{:S(2)}, u32[]{:S(2)}) collective-permute-start(bf16[2,2,32,96]{3,2,1,0:T(8,128)(2,1)S(1)} %settle.1), channel_id=1, source_target_pairs={{0,8},{1,9},{2,10},{3,11},{4,12},{5,13},{6,14},{7,15},{8,0},{9,1},... | collective-permute-start | bytes 73736 | tf_op jit(solution)/shard_map/ppermute | solution.py:170
  24.1 0.6 %place.1.placed = bf16[4,2,32,96]{3,2,1,0:T(8,128)(2,1)} custom-call(bf16[2,2,32,96]{3,2,1,0:T(8,128)(2,1)S(1)} %get-tuple-element.23.first, bf16[2,2,32,96]{3,2,1,0:T(8,128)(2,1)S(1)} %collective-permute-done.8.refs_0_, bf16[2,2,32,96]{3,2,1,0:T(8,128)(2,1)S(1)} %collective-permute-done.7.refs_1_.far), custom_call_target="tpu_custom_call" | custom-call | tf_op jit(solution)/shard_map/place/pallas_call | solution.py:140
  24.7 0.2 collective-permute-done.9.came
  24.9 0.6 %complete.1 = bf16[4,2,32,96]{3,2,1,0:T(8,128)(2,1)} custom-call(bf16[2,2,32,96]{3,2,1,0:T(8,128)(2,1)S(1)} %collective-permute-done.7.refs_1_.far, bf16[2,2,32,96]{3,2,1,0:T(8,128)(2,1)S(1)} %collective-permute-done.9.came, bf16[4,2,32,96]{3,2,1,0:T(8,128)(2,1)} %place.1.placed), custom_call_target="tpu_custom_call", output_to_operand_aliasing={{}: (2, {})} | custom-call | tf_op jit(solution)/shard_map/complete/pallas_call | solution.py:140
  (3 shorter events, 0.0 us)
Async XLA Ops:
  0.0 1.5 %collective-permute-start = (bf16[2,32,384]{2,1,0:T(8,128)(2,1)}, bf16[2,32,384]{2,1,0:T(8,128)(2,1)S(1)}, u32[]{:S(2)}, u32[]{:S(2)}) collective-permute-start(bf16[2,32,384]{2,1,0:T(8,128)(2,1)} %src.1), channel_id=1, source_target_pairs={{0,8},{1,9},{2,10},{3,11},{4,12},{5,13},{6,14},{7,15},{8,0},{9,1},... | collective-permute-start | bytes 147464 | tf_op jit(solution)/shard_map/ppermute | solution.py:170
  0.5 0.8 %copy-start = (bf16[2,32,384]{2,1,0:T(8,128)(2,1)S(1)}, bf16[2,32,384]{2,1,0:T(8,128)(2,1)}, u32[]{:S(2)}) copy-start(bf16[2,32,384]{2,1,0:T(8,128)(2,1)} %src.1) | copy-start | bytes 147460
  1.6 7.8 %collective-permute-start.3 = (bf16[2,384,768]{2,1,0:T(8,128)(2,1)}, bf16[2,384,768]{2,1,0:T(8,128)(2,1)S(1)}, u32[]{:S(2)}, u32[]{:S(2)}) collective-permute-start(bf16[2,384,768]{2,1,0:T(8,128)(2,1)} %ints.1), channel_id=1, source_target_pairs={{0,8},{1,9},{2,10},{3,11},{4,12},{5,13},{6,14},{7,15},{8,0},{9,1},... | collective-permute-start | bytes 3538952 | tf_op jit(solution)/shard_map/ppermute | solution.py:170
  2.0 5.5 %collective-permute-start.2 = (bf16[2,2,32,384]{3,2,1,0:T(8,128)(2,1)S(1)}, bf16[2,2,32,384]{3,2,1,0:T(8,128)(2,1)S(1)}, u32[]{:S(2)}, u32[]{:S(2)}) collective-permute-start(bf16[2,2,32,384]{3,2,1,0:T(8,128)(2,1)S(1)} %join.1.refs_1_), channel_id=1, source_target_pairs={{0,2},{1,3},{2,0},{3,1},{4,6},{5,7},{6,4},{7,5},{8,14},{9,15},{10,... | collective-permute-start | bytes 294920 | tf_op jit(solution)/shard_map/ppermute | solution.py:170
  4.7 4.6 %collective-permute-start.1 = (bf16[2,2,32,384]{3,2,1,0:T(8,128)(2,1)S(1)}, bf16[2,2,32,384]{3,2,1,0:T(8,128)(2,1)S(1)}, u32[]{:S(2)}, u32[]{:S(2)}) collective-permute-start(bf16[2,2,32,384]{3,2,1,0:T(8,128)(2,1)S(1)} %join.1.refs_1_), channel_id=1, source_target_pairs={{0,16},{1,17},{2,18},{3,19},{4,20},{5,21},{6,22},{7,23},{8,12},{9,... | collective-permute-start | bytes 294920 | tf_op jit(solution)/shard_map/ppermute | solution.py:170
  10.0 5.6 %collective-permute-start.4 = (f32[192,128]{1,0:T(8,128)S(1)}, f32[192,128]{1,0:T(8,128)S(1)}, u32[]{:S(2)}, u32[]{:S(2)}) collective-permute-start(f32[192,128]{1,0:T(8,128)S(1)} %get-tuple-element.20), channel_id=1, source_target_pairs={{0,17},{1,16},{2,19},{3,18},{4,21},{5,20},{6,23},{7,22},{8,25},{9,... | collective-permute-start | bytes 294920 | tf_op jit(solution)/shard_map/ppermute | solution.py:170
  12.5 5.7 %collective-permute-start.5 = (f32[192,128]{1,0:T(8,128)S(1)}, f32[192,128]{1,0:T(8,128)S(1)}, u32[]{:S(2)}, u32[]{:S(2)}) collective-permute-start(f32[192,128]{1,0:T(8,128)S(1)} %get-tuple-element.21), channel_id=1, source_target_pairs={{0,16},{1,17},{2,18},{3,19},{4,20},{5,21},{6,22},{7,23},{8,24},{9,... | collective-permute-start | bytes 294920 | tf_op jit(solution)/shard_map/ppermute | solution.py:170
  13.1 5.9 %collective-permute-start.6 = (f32[192,128]{1,0:T(8,128)S(1)}, f32[192,128]{1,0:T(8,128)S(1)}, u32[]{:S(2)}, u32[]{:S(2)}) collective-permute-start(f32[192,128]{1,0:T(8,128)S(1)} %get-tuple-element.22), channel_id=1, source_target_pairs={{0,1},{1,0},{2,3},{3,2},{4,5},{5,4},{6,7},{7,6},{8,9},{9,8},{10,11... | collective-permute-start | bytes 294920 | tf_op jit(solution)/shard_map/ppermute | solution.py:170
  19.1 4.0 %collective-permute-start.8 = (bf16[2,2,32,96]{3,2,1,0:T(8,128)(2,1)S(1)}, bf16[2,2,32,96]{3,2,1,0:T(8,128)(2,1)S(1)}, u32[]{:S(2)}, u32[]{:S(2)}) collective-permute-start(bf16[2,2,32,96]{3,2,1,0:T(8,128)(2,1)S(1)} %get-tuple-element.24), channel_id=1, source_target_pairs={{0,2},{1,3},{2,0},{3,1},{4,6},{5,7},{6,4},{7,5},{8,14},{9,15},{10,... | collective-permute-start | bytes 73736 | tf_op jit(solution)/shard_map/ppermute | solution.py:170
  19.2 4.3 %collective-permute-start.7 = (bf16[2,2,32,96]{3,2,1,0:T(8,128)(2,1)S(1)}, bf16[2,2,32,96]{3,2,1,0:T(8,128)(2,1)S(1)}, u32[]{:S(2)}, u32[]{:S(2)}) collective-permute-start(bf16[2,2,32,96]{3,2,1,0:T(8,128)(2,1)S(1)} %get-tuple-element.23.first), channel_id=1, source_target_pairs={{0,8},{1,9},{2,10},{3,11},{4,12},{5,13},{6,14},{7,15},{8,4},{9,5},... | collective-permute-start | bytes 73736 | tf_op jit(solution)/shard_map/ppermute | solution.py:170
  23.5 1.4 %collective-permute-start.9 = (bf16[2,2,32,96]{3,2,1,0:T(8,128)(2,1)S(1)}, bf16[2,2,32,96]{3,2,1,0:T(8,128)(2,1)S(1)}, u32[]{:S(2)}, u32[]{:S(2)}) collective-permute-start(bf16[2,2,32,96]{3,2,1,0:T(8,128)(2,1)S(1)} %settle.1), channel_id=1, source_target_pairs={{0,8},{1,9},{2,10},{3,11},{4,12},{5,13},{6,14},{7,15},{8,0},{9,1},... | collective-permute-start | bytes 73736 | tf_op jit(solution)/shard_map/ppermute | solution.py:170

commit v8 on v6

--- a/solution.py
+++ b/solution.py
@@ -27,8 +27,10 @@
             limits[kind, g] = jnp.full(limits.shape[2:], counts[kind, g], jnp.int32)
 
 
-def copy(src, dst):
-    dst[...] = src[...]
+def fetch(src, dst, sem):
+    one = pltpu.make_async_copy(src, dst, sem)
+    one.start()
+    one.wait()
 
 
 def join(mine, other, both):
@@ -68,7 +70,8 @@
         totals.append(total)
     turned[...] = jnp.concatenate(totals, axis=0).T
     h = outs[0].shape[0] // 2
-    for (sx, sd), out in zip(steps, outs):
+    for (near, far), out in zip(steps, outs):
+        sx, sd = (jnp.where(core == 0, a, b) for a, b in zip(near, far))
         for c in range(2):
             block = ((row // 2 ^ sx) * 2 + c) * depths + (dep ^ sd)
             out[c * h : (c + 1) * h] = turned[pl.ds(pl.multiple_of(block * h, 8), h), :]
@@ -172,14 +175,18 @@
         load, "load", [HBM] * 3, [shape(integrals.shape, BF16), shape((2, irreps, 8, 128), jnp.int32)], *held,
         scratch=[pltpu.SMEM((2, irreps), jnp.int32), pltpu.SemaphoreType.DMA((2 + irreps,))],
     )
-    mine = call(copy, "fetch", [], shape(amplitudes.shape, BF16), amplitudes)
+    mine = call(
+        fetch, "fetch", [HBM], shape(amplitudes.shape, BF16), pltpu.with_memory_space_constraint(amplitudes, pltpu.HBM),
+        scratch=[pltpu.SemaphoreType.DMA],
+    )
     both = call(join, "join", [], shape((2, irreps, mb, kb), BF16), mine, amps_other)
     later, both = lax.optimization_barrier((integrals, both))
     ints_other = send(later, other_core)
     came = [send(both, chunk(q)) for q in range(half)]
 
     steps = [(sx, sd) for sx in range(chips) for sd in range(depths)]
-    steps = steps[:1] + steps[:0:-1]
+    others = steps[1:-1]
+    steps = [(steps[0],) * 2, (steps[-1],) * 2] + list(zip(others, others[::-1]))
     lanes = irreps * half * mb
     out = call(
         functools.partial(products, sizes, steps), "products", [], [shape((2 * h, lanes), F32)] * len(steps),
@@ -187,8 +194,13 @@
         scratch=[pltpu.VMEM((nb, lanes), F32)],
     )
     sums = [out[0]]
-    for (sx, sd), part in zip(steps[1:], out[1:]):
-        sums.append(send(part, lambda row, col, dep, sx=sx, sd=sd: (row ^ 2 * sx, col, dep ^ sd)))
+    for pair, part in zip(steps[1:], out[1:]):
+
+        def across(row, col, dep, pair=pair):
+            sx, sd = pair[row % 2]
+            return row ^ 2 * sx, col, dep ^ sd
+
+        sums.append(send(part, across))
 
     done = call(
         functools.partial(finish, sizes), "finish", [], [shape((2, irreps, mb, h), BF16)] * half, limits, *sums

time: 25.8 us -> 25.7 us (level)
  local copies, waits for them, and re-layouts: 0.8 us -> 0 us
  Pallas kernels: 2.73 us -> 3.53 us
  starting transfers between devices: 11.6 us -> 12.2 us
  waiting for transfers between devices: 10.4 us -> 9.82 us
    pallas_call x7, Pallas kernels: 2.73 us -> 3.53 us  [call(): pl.pallas_call(kernel, name=name, out_shape=outs, in_specs=specs + [VMEM]...]
    unnamed x2 -> x0, local copies, waits for them, and re-layouts: 0.8 us -> none
    ppermute x10, waiting for transfers between devices: 10.4 us -> 9.82 us  [send(): return lax.ppermute(value, AXES, pairs(move))]
    ppermute x10, starting transfers between devices: 11.6 us -> 12.2 us  [send(): return lax.ppermute(value, AXES, pairs(move))]
  transfers between devices with their start and end apart: 10 -> 10, of which waited for: 8 -> 7; matrix products, arithmetic and copies ran while one was open for 0% -> 0% of each run, Pallas kernels for 5% -> 8%
where the time goes in v8:
time: 25.7 us; the launch traced here: 25.6 us
  starting transfers between devices  12.2 us (47%)
  waiting for transfers between devices  9.82 us (38%)
  Pallas kernels  3.53 us (14%)
    ppermute x10, starting transfers between devices, send(): return lax.ppermute(value, AXES, pairs(move))  12.2 us
    ppermute x10, waiting for transfers between devices, send(): return lax.ppermute(value, AXES, pairs(move))  9.82 us
    pallas_call x7, Pallas kernels, call(): pl.pallas_call(kernel, name=name, out_shape=outs, in_specs=specs + [VMEM]...  3.53 us
  transfers between devices with their start and end apart: 10, of which 7 were waited for; matrix products, arithmetic and copies ran while one was open for 0% of the time, Pallas kernels for 8%

profile of v8, /device:TPU:0, one launch (start us, length us, event | category | flops | bytes accessed | tf_op | source)
XLA Modules:
  0.0 25.6 jit_solution(16183722979042338491)
XLA Ops:
  0.0 0.5 %collective-permute-start = (bf16[2,32,384]{2,1,0:T(8,128)(2,1)}, bf16[2,32,384]{2,1,0:T(8,128)(2,1)S(1)}, u32[]{:S(2)}, u32[]{:S(2)}) collective-permute-start(bf16[2,32,384]{2,1,0:T(8,128)(2,1)} %src.1), channel_id=1, source_target_pairs={{0,8},{1,9},{2,10},{3,11},{4,12},{5,13},{6,14},{7,15},{8,0},{9,1},... | collective-permute-start | bytes 147464 | tf_op jit(solution)/shard_map/ppermute | solution.py:158
  0.5 0.8 %fetch.1.mine = bf16[2,32,384]{2,1,0:T(8,128)(2,1)S(1)} custom-call(bf16[2,32,384]{2,1,0:T(8,128)(2,1)} %src.1), custom_call_target="tpu_custom_call" | custom-call | tf_op jit(solution)/shard_map/fetch/pallas_call | solution.py:129
  1.3 0.3 %collective-permute-done.other = bf16[2,32,384]{2,1,0:T(8,128)(2,1)S(1)} collective-permute-done((bf16[2,32,384]{2,1,0:T(8,128)(2,1)}, bf16[2,32,384]{2,1,0:T(8,128)(2,1)S(1)}, u32[]{:S(2)}, u32[]{:S(2)}) %collective-permute-start) | collective-permute-done | bytes 49184 | tf_op jit(solution)/shard_map/ppermute | solution.py:158
  1.6 0.4 %collective-permute-start.3 = (bf16[2,384,768]{2,1,0:T(8,128)(2,1)}, bf16[2,384,768]{2,1,0:T(8,128)(2,1)S(1)}, u32[]{:S(2)}, u32[]{:S(2)}) collective-permute-start(bf16[2,384,768]{2,1,0:T(8,128)(2,1)} %ints.1), channel_id=1, source_target_pairs={{0,8},{1,9},{2,10},{3,11},{4,12},{5,13},{6,14},{7,15},{8,0},{9,1},... | collective-permute-start | bytes 3538952 | tf_op jit(solution)/shard_map/ppermute | solution.py:158
  2.0 2.7 %collective-permute-start.2 = (bf16[2,2,32,384]{3,2,1,0:T(8,128)(2,1)S(1)}, bf16[2,2,32,384]{3,2,1,0:T(8,128)(2,1)S(1)}, u32[]{:S(2)}, u32[]{:S(2)}) collective-permute-start(bf16[2,2,32,384]{3,2,1,0:T(8,128)(2,1)S(1)} %join.1.refs_1_), channel_id=1, source_target_pairs={{0,2},{1,3},{2,0},{3,1},{4,6},{5,7},{6,4},{7,5},{8,14},{9,15},{10,... | collective-permute-start | bytes 294920 | tf_op jit(solution)/shard_map/ppermute | solution.py:158
  4.7 1.5 %collective-permute-start.1 = (bf16[2,2,32,384]{3,2,1,0:T(8,128)(2,1)S(1)}, bf16[2,2,32,384]{3,2,1,0:T(8,128)(2,1)S(1)}, u32[]{:S(2)}, u32[]{:S(2)}) collective-permute-start(bf16[2,2,32,384]{3,2,1,0:T(8,128)(2,1)S(1)} %join.1.refs_1_), channel_id=1, source_target_pairs={{0,16},{1,17},{2,18},{3,19},{4,20},{5,21},{6,22},{7,23},{8,12},{9,... | collective-permute-start | bytes 294920 | tf_op jit(solution)/shard_map/ppermute | solution.py:158
  6.2 1.3 %load.1 = (bf16[2,384,768]{2,1,0:T(8,128)(2,1)S(1)}, s32[2,2,8,128]{3,2,1,0:T(8,128)S(1)}) custom-call(s32[2]{0:T(128)} %occ.1, s32[2]{0:T(128)} %live.1, bf16[2,384,768]{2,1,0:T(8,128)(2,1)} %ints.1), custom_call_target="tpu_custom_call" | custom-call | tf_op jit(solution)/shard_map/load/pallas_call | solution.py:129
  7.5 0.0 collective-permute-done.2.refs_3_
  7.5 1.8 %collective-permute-done.1.refs_2_ = bf16[2,2,32,384]{3,2,1,0:T(8,128)(2,1)S(1)} collective-permute-done((bf16[2,2,32,384]{3,2,1,0:T(8,128)(2,1)S(1)}, bf16[2,2,32,384]{3,2,1,0:T(8,128)(2,1)S(1)}, u32[]{:S(2)}, u32[]{:S(2)}) %collective-permute-start.1) | collective-permute-done | bytes 98336 | tf_op jit(solution)/shard_map/ppermute | solution.py:158
  9.3 0.0 collective-permute-done.3.refs_5_
  9.3 0.7 %products.1 = (f32[192,128]{1,0:T(8,128)S(1)}, f32[192,128]{1,0:T(8,128)S(1)}, f32[192,128]{1,0:T(8,128)S(1)}, f32[192,128]{1,0:T(8,128)S(1)}) custom-call(s32[2,2,8,128]{3,2,1,0:T(8,128)S(1)} %get-tuple-element.15.refs_0_, bf16[2,2,32,384]{3,2,1,0:T(8,128)(2,1)S(1)} %join.1.refs_1_, bf16[2,2,32,384]{3,2,1,0:T(8,128)(2,1)S(1)} %collective-permute-done.1.refs_2_, ...), custom_call_target="tpu_custom_call" | custom-call | tf_op jit(solution)/shard_map/products/pallas_call | solution.py:129
  10.0 2.5 %collective-permute-start.4 = (f32[192,128]{1,0:T(8,128)S(1)}, f32[192,128]{1,0:T(8,128)S(1)}, u32[]{:S(2)}, u32[]{:S(2)}) collective-permute-start(f32[192,128]{1,0:T(8,128)S(1)} %get-tuple-element.20), channel_id=1, source_target_pairs={{0,17},{1,16},{2,19},{3,18},{4,21},{5,20},{6,23},{7,22},{8,25},{9,... | collective-permute-start | bytes 294920 | tf_op jit(solution)/shard_map/ppermute | solution.py:158
  12.5 0.5 %collective-permute-start.5 = (f32[192,128]{1,0:T(8,128)S(1)}, f32[192,128]{1,0:T(8,128)S(1)}, u32[]{:S(2)}, u32[]{:S(2)}) collective-permute-start(f32[192,128]{1,0:T(8,128)S(1)} %get-tuple-element.21), channel_id=1, source_target_pairs={{0,1},{1,0},{2,3},{3,2},{4,5},{5,4},{6,7},{7,6},{8,24},{9,25},{10,... | collective-permute-start | bytes 294920 | tf_op jit(solution)/shard_map/ppermute | solution.py:158
  13.0 0.5 %collective-permute-start.6 = (f32[192,128]{1,0:T(8,128)S(1)}, f32[192,128]{1,0:T(8,128)S(1)}, u32[]{:S(2)}, u32[]{:S(2)}) collective-permute-start(f32[192,128]{1,0:T(8,128)S(1)} %get-tuple-element.22), channel_id=1, source_target_pairs={{0,16},{1,17},{2,18},{3,19},{4,20},{5,21},{6,22},{7,23},{8,9},{9,8... | collective-permute-start | bytes 294920 | tf_op jit(solution)/shard_map/ppermute | solution.py:158
  13.6 2.0 %collective-permute-done.4.refs_2_ = f32[192,128]{1,0:T(8,128)S(1)} collective-permute-done((f32[192,128]{1,0:T(8,128)S(1)}, f32[192,128]{1,0:T(8,128)S(1)}, u32[]{:S(2)}, u32[]{:S(2)}) %collective-permute-start.4) | collective-permute-done | bytes 98336 | tf_op jit(solution)/shard_map/ppermute | solution.py:158
  15.6 3.0 %collective-permute-done.5.refs_3_ = f32[192,128]{1,0:T(8,128)S(1)} collective-permute-done((f32[192,128]{1,0:T(8,128)S(1)}, f32[192,128]{1,0:T(8,128)S(1)}, u32[]{:S(2)}, u32[]{:S(2)}) %collective-permute-start.5) | collective-permute-done | bytes 98336 | tf_op jit(solution)/shard_map/ppermute | solution.py:158
  18.6 0.0 collective-permute-done.6.refs_4_
  18.6 0.1 finish.1
  18.7 0.6 %collective-permute-start.7 = (bf16[2,2,32,96]{3,2,1,0:T(8,128)(2,1)S(1)}, bf16[2,2,32,96]{3,2,1,0:T(8,128)(2,1)S(1)}, u32[]{:S(2)}, u32[]{:S(2)}) collective-permute-start(bf16[2,2,32,96]{3,2,1,0:T(8,128)(2,1)S(1)} %get-tuple-element.24), channel_id=1, source_target_pairs={{0,2},{1,3},{2,0},{3,1},{4,6},{5,7},{6,4},{7,5},{8,14},{9,15},{10,... | collective-permute-start | bytes 73736 | tf_op jit(solution)/shard_map/ppermute | solution.py:158
  19.4 2.5 %collective-permute-start.8 = (bf16[2,2,32,96]{3,2,1,0:T(8,128)(2,1)S(1)}, bf16[2,2,32,96]{3,2,1,0:T(8,128)(2,1)S(1)}, u32[]{:S(2)}, u32[]{:S(2)}) collective-permute-start(bf16[2,2,32,96]{3,2,1,0:T(8,128)(2,1)S(1)} %get-tuple-element.23.first), channel_id=1, source_target_pairs={{0,8},{1,9},{2,10},{3,11},{4,12},{5,13},{6,14},{7,15},{8,4},{9,5},... | collective-permute-start | bytes 73736 | tf_op jit(solution)/shard_map/ppermute | solution.py:158
  21.8 0.9 %collective-permute-done.7.refs_0_ = bf16[2,2,32,96]{3,2,1,0:T(8,128)(2,1)S(1)} collective-permute-done((bf16[2,2,32,96]{3,2,1,0:T(8,128)(2,1)S(1)}, bf16[2,2,32,96]{3,2,1,0:T(8,128)(2,1)S(1)}, u32[]{:S(2)}, u32[]{:S(2)}) %collective-permute-start.7) | collective-permute-done | bytes 24608 | tf_op jit(solution)/shard_map/ppermute | solution.py:158
  22.7 0.9 %collective-permute-done.8.refs_1_ = bf16[2,2,32,96]{3,2,1,0:T(8,128)(2,1)S(1)} collective-permute-done((bf16[2,2,32,96]{3,2,1,0:T(8,128)(2,1)S(1)}, bf16[2,2,32,96]{3,2,1,0:T(8,128)(2,1)S(1)}, u32[]{:S(2)}, u32[]{:S(2)}) %collective-permute-start.8) | collective-permute-done | bytes 24608 | tf_op jit(solution)/shard_map/ppermute | solution.py:158
  23.6 0.4 %collective-permute-start.9 = (bf16[2,2,32,96]{3,2,1,0:T(8,128)(2,1)S(1)}, bf16[2,2,32,96]{3,2,1,0:T(8,128)(2,1)S(1)}, u32[]{:S(2)}, u32[]{:S(2)}) collective-permute-start(bf16[2,2,32,96]{3,2,1,0:T(8,128)(2,1)S(1)} %settle.1), channel_id=1, source_target_pairs={{0,8},{1,9},{2,10},{3,11},{4,12},{5,13},{6,14},{7,15},{8,0},{9,1},... | collective-permute-start | bytes 73736 | tf_op jit(solution)/shard_map/ppermute | solution.py:158
  24.0 0.9 %collective-permute-done.9.refs_2_ = bf16[2,2,32,96]{3,2,1,0:T(8,128)(2,1)S(1)} collective-permute-done((bf16[2,2,32,96]{3,2,1,0:T(8,128)(2,1)S(1)}, bf16[2,2,32,96]{3,2,1,0:T(8,128)(2,1)S(1)}, u32[]{:S(2)}, u32[]{:S(2)}) %collective-permute-start.9) | collective-permute-done | bytes 24608 | tf_op jit(solution)/shard_map/ppermute | solution.py:158
  24.9 0.6 %assemble.1 = bf16[4,2,32,96]{3,2,1,0:T(8,128)(2,1)} custom-call(bf16[2,2,32,96]{3,2,1,0:T(8,128)(2,1)S(1)} %get-tuple-element.23.first, bf16[2,2,32,96]{3,2,1,0:T(8,128)(2,1)S(1)} %collective-permute-done.7.refs_0_, bf16[2,2,32,96]{3,2,1,0:T(8,128)(2,1)S(1)} %collective-permute-done.8.refs_1_, bf16[2,2,32,96]{3,2,1,0:T(8,128)(2,1)S(1)} %collective-permute-done.9.refs_2_), custom_call_target="tpu_custom_call" | custom-call | tf_op jit(solution)/shard_map/assemble/pallas_call | solution.py:129
  (2 shorter events, 0.0 us)
Async XLA Ops:
  0.0 1.5 %collective-permute-start = (bf16[2,32,384]{2,1,0:T(8,128)(2,1)}, bf16[2,32,384]{2,1,0:T(8,128)(2,1)S(1)}, u32[]{:S(2)}, u32[]{:S(2)}) collective-permute-start(bf16[2,32,384]{2,1,0:T(8,128)(2,1)} %src.1), channel_id=1, source_target_pairs={{0,8},{1,9},{2,10},{3,11},{4,12},{5,13},{6,14},{7,15},{8,0},{9,1},... | collective-permute-start | bytes 147464 | tf_op jit(solution)/shard_map/ppermute | solution.py:158
  1.6 7.8 %collective-permute-start.3 = (bf16[2,384,768]{2,1,0:T(8,128)(2,1)}, bf16[2,384,768]{2,1,0:T(8,128)(2,1)S(1)}, u32[]{:S(2)}, u32[]{:S(2)}) collective-permute-start(bf16[2,384,768]{2,1,0:T(8,128)(2,1)} %ints.1), channel_id=1, source_target_pairs={{0,8},{1,9},{2,10},{3,11},{4,12},{5,13},{6,14},{7,15},{8,0},{9,1},... | collective-permute-start | bytes 3538952 | tf_op jit(solution)/shard_map/ppermute | solution.py:158
  2.0 5.5 %collective-permute-start.2 = (bf16[2,2,32,384]{3,2,1,0:T(8,128)(2,1)S(1)}, bf16[2,2,32,384]{3,2,1,0:T(8,128)(2,1)S(1)}, u32[]{:S(2)}, u32[]{:S(2)}) collective-permute-start(bf16[2,2,32,384]{3,2,1,0:T(8,128)(2,1)S(1)} %join.1.refs_1_), channel_id=1, source_target_pairs={{0,2},{1,3},{2,0},{3,1},{4,6},{5,7},{6,4},{7,5},{8,14},{9,15},{10,... | collective-permute-start | bytes 294920 | tf_op jit(solution)/shard_map/ppermute | solution.py:158
  4.7 4.6 %collective-permute-start.1 = (bf16[2,2,32,384]{3,2,1,0:T(8,128)(2,1)S(1)}, bf16[2,2,32,384]{3,2,1,0:T(8,128)(2,1)S(1)}, u32[]{:S(2)}, u32[]{:S(2)}) collective-permute-start(bf16[2,2,32,384]{3,2,1,0:T(8,128)(2,1)S(1)} %join.1.refs_1_), channel_id=1, source_target_pairs={{0,16},{1,17},{2,18},{3,19},{4,20},{5,21},{6,22},{7,23},{8,12},{9,... | collective-permute-start | bytes 294920 | tf_op jit(solution)/shard_map/ppermute | solution.py:158
  10.0 5.6 %collective-permute-start.4 = (f32[192,128]{1,0:T(8,128)S(1)}, f32[192,128]{1,0:T(8,128)S(1)}, u32[]{:S(2)}, u32[]{:S(2)}) collective-permute-start(f32[192,128]{1,0:T(8,128)S(1)} %get-tuple-element.20), channel_id=1, source_target_pairs={{0,17},{1,16},{2,19},{3,18},{4,21},{5,20},{6,23},{7,22},{8,25},{9,... | collective-permute-start | bytes 294920 | tf_op jit(solution)/shard_map/ppermute | solution.py:158
  12.5 6.1 %collective-permute-start.5 = (f32[192,128]{1,0:T(8,128)S(1)}, f32[192,128]{1,0:T(8,128)S(1)}, u32[]{:S(2)}, u32[]{:S(2)}) collective-permute-start(f32[192,128]{1,0:T(8,128)S(1)} %get-tuple-element.21), channel_id=1, source_target_pairs={{0,1},{1,0},{2,3},{3,2},{4,5},{5,4},{6,7},{7,6},{8,24},{9,25},{10,... | collective-permute-start | bytes 294920 | tf_op jit(solution)/shard_map/ppermute | solution.py:158
  13.0 5.6 %collective-permute-start.6 = (f32[192,128]{1,0:T(8,128)S(1)}, f32[192,128]{1,0:T(8,128)S(1)}, u32[]{:S(2)}, u32[]{:S(2)}) collective-permute-start(f32[192,128]{1,0:T(8,128)S(1)} %get-tuple-element.22), channel_id=1, source_target_pairs={{0,16},{1,17},{2,18},{3,19},{4,20},{5,21},{6,22},{7,23},{8,9},{9,8... | collective-permute-start | bytes 294920 | tf_op jit(solution)/shard_map/ppermute | solution.py:158
  18.7 4.0 %collective-permute-start.7 = (bf16[2,2,32,96]{3,2,1,0:T(8,128)(2,1)S(1)}, bf16[2,2,32,96]{3,2,1,0:T(8,128)(2,1)S(1)}, u32[]{:S(2)}, u32[]{:S(2)}) collective-permute-start(bf16[2,2,32,96]{3,2,1,0:T(8,128)(2,1)S(1)} %get-tuple-element.24), channel_id=1, source_target_pairs={{0,2},{1,3},{2,0},{3,1},{4,6},{5,7},{6,4},{7,5},{8,14},{9,15},{10,... | collective-permute-start | bytes 73736 | tf_op jit(solution)/shard_map/ppermute | solution.py:158
  19.4 4.2 %collective-permute-start.8 = (bf16[2,2,32,96]{3,2,1,0:T(8,128)(2,1)S(1)}, bf16[2,2,32,96]{3,2,1,0:T(8,128)(2,1)S(1)}, u32[]{:S(2)}, u32[]{:S(2)}) collective-permute-start(bf16[2,2,32,96]{3,2,1,0:T(8,128)(2,1)S(1)} %get-tuple-element.23.first), channel_id=1, source_target_pairs={{0,8},{1,9},{2,10},{3,11},{4,12},{5,13},{6,14},{7,15},{8,4},{9,5},... | collective-permute-start | bytes 73736 | tf_op jit(solution)/shard_map/ppermute | solution.py:158
  23.6 1.3 %collective-permute-start.9 = (bf16[2,2,32,96]{3,2,1,0:T(8,128)(2,1)S(1)}, bf16[2,2,32,96]{3,2,1,0:T(8,128)(2,1)S(1)}, u32[]{:S(2)}, u32[]{:S(2)}) collective-permute-start(bf16[2,2,32,96]{3,2,1,0:T(8,128)(2,1)S(1)} %settle.1), channel_id=1, source_target_pairs={{0,8},{1,9},{2,10},{3,11},{4,12},{5,13},{6,14},{7,15},{8,0},{9,1},... | collective-permute-start | bytes 73736 | tf_op jit(solution)/shard_map/ppermute | solution.py:158

commit v9 on v6

--- a/solution.py
+++ b/solution.py
@@ -161,7 +161,7 @@
         def move(row, col, dep):
             if row % 2:
                 return row, col ^ (q + half), dep
-            return (row, col ^ q, dep) if q else (row ^ 2, col, dep)
+            return (row, col ^ q, dep) if q else (row, col, dep ^ 1)
 
         return move
 
@@ -179,7 +179,7 @@
     came = [send(both, chunk(q)) for q in range(half)]
 
     steps = [(sx, sd) for sx in range(chips) for sd in range(depths)]
-    steps = steps[:1] + steps[:0:-1]
+    steps = steps[:1] + steps[-1:] + steps[1:-1]
     lanes = irreps * half * mb
     out = call(
         functools.partial(products, sizes, steps), "products", [], [shape((2 * h, lanes), F32)] * len(steps),

time: 25.8 us -> 25.7 us (level)
  starting transfers between devices: 11.6 us -> 12.1 us
  waiting for transfers between devices: 10.4 us -> 9.92 us
    ppermute x10, waiting for transfers between devices: 10.4 us -> 9.92 us  [send(): return lax.ppermute(value, AXES, pairs(move))]
    ppermute x10, starting transfers between devices: 11.6 us -> 12.1 us  [send(): return lax.ppermute(value, AXES, pairs(move))]
  transfers between devices with their start and end apart: 10 -> 10, of which waited for: 8 -> 7; matrix products, arithmetic and copies ran while one was open for 0% -> 0% of each run, Pallas kernels for 5% -> 5%
where the time goes in v9:
time: 25.7 us; the launch traced here: 25.6 us
  starting transfers between devices  12.1 us (47%)
  waiting for transfers between devices  9.92 us (39%)
  Pallas kernels  2.73 us (11%)
  local copies, waits for them, and re-layouts  0.8 us (3%)
    ppermute x10, starting transfers between devices, send(): return lax.ppermute(value, AXES, pairs(move))  12.1 us
    ppermute x10, waiting for transfers between devices, send(): return lax.ppermute(value, AXES, pairs(move))  9.92 us
    pallas_call x7, Pallas kernels, call(): pl.pallas_call(kernel, name=name, out_shape=outs, in_specs=specs + [VMEM]...  2.73 us
    unnamed x2, local copies, waits for them, and re-layouts  0.8 us
  transfers between devices with their start and end apart: 10, of which 7 were waited for; matrix products, arithmetic and copies ran while one was open for 0% of the time, Pallas kernels for 5%

profile of v9, /device:TPU:0, one launch (start us, length us, event | category | flops | bytes accessed | tf_op | source)
XLA Modules:
  0.0 25.6 jit_solution(12872034777037093503)
XLA Ops:
  0.0 0.5 %collective-permute-start = (bf16[2,32,384]{2,1,0:T(8,128)(2,1)}, bf16[2,32,384]{2,1,0:T(8,128)(2,1)S(1)}, u32[]{:S(2)}, u32[]{:S(2)}) collective-permute-start(bf16[2,32,384]{2,1,0:T(8,128)(2,1)} %src.1), channel_id=1, source_target_pairs={{0,8},{1,9},{2,10},{3,11},{4,12},{5,13},{6,14},{7,15},{8,0},{9,1},... | collective-permute-start | bytes 147464 | tf_op jit(solution)/shard_map/ppermute | solution.py:155
  0.5 0.0 copy-start
  0.5 0.8 %copy-done = bf16[2,32,384]{2,1,0:T(8,128)(2,1)S(1)} copy-done((bf16[2,32,384]{2,1,0:T(8,128)(2,1)S(1)}, bf16[2,32,384]{2,1,0:T(8,128)(2,1)}, u32[]{:S(2)}) %copy-start) | copy-done | bytes 49176
  1.3 0.3 %collective-permute-done.other = bf16[2,32,384]{2,1,0:T(8,128)(2,1)S(1)} collective-permute-done((bf16[2,32,384]{2,1,0:T(8,128)(2,1)}, bf16[2,32,384]{2,1,0:T(8,128)(2,1)S(1)}, u32[]{:S(2)}, u32[]{:S(2)}) %collective-permute-start) | collective-permute-done | bytes 49184 | tf_op jit(solution)/shard_map/ppermute | solution.py:155
  1.6 0.4 %collective-permute-start.3 = (bf16[2,384,768]{2,1,0:T(8,128)(2,1)}, bf16[2,384,768]{2,1,0:T(8,128)(2,1)S(1)}, u32[]{:S(2)}, u32[]{:S(2)}) collective-permute-start(bf16[2,384,768]{2,1,0:T(8,128)(2,1)} %ints.1), channel_id=1, source_target_pairs={{0,8},{1,9},{2,10},{3,11},{4,12},{5,13},{6,14},{7,15},{8,0},{9,1},... | collective-permute-start | bytes 3538952 | tf_op jit(solution)/shard_map/ppermute | solution.py:155
  2.0 2.7 %collective-permute-start.2 = (bf16[2,2,32,384]{3,2,1,0:T(8,128)(2,1)S(1)}, bf16[2,2,32,384]{3,2,1,0:T(8,128)(2,1)S(1)}, u32[]{:S(2)}, u32[]{:S(2)}) collective-permute-start(bf16[2,2,32,384]{3,2,1,0:T(8,128)(2,1)S(1)} %join.1.refs_1_), channel_id=1, source_target_pairs={{0,2},{1,3},{2,0},{3,1},{4,6},{5,7},{6,4},{7,5},{8,14},{9,15},{10,... | collective-permute-start | bytes 294920 | tf_op jit(solution)/shard_map/ppermute | solution.py:155
  4.7 1.5 %collective-permute-start.1 = (bf16[2,2,32,384]{3,2,1,0:T(8,128)(2,1)S(1)}, bf16[2,2,32,384]{3,2,1,0:T(8,128)(2,1)S(1)}, u32[]{:S(2)}, u32[]{:S(2)}) collective-permute-start(bf16[2,2,32,384]{3,2,1,0:T(8,128)(2,1)S(1)} %join.1.refs_1_), channel_id=1, source_target_pairs={{0,1},{1,0},{2,3},{3,2},{4,5},{5,4},{6,7},{7,6},{8,12},{9,13},{10,... | collective-permute-start | bytes 294920 | tf_op jit(solution)/shard_map/ppermute | solution.py:155
  6.2 1.3 %load.1 = (bf16[2,384,768]{2,1,0:T(8,128)(2,1)S(1)}, s32[2,2,8,128]{3,2,1,0:T(8,128)S(1)}) custom-call(s32[2]{0:T(128)} %occ.1, s32[2]{0:T(128)} %live.1, bf16[2,384,768]{2,1,0:T(8,128)(2,1)} %ints.1), custom_call_target="tpu_custom_call" | custom-call | tf_op jit(solution)/shard_map/load/pallas_call | solution.py:126
  7.5 0.0 collective-permute-done.2.refs_3_
  7.5 1.8 %collective-permute-done.1.refs_2_ = bf16[2,2,32,384]{3,2,1,0:T(8,128)(2,1)S(1)} collective-permute-done((bf16[2,2,32,384]{3,2,1,0:T(8,128)(2,1)S(1)}, bf16[2,2,32,384]{3,2,1,0:T(8,128)(2,1)S(1)}, u32[]{:S(2)}, u32[]{:S(2)}) %collective-permute-start.1) | collective-permute-done | bytes 98336 | tf_op jit(solution)/shard_map/ppermute | solution.py:155
  9.3 0.0 collective-permute-done.3.refs_5_
  9.3 0.7 %products.1 = (f32[192,128]{1,0:T(8,128)S(1)}, f32[192,128]{1,0:T(8,128)S(1)}, f32[192,128]{1,0:T(8,128)S(1)}, f32[192,128]{1,0:T(8,128)S(1)}) custom-call(s32[2,2,8,128]{3,2,1,0:T(8,128)S(1)} %get-tuple-element.15.refs_0_, bf16[2,2,32,384]{3,2,1,0:T(8,128)(2,1)S(1)} %join.1.refs_1_, bf16[2,2,32,384]{3,2,1,0:T(8,128)(2,1)S(1)} %collective-permute-done.1.refs_2_, ...), custom_call_target="tpu_custom_call" | custom-call | tf_op jit(solution)/shard_map/products/pallas_call | solution.py:126
  10.0 2.5 %collective-permute-start.4 = (f32[192,128]{1,0:T(8,128)S(1)}, f32[192,128]{1,0:T(8,128)S(1)}, u32[]{:S(2)}, u32[]{:S(2)}) collective-permute-start(f32[192,128]{1,0:T(8,128)S(1)} %get-tuple-element.20), channel_id=1, source_target_pairs={{0,17},{1,16},{2,19},{3,18},{4,21},{5,20},{6,23},{7,22},{8,25},{9,... | collective-permute-start | bytes 294920 | tf_op jit(solution)/shard_map/ppermute | solution.py:155
  12.5 0.5 %collective-permute-start.5 = (f32[192,128]{1,0:T(8,128)S(1)}, f32[192,128]{1,0:T(8,128)S(1)}, u32[]{:S(2)}, u32[]{:S(2)}) collective-permute-start(f32[192,128]{1,0:T(8,128)S(1)} %get-tuple-element.21), channel_id=1, source_target_pairs={{0,1},{1,0},{2,3},{3,2},{4,5},{5,4},{6,7},{7,6},{8,9},{9,8},{10,11... | collective-permute-start | bytes 294920 | tf_op jit(solution)/shard_map/ppermute | solution.py:155
  13.0 0.5 %collective-permute-start.6 = (f32[192,128]{1,0:T(8,128)S(1)}, f32[192,128]{1,0:T(8,128)S(1)}, u32[]{:S(2)}, u32[]{:S(2)}) collective-permute-start(f32[192,128]{1,0:T(8,128)S(1)} %get-tuple-element.22), channel_id=1, source_target_pairs={{0,16},{1,17},{2,18},{3,19},{4,20},{5,21},{6,22},{7,23},{8,24},{9,... | collective-permute-start | bytes 294920 | tf_op jit(solution)/shard_map/ppermute | solution.py:155
  13.6 2.0 %collective-permute-done.4.refs_2_ = f32[192,128]{1,0:T(8,128)S(1)} collective-permute-done((f32[192,128]{1,0:T(8,128)S(1)}, f32[192,128]{1,0:T(8,128)S(1)}, u32[]{:S(2)}, u32[]{:S(2)}) %collective-permute-start.4) | collective-permute-done | bytes 98336 | tf_op jit(solution)/shard_map/ppermute | solution.py:155
  15.6 3.3 %collective-permute-done.5.refs_3_ = f32[192,128]{1,0:T(8,128)S(1)} collective-permute-done((f32[192,128]{1,0:T(8,128)S(1)}, f32[192,128]{1,0:T(8,128)S(1)}, u32[]{:S(2)}, u32[]{:S(2)}) %collective-permute-start.5) | collective-permute-done | bytes 98336 | tf_op jit(solution)/shard_map/ppermute | solution.py:155
  18.9 0.0 collective-permute-done.6.refs_4_
  18.9 0.1 finish.1
  19.0 0.3 %collective-permute-start.7 = (bf16[2,2,32,96]{3,2,1,0:T(8,128)(2,1)S(1)}, bf16[2,2,32,96]{3,2,1,0:T(8,128)(2,1)S(1)}, u32[]{:S(2)}, u32[]{:S(2)}) collective-permute-start(bf16[2,2,32,96]{3,2,1,0:T(8,128)(2,1)S(1)} %get-tuple-element.24), channel_id=1, source_target_pairs={{0,2},{1,3},{2,0},{3,1},{4,6},{5,7},{6,4},{7,5},{8,14},{9,15},{10,... | collective-permute-start | bytes 73736 | tf_op jit(solution)/shard_map/ppermute | solution.py:155
  19.4 2.6 %collective-permute-start.8 = (bf16[2,2,32,96]{3,2,1,0:T(8,128)(2,1)S(1)}, bf16[2,2,32,96]{3,2,1,0:T(8,128)(2,1)S(1)}, u32[]{:S(2)}, u32[]{:S(2)}) collective-permute-start(bf16[2,2,32,96]{3,2,1,0:T(8,128)(2,1)S(1)} %get-tuple-element.23.first), channel_id=1, source_target_pairs={{0,8},{1,9},{2,10},{3,11},{4,12},{5,13},{6,14},{7,15},{8,4},{9,5},... | collective-permute-start | bytes 73736 | tf_op jit(solution)/shard_map/ppermute | solution.py:155
  22.0 1.0 %collective-permute-done.7.refs_0_ = bf16[2,2,32,96]{3,2,1,0:T(8,128)(2,1)S(1)} collective-permute-done((bf16[2,2,32,96]{3,2,1,0:T(8,128)(2,1)S(1)}, bf16[2,2,32,96]{3,2,1,0:T(8,128)(2,1)S(1)}, u32[]{:S(2)}, u32[]{:S(2)}) %collective-permute-start.7) | collective-permute-done | bytes 24608 | tf_op jit(solution)/shard_map/ppermute | solution.py:155
  23.0 0.6 %collective-permute-done.8.refs_1_ = bf16[2,2,32,96]{3,2,1,0:T(8,128)(2,1)S(1)} collective-permute-done((bf16[2,2,32,96]{3,2,1,0:T(8,128)(2,1)S(1)}, bf16[2,2,32,96]{3,2,1,0:T(8,128)(2,1)S(1)}, u32[]{:S(2)}, u32[]{:S(2)}) %collective-permute-start.8) | collective-permute-done | bytes 24608 | tf_op jit(solution)/shard_map/ppermute | solution.py:155
  23.6 0.4 %collective-permute-start.9 = (bf16[2,2,32,96]{3,2,1,0:T(8,128)(2,1)S(1)}, bf16[2,2,32,96]{3,2,1,0:T(8,128)(2,1)S(1)}, u32[]{:S(2)}, u32[]{:S(2)}) collective-permute-start(bf16[2,2,32,96]{3,2,1,0:T(8,128)(2,1)S(1)} %settle.1), channel_id=1, source_target_pairs={{0,8},{1,9},{2,10},{3,11},{4,12},{5,13},{6,14},{7,15},{8,0},{9,1},... | collective-permute-start | bytes 73736 | tf_op jit(solution)/shard_map/ppermute | solution.py:155
  24.0 0.9 %collective-permute-done.9.refs_2_ = bf16[2,2,32,96]{3,2,1,0:T(8,128)(2,1)S(1)} collective-permute-done((bf16[2,2,32,96]{3,2,1,0:T(8,128)(2,1)S(1)}, bf16[2,2,32,96]{3,2,1,0:T(8,128)(2,1)S(1)}, u32[]{:S(2)}, u32[]{:S(2)}) %collective-permute-start.9) | collective-permute-done | bytes 24608 | tf_op jit(solution)/shard_map/ppermute | solution.py:155
  24.9 0.6 %assemble.1 = bf16[4,2,32,96]{3,2,1,0:T(8,128)(2,1)} custom-call(bf16[2,2,32,96]{3,2,1,0:T(8,128)(2,1)S(1)} %get-tuple-element.23.first, bf16[2,2,32,96]{3,2,1,0:T(8,128)(2,1)S(1)} %collective-permute-done.7.refs_0_, bf16[2,2,32,96]{3,2,1,0:T(8,128)(2,1)S(1)} %collective-permute-done.8.refs_1_, bf16[2,2,32,96]{3,2,1,0:T(8,128)(2,1)S(1)} %collective-permute-done.9.refs_2_), custom_call_target="tpu_custom_call" | custom-call | tf_op jit(solution)/shard_map/assemble/pallas_call | solution.py:126
  (3 shorter events, 0.0 us)
Async XLA Ops:
  0.0 1.5 %collective-permute-start = (bf16[2,32,384]{2,1,0:T(8,128)(2,1)}, bf16[2,32,384]{2,1,0:T(8,128)(2,1)S(1)}, u32[]{:S(2)}, u32[]{:S(2)}) collective-permute-start(bf16[2,32,384]{2,1,0:T(8,128)(2,1)} %src.1), channel_id=1, source_target_pairs={{0,8},{1,9},{2,10},{3,11},{4,12},{5,13},{6,14},{7,15},{8,0},{9,1},... | collective-permute-start | bytes 147464 | tf_op jit(solution)/shard_map/ppermute | solution.py:155
  0.5 0.8 %copy-start = (bf16[2,32,384]{2,1,0:T(8,128)(2,1)S(1)}, bf16[2,32,384]{2,1,0:T(8,128)(2,1)}, u32[]{:S(2)}) copy-start(bf16[2,32,384]{2,1,0:T(8,128)(2,1)} %src.1) | copy-start | bytes 147460
  1.6 7.8 %collective-permute-start.3 = (bf16[2,384,768]{2,1,0:T(8,128)(2,1)}, bf16[2,384,768]{2,1,0:T(8,128)(2,1)S(1)}, u32[]{:S(2)}, u32[]{:S(2)}) collective-permute-start(bf16[2,384,768]{2,1,0:T(8,128)(2,1)} %ints.1), channel_id=1, source_target_pairs={{0,8},{1,9},{2,10},{3,11},{4,12},{5,13},{6,14},{7,15},{8,0},{9,1},... | collective-permute-start | bytes 3538952 | tf_op jit(solution)/shard_map/ppermute | solution.py:155
  2.0 5.5 %collective-permute-start.2 = (bf16[2,2,32,384]{3,2,1,0:T(8,128)(2,1)S(1)}, bf16[2,2,32,384]{3,2,1,0:T(8,128)(2,1)S(1)}, u32[]{:S(2)}, u32[]{:S(2)}) collective-permute-start(bf16[2,2,32,384]{3,2,1,0:T(8,128)(2,1)S(1)} %join.1.refs_1_), channel_id=1, source_target_pairs={{0,2},{1,3},{2,0},{3,1},{4,6},{5,7},{6,4},{7,5},{8,14},{9,15},{10,... | collective-permute-start | bytes 294920 | tf_op jit(solution)/shard_map/ppermute | solution.py:155
  4.7 4.6 %collective-permute-start.1 = (bf16[2,2,32,384]{3,2,1,0:T(8,128)(2,1)S(1)}, bf16[2,2,32,384]{3,2,1,0:T(8,128)(2,1)S(1)}, u32[]{:S(2)}, u32[]{:S(2)}) collective-permute-start(bf16[2,2,32,384]{3,2,1,0:T(8,128)(2,1)S(1)} %join.1.refs_1_), channel_id=1, source_target_pairs={{0,1},{1,0},{2,3},{3,2},{4,5},{5,4},{6,7},{7,6},{8,12},{9,13},{10,... | collective-permute-start | bytes 294920 | tf_op jit(solution)/shard_map/ppermute | solution.py:155
  10.0 5.6 %collective-permute-start.4 = (f32[192,128]{1,0:T(8,128)S(1)}, f32[192,128]{1,0:T(8,128)S(1)}, u32[]{:S(2)}, u32[]{:S(2)}) collective-permute-start(f32[192,128]{1,0:T(8,128)S(1)} %get-tuple-element.20), channel_id=1, source_target_pairs={{0,17},{1,16},{2,19},{3,18},{4,21},{5,20},{6,23},{7,22},{8,25},{9,... | collective-permute-start | bytes 294920 | tf_op jit(solution)/shard_map/ppermute | solution.py:155
  12.5 6.4 %collective-permute-start.5 = (f32[192,128]{1,0:T(8,128)S(1)}, f32[192,128]{1,0:T(8,128)S(1)}, u32[]{:S(2)}, u32[]{:S(2)}) collective-permute-start(f32[192,128]{1,0:T(8,128)S(1)} %get-tuple-element.21), channel_id=1, source_target_pairs={{0,1},{1,0},{2,3},{3,2},{4,5},{5,4},{6,7},{7,6},{8,9},{9,8},{10,11... | collective-permute-start | bytes 294920 | tf_op jit(solution)/shard_map/ppermute | solution.py:155
  13.0 5.9 %collective-permute-start.6 = (f32[192,128]{1,0:T(8,128)S(1)}, f32[192,128]{1,0:T(8,128)S(1)}, u32[]{:S(2)}, u32[]{:S(2)}) collective-permute-start(f32[192,128]{1,0:T(8,128)S(1)} %get-tuple-element.22), channel_id=1, source_target_pairs={{0,16},{1,17},{2,18},{3,19},{4,20},{5,21},{6,22},{7,23},{8,24},{9,... | collective-permute-start | bytes 294920 | tf_op jit(solution)/shard_map/ppermute | solution.py:155
  19.0 4.0 %collective-permute-start.7 = (bf16[2,2,32,96]{3,2,1,0:T(8,128)(2,1)S(1)}, bf16[2,2,32,96]{3,2,1,0:T(8,128)(2,1)S(1)}, u32[]{:S(2)}, u32[]{:S(2)}) collective-permute-start(bf16[2,2,32,96]{3,2,1,0:T(8,128)(2,1)S(1)} %get-tuple-element.24), channel_id=1, source_target_pairs={{0,2},{1,3},{2,0},{3,1},{4,6},{5,7},{6,4},{7,5},{8,14},{9,15},{10,... | collective-permute-start | bytes 73736 | tf_op jit(solution)/shard_map/ppermute | solution.py:155
  19.4 4.2 %collective-permute-start.8 = (bf16[2,2,32,96]{3,2,1,0:T(8,128)(2,1)S(1)}, bf16[2,2,32,96]{3,2,1,0:T(8,128)(2,1)S(1)}, u32[]{:S(2)}, u32[]{:S(2)}) collective-permute-start(bf16[2,2,32,96]{3,2,1,0:T(8,128)(2,1)S(1)} %get-tuple-element.23.first), channel_id=1, source_target_pairs={{0,8},{1,9},{2,10},{3,11},{4,12},{5,13},{6,14},{7,15},{8,4},{9,5},... | collective-permute-start | bytes 73736 | tf_op jit(solution)/shard_map/ppermute | solution.py:155
  23.6 1.3 %collective-permute-start.9 = (bf16[2,2,32,96]{3,2,1,0:T(8,128)(2,1)S(1)}, bf16[2,2,32,96]{3,2,1,0:T(8,128)(2,1)S(1)}, u32[]{:S(2)}, u32[]{:S(2)}) collective-permute-start(bf16[2,2,32,96]{3,2,1,0:T(8,128)(2,1)S(1)} %settle.1), channel_id=1, source_target_pairs={{0,8},{1,9},{2,10},{3,11},{4,12},{5,13},{6,14},{7,15},{8,0},{9,1},... | collective-permute-start | bytes 73736 | tf_op jit(solution)/shard_map/ppermute | solution.py:155

commit v10 on v6

--- a/solution.py
+++ b/solution.py
@@ -27,8 +27,10 @@
             limits[kind, g] = jnp.full(limits.shape[2:], counts[kind, g], jnp.int32)
 
 
-def copy(src, dst):
-    dst[...] = src[...]
+def fetch(src, dst, sem):
+    one = pltpu.make_async_copy(src, dst, sem)
+    one.start()
+    one.wait()
 
 
 def join(mine, other, both):
@@ -172,7 +174,10 @@
         load, "load", [HBM] * 3, [shape(integrals.shape, BF16), shape((2, irreps, 8, 128), jnp.int32)], *held,
         scratch=[pltpu.SMEM((2, irreps), jnp.int32), pltpu.SemaphoreType.DMA((2 + irreps,))],
     )
-    mine = call(copy, "fetch", [], shape(amplitudes.shape, BF16), amplitudes)
+    mine = call(
+        fetch, "fetch", [HBM], shape(amplitudes.shape, BF16), pltpu.with_memory_space_constraint(amplitudes, pltpu.HBM),
+        scratch=[pltpu.SemaphoreType.DMA],
+    )
     both = call(join, "join", [], shape((2, irreps, mb, kb), BF16), mine, amps_other)
     later, both = lax.optimization_barrier((integrals, both))
     ints_other = send(later, other_core)

time: 25.8 us -> 25.8 us (level)
  local copies, waits for them, and re-layouts: 0.8 us -> 0 us
  Pallas kernels: 2.73 us -> 3.53 us
    pallas_call x7, Pallas kernels: 2.73 us -> 3.53 us  [call(): pl.pallas_call(kernel, name=name, out_shape=outs, in_specs=specs + [VMEM]...]
    unnamed x2 -> x0, local copies, waits for them, and re-layouts: 0.8 us -> none
  transfers between devices with their start and end apart: 10 -> 10, of which waited for: 8 -> 8; matrix products, arithmetic and copies ran while one was open for 0% -> 0% of each run, Pallas kernels for 5% -> 8%
where the time goes in v10:
time: 25.8 us; the launch traced here: 25.6 us
  starting transfers between devices  11.6 us (45%)
  waiting for transfers between devices  10.4 us (40%)
  Pallas kernels  3.53 us (14%)
    ppermute x10, starting transfers between devices, send(): return lax.ppermute(value, AXES, pairs(move))  11.6 us
    ppermute x10, waiting for transfers between devices, send(): return lax.ppermute(value, AXES, pairs(move))  10.4 us
    pallas_call x7, Pallas kernels, call(): pl.pallas_call(kernel, name=name, out_shape=outs, in_specs=specs + [VMEM]...  3.53 us
  transfers between devices with their start and end apart: 10, of which 8 were waited for; matrix products, arithmetic and copies ran while one was open for 0% of the time, Pallas kernels for 8%

profile of v10, /device:TPU:0, one launch (start us, length us, event | category | flops | bytes accessed | tf_op | source)
XLA Modules:
  0.0 25.6 jit_solution(3780360106976464916)
XLA Ops:
  0.0 0.5 %collective-permute-start = (bf16[2,32,384]{2,1,0:T(8,128)(2,1)}, bf16[2,32,384]{2,1,0:T(8,128)(2,1)S(1)}, u32[]{:S(2)}, u32[]{:S(2)}) collective-permute-start(bf16[2,32,384]{2,1,0:T(8,128)(2,1)} %src.1), channel_id=1, source_target_pairs={{0,8},{1,9},{2,10},{3,11},{4,12},{5,13},{6,14},{7,15},{8,0},{9,1},... | collective-permute-start | bytes 147464 | tf_op jit(solution)/shard_map/ppermute | solution.py:157
  0.5 0.8 %fetch.1.mine = bf16[2,32,384]{2,1,0:T(8,128)(2,1)S(1)} custom-call(bf16[2,32,384]{2,1,0:T(8,128)(2,1)} %src.1), custom_call_target="tpu_custom_call" | custom-call | tf_op jit(solution)/shard_map/fetch/pallas_call | solution.py:128
  1.3 0.3 %collective-permute-done.other = bf16[2,32,384]{2,1,0:T(8,128)(2,1)S(1)} collective-permute-done((bf16[2,32,384]{2,1,0:T(8,128)(2,1)}, bf16[2,32,384]{2,1,0:T(8,128)(2,1)S(1)}, u32[]{:S(2)}, u32[]{:S(2)}) %collective-permute-start) | collective-permute-done | bytes 49184 | tf_op jit(solution)/shard_map/ppermute | solution.py:157
  1.6 0.4 %collective-permute-start.3 = (bf16[2,384,768]{2,1,0:T(8,128)(2,1)}, bf16[2,384,768]{2,1,0:T(8,128)(2,1)S(1)}, u32[]{:S(2)}, u32[]{:S(2)}) collective-permute-start(bf16[2,384,768]{2,1,0:T(8,128)(2,1)} %ints.1), channel_id=1, source_target_pairs={{0,8},{1,9},{2,10},{3,11},{4,12},{5,13},{6,14},{7,15},{8,0},{9,1},... | collective-permute-start | bytes 3538952 | tf_op jit(solution)/shard_map/ppermute | solution.py:157
  2.0 2.7 %collective-permute-start.2 = (bf16[2,2,32,384]{3,2,1,0:T(8,128)(2,1)S(1)}, bf16[2,2,32,384]{3,2,1,0:T(8,128)(2,1)S(1)}, u32[]{:S(2)}, u32[]{:S(2)}) collective-permute-start(bf16[2,2,32,384]{3,2,1,0:T(8,128)(2,1)S(1)} %join.1.refs_1_), channel_id=1, source_target_pairs={{0,2},{1,3},{2,0},{3,1},{4,6},{5,7},{6,4},{7,5},{8,14},{9,15},{10,... | collective-permute-start | bytes 294920 | tf_op jit(solution)/shard_map/ppermute | solution.py:157
  4.7 1.5 %collective-permute-start.1 = (bf16[2,2,32,384]{3,2,1,0:T(8,128)(2,1)S(1)}, bf16[2,2,32,384]{3,2,1,0:T(8,128)(2,1)S(1)}, u32[]{:S(2)}, u32[]{:S(2)}) collective-permute-start(bf16[2,2,32,384]{3,2,1,0:T(8,128)(2,1)S(1)} %join.1.refs_1_), channel_id=1, source_target_pairs={{0,16},{1,17},{2,18},{3,19},{4,20},{5,21},{6,22},{7,23},{8,12},{9,... | collective-permute-start | bytes 294920 | tf_op jit(solution)/shard_map/ppermute | solution.py:157
  6.2 1.3 %load.1 = (bf16[2,384,768]{2,1,0:T(8,128)(2,1)S(1)}, s32[2,2,8,128]{3,2,1,0:T(8,128)S(1)}) custom-call(s32[2]{0:T(128)} %occ.1, s32[2]{0:T(128)} %live.1, bf16[2,384,768]{2,1,0:T(8,128)(2,1)} %ints.1), custom_call_target="tpu_custom_call" | custom-call | tf_op jit(solution)/shard_map/load/pallas_call | solution.py:128
  7.5 0.0 collective-permute-done.2.refs_3_
  7.5 1.8 %collective-permute-done.1.refs_2_ = bf16[2,2,32,384]{3,2,1,0:T(8,128)(2,1)S(1)} collective-permute-done((bf16[2,2,32,384]{3,2,1,0:T(8,128)(2,1)S(1)}, bf16[2,2,32,384]{3,2,1,0:T(8,128)(2,1)S(1)}, u32[]{:S(2)}, u32[]{:S(2)}) %collective-permute-start.1) | collective-permute-done | bytes 98336 | tf_op jit(solution)/shard_map/ppermute | solution.py:157
  9.3 0.0 collective-permute-done.3.refs_5_
  9.3 0.7 %products.1 = (f32[192,128]{1,0:T(8,128)S(1)}, f32[192,128]{1,0:T(8,128)S(1)}, f32[192,128]{1,0:T(8,128)S(1)}, f32[192,128]{1,0:T(8,128)S(1)}) custom-call(s32[2,2,8,128]{3,2,1,0:T(8,128)S(1)} %get-tuple-element.15.refs_0_, bf16[2,2,32,384]{3,2,1,0:T(8,128)(2,1)S(1)} %join.1.refs_1_, bf16[2,2,32,384]{3,2,1,0:T(8,128)(2,1)S(1)} %collective-permute-done.1.refs_2_, ...), custom_call_target="tpu_custom_call" | custom-call | tf_op jit(solution)/shard_map/products/pallas_call | solution.py:128
  10.0 2.5 %collective-permute-start.4 = (f32[192,128]{1,0:T(8,128)S(1)}, f32[192,128]{1,0:T(8,128)S(1)}, u32[]{:S(2)}, u32[]{:S(2)}) collective-permute-start(f32[192,128]{1,0:T(8,128)S(1)} %get-tuple-element.20), channel_id=1, source_target_pairs={{0,17},{1,16},{2,19},{3,18},{4,21},{5,20},{6,23},{7,22},{8,25},{9,... | collective-permute-start | bytes 294920 | tf_op jit(solution)/shard_map/ppermute | solution.py:157
  12.5 0.5 %collective-permute-start.5 = (f32[192,128]{1,0:T(8,128)S(1)}, f32[192,128]{1,0:T(8,128)S(1)}, u32[]{:S(2)}, u32[]{:S(2)}) collective-permute-start(f32[192,128]{1,0:T(8,128)S(1)} %get-tuple-element.21), channel_id=1, source_target_pairs={{0,16},{1,17},{2,18},{3,19},{4,20},{5,21},{6,22},{7,23},{8,24},{9,... | collective-permute-start | bytes 294920 | tf_op jit(solution)/shard_map/ppermute | solution.py:157
  13.1 0.5 %collective-permute-start.6 = (f32[192,128]{1,0:T(8,128)S(1)}, f32[192,128]{1,0:T(8,128)S(1)}, u32[]{:S(2)}, u32[]{:S(2)}) collective-permute-start(f32[192,128]{1,0:T(8,128)S(1)} %get-tuple-element.22), channel_id=1, source_target_pairs={{0,1},{1,0},{2,3},{3,2},{4,5},{5,4},{6,7},{7,6},{8,9},{9,8},{10,11... | collective-permute-start | bytes 294920 | tf_op jit(solution)/shard_map/ppermute | solution.py:157
  13.6 2.0 %collective-permute-done.4.refs_2_ = f32[192,128]{1,0:T(8,128)S(1)} collective-permute-done((f32[192,128]{1,0:T(8,128)S(1)}, f32[192,128]{1,0:T(8,128)S(1)}, u32[]{:S(2)}, u32[]{:S(2)}) %collective-permute-start.4) | collective-permute-done | bytes 98336 | tf_op jit(solution)/shard_map/ppermute | solution.py:157
  15.6 2.6 %collective-permute-done.5.refs_3_ = f32[192,128]{1,0:T(8,128)S(1)} collective-permute-done((f32[192,128]{1,0:T(8,128)S(1)}, f32[192,128]{1,0:T(8,128)S(1)}, u32[]{:S(2)}, u32[]{:S(2)}) %collective-permute-start.5) | collective-permute-done | bytes 98336 | tf_op jit(solution)/shard_map/ppermute | solution.py:157
  18.2 0.8 %collective-permute-done.6.refs_4_ = f32[192,128]{1,0:T(8,128)S(1)} collective-permute-done((f32[192,128]{1,0:T(8,128)S(1)}, f32[192,128]{1,0:T(8,128)S(1)}, u32[]{:S(2)}, u32[]{:S(2)}) %collective-permute-start.6) | collective-permute-done | bytes 98336 | tf_op jit(solution)/shard_map/ppermute | solution.py:157
  19.0 0.1 finish.1
  19.1 0.1 collective-permute-start.7
  19.2 2.3 %collective-permute-start.8 = (bf16[2,2,32,96]{3,2,1,0:T(8,128)(2,1)S(1)}, bf16[2,2,32,96]{3,2,1,0:T(8,128)(2,1)S(1)}, u32[]{:S(2)}, u32[]{:S(2)}) collective-permute-start(bf16[2,2,32,96]{3,2,1,0:T(8,128)(2,1)S(1)} %get-tuple-element.23.first), channel_id=1, source_target_pairs={{0,8},{1,9},{2,10},{3,11},{4,12},{5,13},{6,14},{7,15},{8,4},{9,5},... | collective-permute-start | bytes 73736 | tf_op jit(solution)/shard_map/ppermute | solution.py:157
  21.5 1.6 %collective-permute-done.7.refs_0_ = bf16[2,2,32,96]{3,2,1,0:T(8,128)(2,1)S(1)} collective-permute-done((bf16[2,2,32,96]{3,2,1,0:T(8,128)(2,1)S(1)}, bf16[2,2,32,96]{3,2,1,0:T(8,128)(2,1)S(1)}, u32[]{:S(2)}, u32[]{:S(2)}) %collective-permute-start.7) | collective-permute-done | bytes 24608 | tf_op jit(solution)/shard_map/ppermute | solution.py:157
  23.1 0.4 %collective-permute-done.8.refs_1_ = bf16[2,2,32,96]{3,2,1,0:T(8,128)(2,1)S(1)} collective-permute-done((bf16[2,2,32,96]{3,2,1,0:T(8,128)(2,1)S(1)}, bf16[2,2,32,96]{3,2,1,0:T(8,128)(2,1)S(1)}, u32[]{:S(2)}, u32[]{:S(2)}) %collective-permute-start.8) | collective-permute-done | bytes 24608 | tf_op jit(solution)/shard_map/ppermute | solution.py:157
  23.5 0.6 %collective-permute-start.9 = (bf16[2,2,32,96]{3,2,1,0:T(8,128)(2,1)S(1)}, bf16[2,2,32,96]{3,2,1,0:T(8,128)(2,1)S(1)}, u32[]{:S(2)}, u32[]{:S(2)}) collective-permute-start(bf16[2,2,32,96]{3,2,1,0:T(8,128)(2,1)S(1)} %settle.1), channel_id=1, source_target_pairs={{0,8},{1,9},{2,10},{3,11},{4,12},{5,13},{6,14},{7,15},{8,0},{9,1},... | collective-permute-start | bytes 73736 | tf_op jit(solution)/shard_map/ppermute | solution.py:157
  24.1 0.9 %collective-permute-done.9.refs_2_ = bf16[2,2,32,96]{3,2,1,0:T(8,128)(2,1)S(1)} collective-permute-done((bf16[2,2,32,96]{3,2,1,0:T(8,128)(2,1)S(1)}, bf16[2,2,32,96]{3,2,1,0:T(8,128)(2,1)S(1)}, u32[]{:S(2)}, u32[]{:S(2)}) %collective-permute-start.9) | collective-permute-done | bytes 24608 | tf_op jit(solution)/shard_map/ppermute | solution.py:157
  24.9 0.6 %assemble.1 = bf16[4,2,32,96]{3,2,1,0:T(8,128)(2,1)} custom-call(bf16[2,2,32,96]{3,2,1,0:T(8,128)(2,1)S(1)} %get-tuple-element.23.first, bf16[2,2,32,96]{3,2,1,0:T(8,128)(2,1)S(1)} %collective-permute-done.7.refs_0_, bf16[2,2,32,96]{3,2,1,0:T(8,128)(2,1)S(1)} %collective-permute-done.8.refs_1_, bf16[2,2,32,96]{3,2,1,0:T(8,128)(2,1)S(1)} %collective-permute-done.9.refs_2_), custom_call_target="tpu_custom_call" | custom-call | tf_op jit(solution)/shard_map/assemble/pallas_call | solution.py:128
  (2 shorter events, 0.0 us)
Async XLA Ops:
  0.0 1.5 %collective-permute-start = (bf16[2,32,384]{2,1,0:T(8,128)(2,1)}, bf16[2,32,384]{2,1,0:T(8,128)(2,1)S(1)}, u32[]{:S(2)}, u32[]{:S(2)}) collective-permute-start(bf16[2,32,384]{2,1,0:T(8,128)(2,1)} %src.1), channel_id=1, source_target_pairs={{0,8},{1,9},{2,10},{3,11},{4,12},{5,13},{6,14},{7,15},{8,0},{9,1},... | collective-permute-start | bytes 147464 | tf_op jit(solution)/shard_map/ppermute | solution.py:157
  1.6 7.8 %collective-permute-start.3 = (bf16[2,384,768]{2,1,0:T(8,128)(2,1)}, bf16[2,384,768]{2,1,0:T(8,128)(2,1)S(1)}, u32[]{:S(2)}, u32[]{:S(2)}) collective-permute-start(bf16[2,384,768]{2,1,0:T(8,128)(2,1)} %ints.1), channel_id=1, source_target_pairs={{0,8},{1,9},{2,10},{3,11},{4,12},{5,13},{6,14},{7,15},{8,0},{9,1},... | collective-permute-start | bytes 3538952 | tf_op jit(solution)/shard_map/ppermute | solution.py:157
  2.0 5.5 %collective-permute-start.2 = (bf16[2,2,32,384]{3,2,1,0:T(8,128)(2,1)S(1)}, bf16[2,2,32,384]{3,2,1,0:T(8,128)(2,1)S(1)}, u32[]{:S(2)}, u32[]{:S(2)}) collective-permute-start(bf16[2,2,32,384]{3,2,1,0:T(8,128)(2,1)S(1)} %join.1.refs_1_), channel_id=1, source_target_pairs={{0,2},{1,3},{2,0},{3,1},{4,6},{5,7},{6,4},{7,5},{8,14},{9,15},{10,... | collective-permute-start | bytes 294920 | tf_op jit(solution)/shard_map/ppermute | solution.py:157
  4.7 4.6 %collective-permute-start.1 = (bf16[2,2,32,384]{3,2,1,0:T(8,128)(2,1)S(1)}, bf16[2,2,32,384]{3,2,1,0:T(8,128)(2,1)S(1)}, u32[]{:S(2)}, u32[]{:S(2)}) collective-permute-start(bf16[2,2,32,384]{3,2,1,0:T(8,128)(2,1)S(1)} %join.1.refs_1_), channel_id=1, source_target_pairs={{0,16},{1,17},{2,18},{3,19},{4,20},{5,21},{6,22},{7,23},{8,12},{9,... | collective-permute-start | bytes 294920 | tf_op jit(solution)/shard_map/ppermute | solution.py:157
  10.0 5.6 %collective-permute-start.4 = (f32[192,128]{1,0:T(8,128)S(1)}, f32[192,128]{1,0:T(8,128)S(1)}, u32[]{:S(2)}, u32[]{:S(2)}) collective-permute-start(f32[192,128]{1,0:T(8,128)S(1)} %get-tuple-element.20), channel_id=1, source_target_pairs={{0,17},{1,16},{2,19},{3,18},{4,21},{5,20},{6,23},{7,22},{8,25},{9,... | collective-permute-start | bytes 294920 | tf_op jit(solution)/shard_map/ppermute | solution.py:157
  12.5 5.7 %collective-permute-start.5 = (f32[192,128]{1,0:T(8,128)S(1)}, f32[192,128]{1,0:T(8,128)S(1)}, u32[]{:S(2)}, u32[]{:S(2)}) collective-permute-start(f32[192,128]{1,0:T(8,128)S(1)} %get-tuple-element.21), channel_id=1, source_target_pairs={{0,16},{1,17},{2,18},{3,19},{4,20},{5,21},{6,22},{7,23},{8,24},{9,... | collective-permute-start | bytes 294920 | tf_op jit(solution)/shard_map/ppermute | solution.py:157
  13.1 5.9 %collective-permute-start.6 = (f32[192,128]{1,0:T(8,128)S(1)}, f32[192,128]{1,0:T(8,128)S(1)}, u32[]{:S(2)}, u32[]{:S(2)}) collective-permute-start(f32[192,128]{1,0:T(8,128)S(1)} %get-tuple-element.22), channel_id=1, source_target_pairs={{0,1},{1,0},{2,3},{3,2},{4,5},{5,4},{6,7},{7,6},{8,9},{9,8},{10,11... | collective-permute-start | bytes 294920 | tf_op jit(solution)/shard_map/ppermute | solution.py:157
  19.1 4.0 %collective-permute-start.7 = (bf16[2,2,32,96]{3,2,1,0:T(8,128)(2,1)S(1)}, bf16[2,2,32,96]{3,2,1,0:T(8,128)(2,1)S(1)}, u32[]{:S(2)}, u32[]{:S(2)}) collective-permute-start(bf16[2,2,32,96]{3,2,1,0:T(8,128)(2,1)S(1)} %get-tuple-element.24), channel_id=1, source_target_pairs={{0,2},{1,3},{2,0},{3,1},{4,6},{5,7},{6,4},{7,5},{8,14},{9,15},{10,... | collective-permute-start | bytes 73736 | tf_op jit(solution)/shard_map/ppermute | solution.py:157
  19.2 4.3 %collective-permute-start.8 = (bf16[2,2,32,96]{3,2,1,0:T(8,128)(2,1)S(1)}, bf16[2,2,32,96]{3,2,1,0:T(8,128)(2,1)S(1)}, u32[]{:S(2)}, u32[]{:S(2)}) collective-permute-start(bf16[2,2,32,96]{3,2,1,0:T(8,128)(2,1)S(1)} %get-tuple-element.23.first), channel_id=1, source_target_pairs={{0,8},{1,9},{2,10},{3,11},{4,12},{5,13},{6,14},{7,15},{8,4},{9,5},... | collective-permute-start | bytes 73736 | tf_op jit(solution)/shard_map/ppermute | solution.py:157
  23.5 1.4 %collective-permute-start.9 = (bf16[2,2,32,96]{3,2,1,0:T(8,128)(2,1)S(1)}, bf16[2,2,32,96]{3,2,1,0:T(8,128)(2,1)S(1)}, u32[]{:S(2)}, u32[]{:S(2)}) collective-permute-start(bf16[2,2,32,96]{3,2,1,0:T(8,128)(2,1)S(1)} %settle.1), channel_id=1, source_target_pairs={{0,8},{1,9},{2,10},{3,11},{4,12},{5,13},{6,14},{7,15},{8,0},{9,1},... | collective-permute-start | bytes 73736 | tf_op jit(solution)/shard_map/ppermute | solution.py:157
